TPU v7x, 256 devices: a whole 4x4x8 slice. The times are simulated.
256 devices in a mesh: expert: 8 (over z), context: 32 (over y, x, core).
Axes of the slice: x: 4, y: 4, z: 8, core: 2. Of those that a mesh axis runs over, the one named last changes fastest.
Arguments:
- hidden: bfloat16 [4096, 2048], P('context'), may hold values from -6 to 6
- upstream: bfloat16 [4096, 2048], P('context'), may hold values from -6 to 6
- norm_gain: float32 [2048], replicated, may hold values from 0.5 to 1.5
- route_ids: int32 [4096, 8], P('context'), may hold values from 0 to 127, all different within a row; in each aligned block of 128 rows (0 to 127, 128 to 255, ...) at most 12 rows name the same one
- route_weights: bfloat16 [4096, 8], P('context'), may hold values from 0.049804688 to 0.29882812
- w_gate: bfloat16 [128, 2048, 1024], P('context', None, 'expert'), may hold values from -0.125 to 0.125
- w_up: bfloat16 [128, 2048, 1024], P('context', None, 'expert'), may hold values from -0.125 to 0.125
- w_down: bfloat16 [128, 1024, 2048], P('context', 'expert'), may hold values from -0.1875 to 0.1875
- w_out: bfloat16 [2048, 2048], P('expert'), may hold values from -0.125 to 0.125
- queries: bfloat16 [4096, 2048], P('context', 'expert'), may hold values from -48 to 48
- keys: bfloat16 [4096, 256], P('context'), may hold values from -4 to 4
- values: bfloat16 [4096, 256], P('context'), may hold values from -6 to 6
Outputs:
- d_hidden: bfloat16 [4096, 2048], P('context')
- d_route: float32 [4096, 8], P('context')
- d_queries: float32 [4096, 2048], P('context', 'expert')
- d_keys: float32 [4096, 256], P('context')
- d_values: float32 [4096, 256], P('context')
Inputs may be any that keep to these rules, and one draw needn't show every extreme that they name: `route_ids`: in each aligned block of 128 rows, no expert is named by more than 12 rows, a bound that some block reaches.
All inputs are finite; a program needn't handle non-finite values.
Results may differ from a plain program's by a relative error of at most 0.015.
Values may be sent and summed in bfloat16 or wider, within the bound.
No kernel may reach another device: no remote copies, remote signals or barrier semaphores. Data moves between devices by JAX's collectives and lax.ppermute only.
A program may use at most 128 MiB of HBM per device.

v0:
```python
import math

import jax
import jax.numpy as jnp
from jax import lax
from jax.sharding import PartitionSpec as P

HEADS = 16
KV_HEADS = 2
HEAD_DIM = 128
CAP = 12


epsilon = 1e-06


def silu_slope(pre_act):
    sigmoid = jax.nn.sigmoid(pre_act)
    return sigmoid * (1.0 + pre_act * (1.0 - sigmoid))


def expert_terms(normed, upstream, weights, w_gate, w_up, w_down):
    gate_pre = jnp.einsum("slnd,ldf->slnf", normed, w_gate, preferred_element_type=jnp.float32)
    up_proj = jnp.einsum("slnd,ldf->slnf", normed, w_up, preferred_element_type=jnp.float32)
    active = jax.nn.silu(gate_pre)
    product = (active * up_proj).astype(jnp.bfloat16)
    scaled = (weights.astype(jnp.float32)[..., None] * upstream.astype(jnp.float32)).astype(
        jnp.bfloat16
    )
    d_product = jnp.einsum("slnd,lfd->slnf", scaled, w_down, preferred_element_type=jnp.float32)
    d_gate = (d_product * up_proj * silu_slope(gate_pre)).astype(jnp.bfloat16)
    d_up = (d_product * active).astype(jnp.bfloat16)
    d_rows = jnp.einsum("slnf,ldf->slnd", d_gate, w_gate, preferred_element_type=jnp.float32)
    d_rows = d_rows + jnp.einsum("slnf,ldf->slnd", d_up, w_up, preferred_element_type=jnp.float32)
    projected = jnp.einsum("slnd,lfd->slnf", upstream, w_down, preferred_element_type=jnp.float32)
    d_weight = jnp.sum(product.astype(jnp.float32) * projected, axis=3)
    return (d_rows.astype(jnp.bfloat16), d_weight.astype(jnp.bfloat16))


def body(
    hidden,
    upstream,
    norm_gain,
    route_ids,
    route_weights,
    w_gate,
    w_up,
    w_down,
    w_out,
    queries,
    keys,
    values,
):
    ctx_count = lax.axis_size("context")
    token_count = hidden.shape[0]
    feature_width = hidden.shape[1]
    route_count = route_ids.shape[1]
    local_experts = w_gate.shape[0]
    expert_total = local_experts * ctx_count
    slot_count = CAP
    hidden_wide = hidden.astype(jnp.float32)
    inv_rms = lax.rsqrt(jnp.mean(hidden_wide * hidden_wide, axis=1, keepdims=True) + epsilon)
    normed = (hidden_wide * inv_rms * norm_gain).astype(jnp.bfloat16)
    flat_ids = route_ids.reshape(-1)
    one_hot = (flat_ids[:, None] == jnp.arange(expert_total, dtype=jnp.int32)[None, :]).astype(
        jnp.int32
    )
    slot_rank = jnp.sum(jnp.cumsum(one_hot, axis=0) * one_hot, axis=1) - 1
    position = flat_ids * slot_count + slot_rank
    token_of = jnp.arange(token_count * route_count, dtype=jnp.int32) // route_count
    buffer_rows = expert_total * slot_count
    send_rows = (
        jnp.zeros((buffer_rows, feature_width), jnp.bfloat16).at[position].set(normed[token_of])
    )
    send_grad = (
        jnp.zeros((buffer_rows, feature_width), jnp.bfloat16).at[position].set(upstream[token_of])
    )
    send_weight = (
        jnp.zeros((buffer_rows,), jnp.bfloat16).at[position].set(route_weights.reshape(-1))
    )
    block_shape = (ctx_count, local_experts, slot_count, feature_width)
    weight_block = send_weight.reshape(ctx_count, local_experts, slot_count)
    rows_in = lax.all_to_all(
        send_rows.reshape(block_shape), "context", split_axis=0, concat_axis=0, tiled=True
    )
    grad_in = lax.all_to_all(
        send_grad.reshape(block_shape), "context", split_axis=0, concat_axis=0, tiled=True
    )
    weight_in = lax.all_to_all(weight_block, "context", split_axis=0, concat_axis=0, tiled=True)
    d_rows, d_weight = expert_terms(rows_in, grad_in, weight_in, w_gate, w_up, w_down)
    back_rows = lax.all_to_all(d_rows, "context", split_axis=0, concat_axis=0, tiled=True)
    back_weight = lax.all_to_all(d_weight, "context", split_axis=0, concat_axis=0, tiled=True)
    back_width = back_rows.shape[3]
    picked = back_rows.reshape(buffer_rows, back_width)[position].astype(jnp.float32)
    partial_rows = jnp.sum(picked.reshape(token_count, route_count, back_width), axis=1)
    partial_weight = (
        back_weight.reshape(-1)[position].astype(jnp.float32).reshape(token_count, route_count)
    )
    d_normed, d_route = lax.psum((partial_rows, partial_weight), "expert")
    gained = d_normed * norm_gain
    inner = jnp.mean(gained * hidden_wide, axis=1, keepdims=True)
    d_hidden = (
        upstream.astype(jnp.float32)
        + inv_rms * gained
        - hidden_wide * inv_rms * inv_rms * inv_rms * inner
    ).astype(jnp.bfloat16)
    heads_dev = queries.shape[1] // HEAD_DIM
    group_size = HEADS // KV_HEADS
    kv_head = lax.axis_index("expert") * heads_dev // group_size
    own_keys = lax.dynamic_slice_in_dim(keys, kv_head * HEAD_DIM, HEAD_DIM, 1)
    own_values = lax.dynamic_slice_in_dim(values, kv_head * HEAD_DIM, HEAD_DIM, 1)
    all_keys, all_values = (
        lax.all_gather(own_keys, "context", axis=0, tiled=True),
        lax.all_gather(own_values, "context", axis=0, tiled=True),
    )
    d_out = jnp.einsum("td,cd->tc", d_hidden, w_out, preferred_element_type=jnp.float32).astype(
        jnp.bfloat16
    )
    query_rows = (
        queries.reshape(token_count, heads_dev, HEAD_DIM).transpose(1, 0, 2).reshape(-1, HEAD_DIM)
    )
    grad_rows = (
        d_out.reshape(token_count, heads_dev, HEAD_DIM).transpose(1, 0, 2).reshape(-1, HEAD_DIM)
    )
    score_scale = 1.0 / math.sqrt(HEAD_DIM)
    scores = score_scale * jnp.einsum(
        "rc,sc->rs", query_rows, all_keys, preferred_element_type=jnp.float32
    )
    row_max = jnp.max(scores, axis=1, keepdims=True)
    shifted = jnp.exp(scores - row_max)
    softmax = shifted / jnp.sum(shifted, axis=1, keepdims=True)
    softmax_low = softmax.astype(jnp.bfloat16)
    d_soft = jnp.einsum("rc,sc->rs", grad_rows, all_values, preferred_element_type=jnp.float32)
    delta = jnp.sum(softmax * d_soft, axis=1, keepdims=True)
    d_scores = (softmax * (d_soft - delta)).astype(jnp.bfloat16)
    query_grad = score_scale * jnp.einsum(
        "rs,sc->rc", d_scores, all_keys, preferred_element_type=jnp.float32
    )
    key_part = score_scale * jnp.einsum(
        "rs,rc->sc", d_scores, query_rows, preferred_element_type=jnp.float32
    )
    value_part = jnp.einsum("rs,rc->sc", softmax_low, grad_rows, preferred_element_type=jnp.float32)
    d_queries = (
        query_grad.reshape(heads_dev, token_count, HEAD_DIM)
        .transpose(1, 0, 2)
        .reshape(token_count, -1)
    )
    head_mask = (jnp.arange(KV_HEADS, dtype=jnp.int32) == kv_head).astype(jnp.float32)
    key_mine, value_mine = (
        lax.psum_scatter(key_part, "context", scatter_dimension=0, tiled=True),
        lax.psum_scatter(value_part, "context", scatter_dimension=0, tiled=True),
    )
    key_wide = (key_mine[:, None, :] * head_mask[None, :, None]).reshape(
        token_count, KV_HEADS * HEAD_DIM
    )
    value_wide = (value_mine[:, None, :] * head_mask[None, :, None]).reshape(
        token_count, KV_HEADS * HEAD_DIM
    )
    d_keys, d_values = lax.psum((key_wide, value_wide), "expert")
    return (d_hidden, d_route, d_queries, d_keys, d_values)


def solution(mesh):
    placed = (
        P("context", None),
        P("context", None),
        P(),
        P("context", None),
        P("context", None),
        P("context", None, "expert"),
        P("context", None, "expert"),
        P("context", "expert", None),
        P("expert", None),
        P("context", "expert"),
        P("context", None),
        P("context", None),
    )
    return jax.shard_map(
        body,
        mesh=mesh,
        in_specs=placed,
        out_specs=(
            P("context", None),
            P("context", None),
            P("context", "expert"),
            P("context", None),
            P("context", None),
        ),
        check_vma=False,
    )
```

profile of v0, /device:TPU:2, one launch (start us, length us, event | category | flops | bytes accessed | tf_op | source)
XLA Modules:
  0.0 748.1 jit_solution(9588568585199000721)
XLA Ops:
  8.0 0.8 broadcast_multiply_fusion
  11.8 7.6 %scatter_custom_fusion = bf16[1536]{0:T(1024)(128)(2,1)S(1)} fusion(s32[1024]{0:T(1024)S(1)} %bitcast.120, bf16[1024]{0:T(1024)(128)(2,1)S(1)} %reshape.229, bf16[]{:T(256)} %constant.57.clone.1), kind=kCustom, calls=%fused_computation.93 | custom fusion | bytes 3074 | tf_op jit(solution)/shard_map/scatter | solution.py:79
  20.2 7.9 %all-to-all-start = ((bf16[32,4,12]{2,1,0:T(4,128)(2,1)}), bf16[32,4,12]{2,1,0:T(4,128)(2,1)S(1)}, u32[]{:S(2)}, u32[]{:S(2)}) async-start(bf16[32,4,12]{2,1,0:T(4,128)(2,1)} %reshape.180), calls=%async_computation | async-start | bytes 65536 | tf_op jit(solution)/shard_map/all_to_all | solution.py:89
  28.1 24.6 %scatter_custom_fusion.1 = bf16[1536,2048]{1,0:T(8,128)(2,1)} fusion(s32[1024]{0:T(1024)S(1)} %bitcast.121, bf16[128,2048]{1,0:T(8,128)(2,1)} %param.13, s32[1024]{0:T(1024)S(1)} %broadcast_clamp_fusion.1, bf16[]{:T(256)} %constant.57.clone.1), kind=kCustom, calls=%fused_computation.28 | custom fusion | bytes 6291968 | tf_op jit(solution)/shard_map/scatter | solution.py:76
  52.8 10.6 %reshape.181 = bf16[32,4,12,2048]{3,2,1,0:T(8,128)(2,1)} reshape(bf16[1536,2048]{1,0:T(8,128)(2,1)} %scatter_custom_fusion.1) | data formatting | bytes 12582912 | tf_op jit(solution)/shard_map/reshape | solution.py:87
  63.4 12.0 %copy.153 = bf16[32,4,12,2048]{3,1,2,0:T(4,128)(2,1)} copy(bf16[32,4,12,2048]{3,2,1,0:T(8,128)(2,1)} %reshape.181) | data formatting | bytes 12582912 | tf_op jit(solution)/shard_map/reshape | solution.py:87
  75.4 8.1 %all-to-all-start.1 = ((bf16[32,4,12,2048]{3,1,2,0:T(4,128)(2,1)}), bf16[32,4,12,2048]{3,1,2,0:T(4,128)(2,1)}, u32[]{:S(2)}, u32[]{:S(2)}) async-start(bf16[32,4,12,2048]{3,1,2,0:T(4,128)(2,1)} %copy.153), calls=%async_computation.1 | async-start | bytes 12582912 | tf_op jit(solution)/shard_map/all_to_all | solution.py:86
  84.0 23.8 %scatter_custom_fusion.2 = bf16[1536,2048]{1,0:T(8,128)(2,1)} fusion(s32[1024]{0:T(1024)S(1)} %bitcast.122, bf16[128,2048]{1,0:T(8,128)(2,1)S(1)} %fusion.60, s32[1024]{0:T(1024)S(1)} %broadcast_clamp_fusion.1, bf16[]{:T(256)} %constant.57.clone.1), kind=kCustom, calls=%fused_computation.26 | custom fusion | bytes 6291458 | tf_op jit(solution)/shard_map/scatter | solution.py:73
  107.8 10.6 %reshape.182 = bf16[32,4,12,2048]{3,2,1,0:T(8,128)(2,1)} reshape(bf16[1536,2048]{1,0:T(8,128)(2,1)} %scatter_custom_fusion.2) | data formatting | bytes 12582912 | tf_op jit(solution)/shard_map/reshape | solution.py:84
  118.3 12.0 %copy.155 = bf16[32,4,12,2048]{3,1,2,0:T(4,128)(2,1)} copy(bf16[32,4,12,2048]{3,2,1,0:T(8,128)(2,1)} %reshape.182) | data formatting | bytes 12582912 | tf_op jit(solution)/shard_map/reshape | solution.py:84
  130.3 28.3 %all-to-all-done.1 = bf16[32,4,12,2048]{3,1,2,0:T(4,128)(2,1)} async-done(((bf16[32,4,12,2048]{3,1,2,0:T(4,128)(2,1)}), bf16[32,4,12,2048]{3,1,2,0:T(4,128)(2,1)}, u32[]{:S(2)}, u32[]{:S(2)}) %all-to-all-start.1) | async-done | bytes 6291488 | tf_op jit(solution)/shard_map/all_to_all | solution.py:86
  158.6 7.6 %all-to-all-start.2 = ((bf16[32,4,12,2048]{3,1,2,0:T(4,128)(2,1)}), bf16[32,4,12,2048]{3,1,2,0:T(4,128)(2,1)}, u32[]{:S(2)}, u32[]{:S(2)}) async-start(bf16[32,4,12,2048]{3,1,2,0:T(4,128)(2,1)} %copy.155), calls=%async_computation.2 | async-start | bytes 12582912 | tf_op jit(solution)/shard_map/all_to_all | solution.py:83
  166.6 8.0 %multiply_convert_fusion = bf16[32,4,12,2048]{3,1,2,0:T(4,128)(2,1)} fusion(bf16[32,4,12,2048]{3,1,2,0:T(4,128)(2,1)} %all-to-all-done.1, f32[32,4,12]{1,2,0:T(8,128)S(1)} %copy.152), kind=kLoop, calls=%fused_computation.8 | loop fusion | flops 9437184 | bytes 12589056 | tf_op jit(solution)/shard_map/convert_element_type | solution.py:27
  174.5 7.1 fusion.37
  181.6 59.7 %all-to-all-done.2 = bf16[32,4,12,2048]{3,1,2,0:T(4,128)(2,1)} async-done(((bf16[32,4,12,2048]{3,1,2,0:T(4,128)(2,1)}), bf16[32,4,12,2048]{3,1,2,0:T(4,128)(2,1)}, u32[]{:S(2)}, u32[]{:S(2)}) %all-to-all-start.2) | async-done | bytes 6291488 | tf_op jit(solution)/shard_map/all_to_all | solution.py:83
  241.3 6.5 fusion.32
  247.8 7.0 fusion.27
  254.8 6.5 fusion.20
  261.3 9.1 %fusion = bf16[32,4,12,2048]{3,0,2,1:T(8,128)(2,1)} fusion(f32[4,32,12,2048]{3,1,2,0:T(8,128)} %fusion.20, bf16[4,2048,128]{2,1,0:T(8,128)(2,1)S(1)} %copy-done.10, f32[32,4,12,128]{3,0,2,1:T(8,128)S(1)} %fusion.37, f32[32,4,12,128]{3,0,2,1:T(8,128)S(1)} %fusion.32), kind=kOutput, calls=%fused_computation.10 | convolution fusion | flops 812777472 | bytes 22544384 | tf_op jit(solution)/shard_map/slnf,ldf->slnd/dot_general | solution.py:34
  270.3 10.2 %copy.158 = bf16[32,4,12,2048]{3,1,2,0:T(4,128)(2,1)} copy(bf16[32,4,12,2048]{3,0,2,1:T(8,128)(2,1)} %fusion) | data formatting | bytes 12582912 | tf_op jit(solution)/shard_map/convert_element_type | solution.py:37
  280.6 7.7 %all-to-all-start.3 = ((bf16[32,4,12,2048]{3,1,2,0:T(4,128)(2,1)}), bf16[32,4,12,2048]{3,1,2,0:T(4,128)(2,1)}, u32[]{:S(2)}, u32[]{:S(2)}) async-start(bf16[32,4,12,2048]{3,1,2,0:T(4,128)(2,1)} %copy.158), calls=%async_computation.3 | async-start | bytes 12582912 | tf_op jit(solution)/shard_map/all_to_all | solution.py:91
  289.2 74.7 %all-to-all-done.3 = bf16[32,4,12,2048]{3,1,2,0:T(4,128)(2,1)} async-done(((bf16[32,4,12,2048]{3,1,2,0:T(4,128)(2,1)}), bf16[32,4,12,2048]{3,1,2,0:T(4,128)(2,1)}, u32[]{:S(2)}, u32[]{:S(2)}) %all-to-all-start.3) | async-done | bytes 6291488 | tf_op jit(solution)/shard_map/all_to_all | solution.py:91
  364.0 11.5 %copy.159 = bf16[32,4,12,2048]{3,2,1,0:T(8,128)(2,1)} copy(bf16[32,4,12,2048]{3,1,2,0:T(4,128)(2,1)} %all-to-all-done.3) | data formatting | bytes 12582912 | tf_op jit(solution)/shard_map/all_to_all | solution.py:91
  375.4 10.7 %reshape.183 = bf16[1536,2048]{1,0:T(8,128)(2,1)} reshape(bf16[32,4,12,2048]{3,2,1,0:T(8,128)(2,1)} %copy.159) | data formatting | bytes 12582912 | tf_op jit(solution)/shard_map/reshape | solution.py:94
  386.2 12.4 %gather_fusion = bf16[1024,2048]{1,0:T(8,128)(2,1)} fusion(bf16[1536,2048]{1,0:T(8,128)(2,1)} %reshape.183, s32[1024]{0:T(1024)S(1)} %broadcast_clamp_fusion), kind=kCustom, calls=%fused_computation.2 | custom fusion | bytes 8392704 | tf_op jit(solution)/shard_map/gather | solution.py:94
  398.6 6.0 convert_reduce_fusion
  405.9 2.1 fusion.79
  408.0 1.9 copy-done.2
  410.6 70.9 %all-reduce.4.cloned.1.call-done = f32[128,2048]{1,0:T(8,128)} async-done(((f32[128,2048]{1,0:T(8,128)}), f32[128,2048]{1,0:T(8,128)}) %all-reduce.4.cloned.1.call-update) | async-done | bytes 1048592 | tf_op jit(solution)/shard_map/psum | solution.py:99
  481.5 1.6 fusion.66
  483.1 1.6 fusion.64
  486.1 2.2 fusion.19
  488.3 3.7 fusion.9
  492.1 1.0 fusion.10
  493.1 2.0 convolution_multiply_fusion.1
  495.2 7.8 %fusion.54 = bf16[32,4,12]{0,2,1:T(8,128)(2,1)S(1)} fusion(bf16[4,128,2048]{2,1,0:T(8,128)(2,1)} %param.19, bf16[32,4,12,2048]{3,1,2,0:T(4,128)(2,1)} %all-to-all-done.1, f32[32,4,12,128]{3,0,2,1:T(8,128)} %copy-done.12, f32[32,4,12,128]{3,0,2,1:T(8,128)} %copy-done.8), kind=kOutput, calls=%fused_computation.53 | convolution fusion | flops 807074304 | bytes 9964544 | tf_op jit(solution)/shard_map/slnd,lfd->slnf/dot_general | solution.py:35
  503.8 7.4 all-to-all-start.4
  511.3 6.1 all-to-all-done.4
  517.5 6.8 gather_fusion.1
  524.4 29.6 %psum.29 = f32[128,8]{1,0:T(8,128)S(1)} all-reduce(f32[128,8]{1,0:T(8,128)S(1)} %reshape.192), channel_id=1, replica_groups=mesh['expert'=8,'context'=32] {'expert'}, use_global_device_ids=true, to_apply=%region_11.12 | all-reduce | flops 1024 | bytes 8192 | tf_op jit(solution)/shard_map/psum | solution.py:99
  554.7 18.3 %reduce-scatter.5.cloned.1.call-done = f32[128,128]{1,0:T(8,128)} async-done(((f32[4096,128]{1,0:T(8,128)}), f32[128,128]{1,0:T(8,128)}) %reduce-scatter.5.cloned.1.call-update) | async-done | bytes 65552 | tf_op jit(solution)/shard_map/reduce_scatter | solution.py:151
  573.0 89.6 %reduce-scatter.3.cloned.1.call-done = f32[128,128]{1,0:T(8,128)} async-done(((f32[4096,128]{1,0:T(8,128)}), f32[128,128]{1,0:T(8,128)}) %reduce-scatter.3.cloned.1.call-update) | async-done | bytes 65552 | tf_op jit(solution)/shard_map/reduce_scatter | solution.py:150
  662.6 0.9 mul.218
  663.5 0.9 mul.212
  665.2 2.4 convolution_multiply_fusion.2
  668.2 69.4 %all-reduce.6.cloned.1.call-done = (f32[128,256]{1,0:T(8,128)}, f32[128,256]{1,0:T(8,128)}) async-done(((f32[128,256]{1,0:T(8,128)}, f32[128,256]{1,0:T(8,128)}), (f32[128,256]{1,0:T(8,128)}, f32[128,256]{1,0:T(8,128)})) %all-reduce.6.cloned.1.call-update) | async-done | bytes 262160 | tf_op jit(solution)/shard_map/psum | solution.py:159
  737.6 1.6 copy.209
  739.2 1.6 copy.210
  (92 shorter events, 11.7 us)
Async XLA Ops:
  8.0 233.3 %copy-start = (bf16[4,2048,128]{2,1,0:T(8,128)(2,1)S(1)}, bf16[4,2048,128]{2,1,0:T(8,128)(2,1)}, u32[]{:S(2)}) copy-start(bf16[4,2048,128]{2,1,0:T(8,128)(2,1)} %param.17) | copy-start | bytes 6291460
  20.2 55.2 %all-to-all-start = ((bf16[32,4,12]{2,1,0:T(4,128)(2,1)}), bf16[32,4,12]{2,1,0:T(4,128)(2,1)S(1)}, u32[]{:S(2)}, u32[]{:S(2)}) async-start(bf16[32,4,12]{2,1,0:T(4,128)(2,1)} %reshape.180), calls=%async_computation | async-start | bytes 65536 | tf_op jit(solution)/shard_map/all_to_all | solution.py:89
  75.4 8.2 %copy-start.7 = (bf16[128,2048]{1,0:T(8,128)(2,1)S(1)}, bf16[128,2048]{1,0:T(8,128)(2,1)}, u32[]{:S(2)}) copy-start(bf16[128,2048]{1,0:T(8,128)(2,1)} %param.12) | copy-start | bytes 1572868
  75.4 8.4 %copy-start.14 = (f32[2048]{0:T(1024)S(1)}, f32[2048]{0:T(1024)}, u32[]{:S(2)}) copy-start(f32[2048]{0:T(1024)} %param.14) | copy-start | bytes 24580
  75.4 83.2 %all-to-all-start.1 = ((bf16[32,4,12,2048]{3,1,2,0:T(4,128)(2,1)}), bf16[32,4,12,2048]{3,1,2,0:T(4,128)(2,1)}, u32[]{:S(2)}, u32[]{:S(2)}) async-start(bf16[32,4,12,2048]{3,1,2,0:T(4,128)(2,1)} %copy.153), calls=%async_computation.1 | async-start | bytes 12582912 | tf_op jit(solution)/shard_map/all_to_all | solution.py:86
  158.6 82.7 %all-to-all-start.2 = ((bf16[32,4,12,2048]{3,1,2,0:T(4,128)(2,1)}), bf16[32,4,12,2048]{3,1,2,0:T(4,128)(2,1)}, u32[]{:S(2)}, u32[]{:S(2)}) async-start(bf16[32,4,12,2048]{3,1,2,0:T(4,128)(2,1)} %copy.155), calls=%async_computation.2 | async-start | bytes 12582912 | tf_op jit(solution)/shard_map/all_to_all | solution.py:83
  241.3 6.5 copy-start.10
  247.8 13.5 %copy-start.8 = (f32[32,4,12,128]{3,0,2,1:T(8,128)}, f32[32,4,12,128]{3,0,2,1:T(8,128)S(1)}, u32[]{:S(2)}) copy-start(f32[32,4,12,128]{3,0,2,1:T(8,128)S(1)} %fusion.32) | copy-start | bytes 2359300
  254.8 6.5 copy-start.12
  280.6 7.8 %copy-start.16 = (bf16[128,256]{1,0:T(8,128)(2,1)S(1)}, bf16[128,256]{1,0:T(8,128)(2,1)}, u32[]{:S(2)}) copy-start(bf16[128,256]{1,0:T(8,128)(2,1)} %param.22) | copy-start | bytes 196612
  280.6 83.4 %all-to-all-start.3 = ((bf16[32,4,12,2048]{3,1,2,0:T(4,128)(2,1)}), bf16[32,4,12,2048]{3,1,2,0:T(4,128)(2,1)}, u32[]{:S(2)}, u32[]{:S(2)}) async-start(bf16[32,4,12,2048]{3,1,2,0:T(4,128)(2,1)} %copy.158), calls=%async_computation.3 | async-start | bytes 12582912 | tf_op jit(solution)/shard_map/all_to_all | solution.py:91
  288.2 117.7 %all-gather.3.cloned.1.call-start = ((), (), s32[]{:S(2)}) async-start(), calls=%async_computation.8 | async-start | bytes 1081344 | tf_op jit(solution)/shard_map/all_gather | solution.py:113
  289.0 192.5 %all-reduce.4.cloned.1.call-start = ((), (), s32[]{:S(2)}) async-start(), calls=%async_computation.7 | async-start | bytes 2097152 | tf_op jit(solution)/shard_map/psum | solution.py:99
  398.6 6.1 copy-start.17
  398.6 7.1 copy-start.15
  404.6 83.7 %all-gather.5.cloned.1.call-start = ((), (), s32[]{:S(2)}) async-start(), calls=%async_computation.9 | async-start | bytes 1081344 | tf_op jit(solution)/shard_map/all_gather | solution.py:114
  405.4 167.6 %reduce-scatter.5.cloned.1.call-start = ((), (), s32[]{:S(2)}) async-start(), calls=%async_computation.11 | async-start | bytes 2162688 | tf_op jit(solution)/shard_map/reduce_scatter | solution.py:151
  408.0 1.9 copy-start.2
  408.0 75.1 %copy-start.13 = (bf16[128,2048]{1,0:T(8,128)(2,1)S(1)}, bf16[128,2048]{1,0:T(8,128)(2,1)}, u32[]{:S(2)}) copy-start(bf16[128,2048]{1,0:T(8,128)(2,1)} %param.13) | copy-start | bytes 1572868
  409.9 75.6 %copy-start.11 = (bf16[256,2048]{1,0:T(8,128)(2,1)S(1)}, bf16[256,2048]{1,0:T(8,128)(2,1)}, u32[]{:S(2)}) copy-start(bf16[256,2048]{1,0:T(8,128)(2,1)} %param.20) | copy-start | bytes 3145732
  481.5 4.6 copy-start.3
  484.8 0.8 copy-start.9
  488.3 174.4 %reduce-scatter.3.cloned.1.call-start = ((), (), s32[]{:S(2)}) async-start(), calls=%async_computation.10 | async-start | bytes 2162688 | tf_op jit(solution)/shard_map/reduce_scatter | solution.py:150
  488.3 3.8 copy-start.4
  493.1 2.1 copy-start.5
  495.2 170.0 %copy-start.6 = (bf16[4096,128]{1,0:T(8,128)(2,1)S(1)}, bf16[4096,128]{1,0:T(8,128)(2,1)}, u32[]{:S(2)}) copy-start(bf16[4096,128]{1,0:T(8,128)(2,1)} %all-gather.3.cloned.1.call-done) | copy-start | bytes 3145732
  495.2 245.5 %copy-start.1 = (bf16[4,2048,128]{2,1,0:T(8,128)(2,1)S(1)}, bf16[4,2048,128]{2,1,0:T(8,128)(2,1)}, u32[]{:S(2)}) copy-start(bf16[4,2048,128]{2,1,0:T(8,128)(2,1)} %param.17) | copy-start | bytes 6291460
  503.8 13.6 %all-to-all-start.4 = ((bf16[32,4,12]{2,1,0:T(4,128)(2,1)}), bf16[32,4,12]{2,1,0:T(4,128)(2,1)S(1)}, u32[]{:S(2)}, u32[]{:S(2)}) async-start(bf16[32,4,12]{2,1,0:T(4,128)(2,1)} %copy.162), calls=%async_computation.4 | async-start | bytes 65536 | tf_op jit(solution)/shard_map/all_to_all | solution.py:92
  511.2 226.4 %all-reduce.6.cloned.1.call-start = ((), (), s32[]{:S(2)}) async-start(), calls=%async_computation.12 | async-start | bytes 524288 | tf_op jit(solution)/shard_map/psum | solution.py:159
Sparse Core Ops, SparseCore 0:
  292.2 84.0 all-gather.2
  408.6 48.5 all-gather.4
  488.4 84.5 reduce-scatter.4
  576.7 85.8 reduce-scatter.2
Sparse Core Ops, SparseCore 1:
  404.7 76.7 all-reduce.3
  665.2 72.3 all-reduce.5
where the time goes:
time: 754 us; the launch traced here: 748 us
  waiting for transfers between devices  417 us (55%)
  local copies, waits for them, and re-layouts  168 us (22%)
  matrix products  56.7 us (8%)
  starting transfers between devices  39.4 us (5%)
  blocking collectives  29.6 us (4%)
  other arithmetic  21.5 us (3%)
  between operations  15.9 us (2%)
    reduce_scatter x1, waiting for transfers between devices, body(): lax.psum_scatter(key_part, 'context', scatter_dimension=0, tiled=True)  89.6 us
    all_to_all x1, waiting for transfers between devices, body(): lax.all_to_all(d_rows, 'context', split_axis=0, concat_axis=0, tiled=True)  74.7 us
    psum x1, waiting for transfers between devices, body(): d_normed, d_route = lax.psum((partial_rows, partial_weight), 'expert')  70.9 us
    psum x1, waiting for transfers between devices, body(): d_keys, d_values = lax.psum((key_wide, value_wide), 'expert')  69.4 us
    all_to_all x1, waiting for transfers between devices, body(): lax.all_to_all(send_rows.reshape(block_shape), 'context', split_axis=0, c...  59.7 us
    scatter x2, local copies, waits for them, and re-layouts, body(): jnp.zeros((buffer_rows, feature_width), jnp.bfloat16).at[position]  48.4 us
    psum x1, blocking collectives, body(): d_normed, d_route = lax.psum((partial_rows, partial_weight), 'expert')  29.6 us
    all_to_all x1, waiting for transfers between devices, body(): lax.all_to_all(send_grad.reshape(block_shape), 'context', split_axis=0, c...  28.3 us
  transfers between devices with their start and end apart: 11, of which 8 were waited for; matrix products, arithmetic and copies ran while one was open for 25% of the time, Pallas kernels for 0%

commit v1 on v0

v1 whole, which is shorter than its diff:
```python
import math

import jax
import jax.numpy as jnp
from jax import lax
from jax.experimental import pallas as pl
from jax.experimental.pallas import tpu as pltpu
from jax.sharding import PartitionSpec as P

HEAD_DIM = 128
CAP = 12
PAIR = 2 * CAP
EPS = 1e-06
BF = jnp.bfloat16
F32 = jnp.float32
SCALE = 1.0 / math.sqrt(HEAD_DIM)
NT = (((1,), (1,)), ((), ()))
TN = (((0,), (0,)), ((), ()))
MB = 1 << 20


def nt(a, b):
    return lax.dot_general(a, b, NT, preferred_element_type=F32)


def tn(a, b):
    return lax.dot_general(a, b, TN, preferred_element_type=F32)


def nn(a, b):
    return jnp.dot(a, b, preferred_element_type=F32)


def params(mib=60):
    return pltpu.CompilerParams(vmem_limit_bytes=mib * MB)


def whole(shape):
    return pl.BlockSpec(shape, lambda *_: (0,) * len(shape))


def lane_expert(quarter, per, count, shape):
    lane = lax.broadcasted_iota(jnp.int32, shape, 1)
    return jnp.where(lane < count, lane * per + quarter, -1)


def slot_split(shape, axis, first):
    slot = (lax.broadcasted_iota(jnp.int32, shape, axis) + first).astype(F32)
    lane = jnp.floor((slot + 0.5) * (1.0 / PAIR))
    rank = slot - PAIR * lane
    half = jnp.where(rank > CAP - 0.5, 1.0, 0.0)
    return lane, half, rank - CAP * half


def route_kernel(rows, per, count, q_ref, ids_ref, rw_ref, hid_ref, up_ref, gain_ref,
                 send_ref, st_ref, sw0_ref, sw1_ref, m_ref, r_ref, w_ref, n_ref):
    step = pl.program_id(0)
    tokens = ids_ref.shape[0]

    @pl.when(step == 0)
    def _():
        ids = ids_ref[...]
        weights = rw_ref[...].astype(F32)
        named = lane_expert(q_ref[0], per, count, (tokens, 128))
        member = jnp.zeros((tokens, 128), F32)
        weight = jnp.zeros((tokens, 128), F32)
        for k in range(ids.shape[1]):
            hit = ids[:, k : k + 1] == named
            member = member + jnp.where(hit, 1.0, 0.0)
            weight = weight + jnp.where(hit, weights[:, k : k + 1], 0.0)
        m_ref[...] = member.astype(BF)
        w_ref[...] = weight.astype(BF)
        row = lax.broadcasted_iota(jnp.int32, (tokens, tokens), 0)
        col = lax.broadcasted_iota(jnp.int32, (tokens, tokens), 1)
        below = jnp.where(col < row, 1.0, 0.0).astype(BF)
        r_ref[...] = nn(below, member.astype(BF)).astype(BF)
        wide = hid_ref[...].astype(F32)
        inv = lax.rsqrt(jnp.mean(wide * wide, axis=1, keepdims=True) + EPS)
        n_ref[:tokens] = (wide * inv * gain_ref[...]).astype(BF)
        n_ref[tokens:] = up_ref[...]

    first = step * rows
    member, rank, weight = m_ref[...], r_ref[...], w_ref[...]
    lane_of, half_of, rank_of = slot_split((rows, 128), 0, first)
    lane = lax.broadcasted_iota(jnp.int32, (rows, 128), 1).astype(F32)
    spread = jnp.where(lane == lane_of, 1.0, 0.0).astype(BF)
    chosen = (nt(spread, member) > 0.5) & (nt(spread, rank) == rank_of)
    s0 = jnp.where(chosen & (half_of < 0.5), 1.0, 0.0).astype(BF)
    s1 = jnp.where(chosen & (half_of > 0.5), 1.0, 0.0).astype(BF)
    send_ref[...] = nn(jnp.concatenate([s0, s1], axis=1), n_ref[...]).astype(BF)
    _, half_row, rank_row = slot_split((tokens, rows), 1, first)
    chosen_t = (nt(member, spread) > 0.5) & (nt(rank, spread) == rank_row)
    weight_t = nt(weight, spread)
    st_ref[...] = jnp.where(chosen_t & (half_row < 0.5), 1.0, 0.0).astype(BF)
    sw0_ref[...] = jnp.where(chosen_t & (half_row < 0.5), weight_t, 0.0).astype(BF)
    sw1_ref[...] = jnp.where(chosen_t & (half_row > 0.5), weight_t, 0.0).astype(BF)


def route(quarter, per, count, ids, weights, hidden, upstream, gain):
    tokens, width = hidden.shape
    rows = 384
    slots = count * PAIR
    matrix = pl.BlockSpec((tokens, rows), lambda i, p: (0, i))
    return pl.pallas_call(
        lambda *refs: route_kernel(rows, per, count, *refs),
        grid_spec=pltpu.PrefetchScalarGridSpec(
            num_scalar_prefetch=1,
            grid=(slots // rows,),
            in_specs=[
                whole((tokens, ids.shape[1])),
                whole((tokens, ids.shape[1])),
                whole((tokens, width)),
                whole((tokens, width)),
                whole((1, width)),
            ],
            out_specs=[pl.BlockSpec((rows, width), lambda i, p: (i, 0)), matrix, matrix, matrix],
            scratch_shapes=[
                pltpu.VMEM((tokens, 128), BF),
                pltpu.VMEM((tokens, 128), BF),
                pltpu.VMEM((tokens, 128), BF),
                pltpu.VMEM((2 * tokens, width), BF),
            ],
        ),
        out_shape=[jax.ShapeDtypeStruct((slots, width), BF)]
        + [jax.ShapeDtypeStruct((tokens, slots), BF)] * 3,
        compiler_params=params(),
        name="route",
    )(quarter, ids, weights, hidden, upstream, gain)


def expert_kernel(rows, q_ref, xy_ref, go_ref, uo_ref, do_ref, *refs):
    gu_refs, d_refs, out_ref = refs[:3], refs[3:6], refs[6]
    half_width = xy_ref.shape[1] // 2
    xy = xy_ref[...]
    w_gate = jnp.concatenate([go_ref[0]] + [r[0] for r in gu_refs], axis=1)
    w_up = jnp.concatenate([uo_ref[0]] + [r[1] for r in gu_refs], axis=1)
    w_down = jnp.concatenate([do_ref[0]] + [r[0] for r in d_refs], axis=0)
    gate = nn(xy, w_gate)
    up = nn(xy, w_up)
    proj = pltpu.roll(nt(xy, w_down), rows - CAP, 0)
    sig = 1.0 / (1.0 + jnp.exp(-gate))
    silu = gate * sig
    act = (silu * up).astype(BF).astype(F32)
    d_gate = (proj * up * (sig * (1.0 + gate * (1.0 - sig)))).astype(BF)
    d_up = (proj * silu).astype(BF)
    d_route = jnp.sum(act * proj, axis=1, keepdims=True)
    d_rows = nt(jnp.concatenate([d_gate, d_up], axis=1), jnp.concatenate([w_gate, w_up], axis=1))
    _, half, _ = slot_split((rows, 1), 0, 0)
    out = jnp.where(half > 0.5, pltpu.roll(d_rows[:, half_width:], CAP, 0), d_rows[:, :half_width])
    out_ref[:, :half_width] = out.astype(BF)
    out_ref[:, half_width:] = jnp.broadcast_to(d_route, (rows, 128)).astype(BF)


def expert(quarter, xy, w_gate, w_up, w_down, got_in, got_down):
    slots, width = xy.shape
    unit = w_gate.shape[2]
    rows = 384
    own = pl.BlockSpec((1, width, unit), lambda i, p: (p[0], 0, 0))
    return pl.pallas_call(
        lambda *refs: expert_kernel(rows, *refs),
        grid_spec=pltpu.PrefetchScalarGridSpec(
            num_scalar_prefetch=1,
            grid=(slots // rows,),
            in_specs=[
                pl.BlockSpec((rows, width), lambda i, p: (i, 0)),
                own,
                own,
                pl.BlockSpec((1, unit, width), lambda i, p: (p[0], 0, 0)),
            ]
            + [whole((2, width, unit))] * 3
            + [whole((1, unit, width))] * 3,
            out_specs=pl.BlockSpec((rows, width // 2 + 128), lambda i, p: (i, 0)),
        ),
        out_shape=jax.ShapeDtypeStruct((slots, width // 2 + 128), BF),
        compiler_params=params(),
        name="expert",
    )(quarter, xy, w_gate, w_up, w_down, *got_in, *got_down)


def gather_kernel(per, count, q_ref, back_ref, st_ref, sw0_ref, sw1_ref, ids_ref, hid_ref, gain_ref, out_ref):
    tokens, width = hid_ref.shape
    half_width = width // 2
    wide = hid_ref[...].astype(F32)
    inv = lax.rsqrt(jnp.mean(wide * wide, axis=1, keepdims=True) + EPS)
    rows = back_ref[:, :half_width]
    d_normed = jnp.concatenate([nn(sw0_ref[...], rows), nn(sw1_ref[...], rows)], axis=1)
    g = d_normed * gain_ref[...]
    inner = jnp.mean(g * wide, axis=1, keepdims=True)
    out_ref[:, :width] = (inv * g - wide * (inv * inv * inv * inner)).astype(BF)
    slots = back_ref.shape[0]
    lane_of, _, _ = slot_split((slots, 128), 0, 0)
    lane = lax.broadcasted_iota(jnp.int32, (slots, 128), 1).astype(F32)
    placed = jnp.where(lane == lane_of, back_ref[:, half_width:].astype(F32), 0.0).astype(BF)
    route = nn(st_ref[...], placed)
    named = lane_expert(q_ref[0], per, count, (tokens, 128))
    ids = ids_ref[...]
    column = lax.broadcasted_iota(jnp.int32, (tokens, 128), 1)
    out = jnp.zeros((tokens, 128), F32)
    for k in range(ids.shape[1]):
        value = jnp.sum(jnp.where(ids[:, k : k + 1] == named, route, 0.0), axis=1, keepdims=True)
        out = jnp.where(column == k, value, out)
    out_ref[:, width:] = out.astype(BF)


def on_chip(kernel, name, out_shape, scalars, arrays, scratch=()):
    vmem = pl.BlockSpec(memory_space=pltpu.VMEM)
    many = isinstance(out_shape, list)
    return pl.pallas_call(
        kernel,
        in_specs=[pl.BlockSpec(memory_space=pltpu.SMEM)] * len(scalars) + [vmem] * len(arrays),
        out_specs=[vmem] * len(out_shape) if many else vmem,
        out_shape=out_shape,
        scratch_shapes=list(scratch),
        compiler_params=params(),
        name=name,
    )(*scalars, *arrays)


def sum_first(ref):
    total = ref[0].astype(F32)
    for n in range(1, ref.shape[0]):
        total = total + ref[n].astype(F32)
    return total


def finish_kernel(z_ref, in_ref, up_ref, out_ref):
    parts, share, _ = in_ref.shape
    width = up_ref.shape[1]
    total = sum_first(in_ref)
    mine = up_ref[pl.ds(pl.multiple_of(z_ref[0] * share, share), share), :].astype(F32)
    done = jnp.concatenate([total[:, :width] + mine, total[:, width:]], axis=1).astype(BF)
    for n in range(parts):
        out_ref[n] = done


def add_kernel(a_ref, b_ref, out_ref):
    out_ref[...] = (a_ref[...].astype(F32) + b_ref[...].astype(F32)).astype(BF)


def spread_kernel(in_ref, out_ref):
    total = sum_first(in_ref).astype(BF)
    for n in range(out_ref.shape[0]):
        out_ref[n] = total


def last_kernel(in_ref, dk_ref, dv_ref):
    half = in_ref.shape[0] // 2
    for head in range(2):
        total = in_ref[head * half].astype(F32)
        for n in range(1, half):
            total = total + in_ref[head * half + n].astype(F32)
        at = slice(head * HEAD_DIM, (head + 1) * HEAD_DIM)
        dk_ref[:, at] = total[:, :HEAD_DIM]
        dv_ref[:, at] = total[:, HEAD_DIM:]


def heads_to_rows(x):
    return jnp.concatenate([x[:, :HEAD_DIM], x[:, HEAD_DIM:]], axis=0)


def probs_kernel(chunk, q_ref, a_ref, b_ref, p_ref, s_ref):
    half = a_ref.shape[0]
    query = heads_to_rows(q_ref[...])
    top = None
    for n in range(2 * half // chunk):
        src = a_ref if n * chunk < half else b_ref
        at = n * chunk % half
        s = nt(src[at : at + chunk, :HEAD_DIM], query) * SCALE
        s_ref[n * chunk : (n + 1) * chunk] = s
        most = jnp.max(s, axis=0, keepdims=True)
        top = most if top is None else jnp.maximum(top, most)
    total = jnp.zeros_like(top)
    for n in range(2 * half // chunk):
        e = jnp.exp(s_ref[n * chunk : (n + 1) * chunk] - top)
        s_ref[n * chunk : (n + 1) * chunk] = e
        total = total + jnp.sum(e, axis=0, keepdims=True)
    scale = 1.0 / total
    for n in range(2 * half // chunk):
        p_ref[n * chunk : (n + 1) * chunk] = (s_ref[n * chunk : (n + 1) * chunk] * scale).astype(BF)


def probs(queries, kv_a, kv_b):
    count = kv_a.shape[0] + kv_b.shape[0]
    rows = queries.shape[0] * 2
    return pl.pallas_call(
        lambda *refs: probs_kernel(512, *refs),
        out_shape=jax.ShapeDtypeStruct((count, rows), BF),
        scratch_shapes=[pltpu.VMEM((count, rows), F32)],
        compiler_params=params(),
        name="attention_probs",
    )(queries, kv_a, kv_b)


def grads_kernel(chunk, dh_ref, w_ref, q_ref, p_ref, a_ref, b_ref, dq_ref, da_ref, db_ref, dp_ref):
    half = a_ref.shape[0]
    width = w_ref.shape[1]
    d_out_w = nt(w_ref[...], dh_ref[:, :width]).astype(BF)
    d_one, d_two = d_out_w[:HEAD_DIM], d_out_w[HEAD_DIM:]
    d_out_t = jnp.concatenate([d_one, d_two], axis=1)
    d_out = jnp.concatenate([d_one.T, d_two.T], axis=0)
    query = heads_to_rows(q_ref[...])
    delta = jnp.zeros((1, d_out.shape[0]), F32)
    steps = 2 * half // chunk
    for n in range(steps):
        src = a_ref if n * chunk < half else b_ref
        at = n * chunk % half
        span = slice(n * chunk, (n + 1) * chunk)
        dp = nn(src[at : at + chunk, HEAD_DIM:], d_out_t)
        dp_ref[span] = dp
        delta = delta + jnp.sum(dp * p_ref[span].astype(F32), axis=0, keepdims=True)
    d_query = jnp.zeros((HEAD_DIM, d_out.shape[0]), F32)
    for n in range(steps):
        src, dst = (a_ref, da_ref) if n * chunk < half else (b_ref, db_ref)
        at = n * chunk % half
        span = slice(n * chunk, (n + 1) * chunk)
        p = p_ref[span]
        ds = (p.astype(F32) * (dp_ref[span] - delta)).astype(BF)
        dst[at : at + chunk, :HEAD_DIM] = (nn(ds, query) * SCALE).astype(BF)
        dst[at : at + chunk, HEAD_DIM:] = nn(p, d_out).astype(BF)
        d_query = d_query + tn(src[at : at + chunk, :HEAD_DIM], ds)
    d_query = (d_query * SCALE).T
    rows = q_ref.shape[0]
    dq_ref[:, :HEAD_DIM] = d_query[:rows]
    dq_ref[:, HEAD_DIM:] = d_query[rows:]


def body(hidden, upstream, norm_gain, route_ids, route_weights, w_gate, w_up, w_down, w_out, queries, keys, values):
    ctx_count = lax.axis_size("context")
    exp_count = lax.axis_size("expert")
    tokens, width = hidden.shape
    chips = ctx_count // 2
    per = w_gate.shape[0]
    slots = ctx_count * PAIR
    z = lax.axis_index("expert")
    quarter = z % per
    q_arr = quarter.astype(jnp.int32).reshape(1)
    z_arr = z.astype(jnp.int32).reshape(1)
    gain = norm_gain.reshape(1, width)
    swap_core = [(i, i ^ 1) for i in range(ctx_count)]
    same_core = [[2 * i + k for i in range(chips)] for k in range(2)]

    def far(core):
        return -2 if core == 0 else 2

    def moves(step):
        return [
            (i * ctx_count + c, (i + step(c % 2)) % exp_count * ctx_count + c)
            for c in range(ctx_count)
            for i in range(exp_count)
        ]

    got_in, got_down = [], []
    for shift, step in ((1, lambda core: 1), (per - 1, lambda core: -1), (2, far)):
        which = (z + shift) % per
        pick = [lax.dynamic_slice_in_dim(w, which, 1, 0) for w in (w_gate, w_up, w_down)]
        pair = moves(step)
        got_in.append(lax.ppermute(jnp.concatenate(pick[:2], axis=0), ("expert", "context"), pair))
        got_down.append(lax.ppermute(pick[2], ("expert", "context"), pair))

    kv_head = z // (exp_count // 2)
    own_kv = jnp.concatenate(
        [lax.dynamic_slice_in_dim(a, kv_head * HEAD_DIM, HEAD_DIM, 1) for a in (keys, values)], axis=1)
    kv_a = lax.all_gather(own_kv, "context", axis=0, tiled=True, axis_index_groups=same_core)

    send, st, sw0, sw1 = route(q_arr, per, ctx_count, route_ids, route_weights, hidden, upstream, gain)
    xy = lax.all_to_all(send.reshape(ctx_count, PAIR, width), "context", 0, 0, tiled=True)
    rows = expert(q_arr, xy.reshape(slots, width), w_gate, w_up, w_down, got_in, got_down)
    narrow = width // 2 + 128
    rows, kv_a = lax.optimization_barrier((rows, kv_a))
    rows = lax.all_to_all(rows.reshape(ctx_count, PAIR, narrow), "context", 0, 0, tiled=True)
    wide = width + 128
    q = on_chip(
        lambda *refs: gather_kernel(per, ctx_count, *refs), "gather_rows",
        jax.ShapeDtypeStruct((tokens, wide), BF),
        [q_arr], [rows.reshape(slots, narrow), st, sw0, sw1, route_ids, hidden, gain])

    share = tokens // exp_count
    parts = (exp_count, share, wide)
    arrived = lax.all_to_all(q.reshape(parts), "expert", 0, 0, tiled=True)
    done = on_chip(finish_kernel, "finish_hidden", jax.ShapeDtypeStruct(parts, BF), [z_arr], [arrived, upstream])
    done = lax.all_to_all(done, "expert", 0, 0, tiled=True).reshape(tokens, wide)
    d_hidden = done[:, :width]
    d_route = done[:, width : width + route_ids.shape[1]].astype(F32)

    kv_b = lax.ppermute(kv_a, "context", swap_core)
    queries, q = lax.optimization_barrier((queries, q))
    soft = probs(queries, kv_a, kv_b)
    d_queries, da, db = on_chip(
        lambda *refs: grads_kernel(512, *refs), "attention_grads",
        [
            jax.ShapeDtypeStruct(queries.shape, F32),
            jax.ShapeDtypeStruct(kv_a.shape, BF),
            jax.ShapeDtypeStruct(kv_b.shape, BF),
        ],
        [], [done, w_out, queries, soft, kv_a, kv_b], [pltpu.VMEM(soft.shape, F32)])
    db = lax.ppermute(db, "context", swap_core)
    part = on_chip(add_kernel, "add_cores", jax.ShapeDtypeStruct(da.shape, BF), [], [da, db])
    part = lax.all_to_all(
        part.reshape(chips, tokens, 2 * HEAD_DIM), "context", 0, 0, tiled=True, axis_index_groups=same_core)
    block = (exp_count, tokens, 2 * HEAD_DIM)
    part = on_chip(spread_kernel, "sum_chips", jax.ShapeDtypeStruct(block, BF), [], [part])
    part = lax.all_to_all(part, "expert", 0, 0, tiled=True)
    d_keys, d_values = on_chip(
        last_kernel, "sum_heads", [jax.ShapeDtypeStruct((tokens, 2 * HEAD_DIM), F32)] * 2, [], [part])
    return (d_hidden, d_route, d_queries, d_keys, d_values)


def solution(mesh):
    placed = (
        P("context", None),
        P("context", None),
        P(),
        P("context", None),
        P("context", None),
        P("context", None, "expert"),
        P("context", None, "expert"),
        P("context", "expert", None),
        P("expert", None),
        P("context", "expert"),
        P("context", None),
        P("context", None),
    )
    return jax.shard_map(
        body,
        mesh=mesh,
        in_specs=placed,
        out_specs=(
            P("context", None),
            P("context", None),
            P("context", "expert"),
            P("context", None),
            P("context", None),
        ),
        check_vma=False,
    )
```

time: 754 us -> 272 us (0.36)
  waiting for transfers between devices: 417 us -> 111 us
  local copies, waits for them, and re-layouts: 168 us -> 14.8 us
  matrix products: 56.7 us -> 0 us
  Pallas kernels: 0 us -> 42.6 us
  blocking collectives: 29.6 us -> 56.6 us
  other arithmetic: 21.5 us -> 0.94 us
  starting transfers between devices: 39.4 us -> 30.6 us
    psum x2 -> x0, waiting for transfers between devices: 140 us -> none  [the longest x1 70.9 us: body(): d_normed, d_route = lax.psum((partial_rows, partial_weight), 'expert')]
    all_to_all x5 -> x4, waiting for transfers between devices: 169 us -> 46.4 us  [the longest x1 18.5 us: body(): arrived = lax.all_to_all(q.reshape(parts), 'expert', 0, 0, tiled=True)]
    reduce_scatter x2 -> x0, waiting for transfers between devices: 108 us -> none  [the longest x1 89.6 us: body(): lax.psum_scatter(key_part, 'context', scatter_dimension=0, tiled=True)]
    ppermute x0 -> x8, waiting for transfers between devices: none -> 64.3 us  [the longest x3 61.5 us: body(): got_down.append(lax.ppermute(pick[2], ('expert', 'context'), pair))]
    reshape x10 -> x0, local copies, waits for them, and re-layouts: 57.5 us -> none  [the longest x2 22.6 us: body(): send_grad.reshape(block_shape)]
    dot_general x12 -> x0, matrix products: 56.7 us -> none  [the longest x1 9.06 us: expert_terms(): jnp.einsum('slnf,ldf->slnd', d_up, w_up, preferred_element_type=jnp.float32)]
    all_to_all x0 -> x2, blocking collectives: none -> 56.6 us  [the longest x1 34.7 us: body(): lax.all_to_all(rows.reshape(ctx_count, PAIR, narrow), 'context', 0, 0, ti...]
    scatter x3 -> x0, local copies, waits for them, and re-layouts: 56 us -> none  [the longest x2 48.4 us: body(): jnp.zeros((buffer_rows, feature_width), jnp.bfloat16).at[position]]
  transfers between devices with their start and end apart: 11 -> 13, of which waited for: 8 -> 7; matrix products, arithmetic and copies ran while one was open for 25% -> 2% of each run, Pallas kernels for 0% -> 7%
where the time goes in v1:
time: 272 us; the launch traced here: 270 us
  waiting for transfers between devices  111 us (41%)
  blocking collectives  56.6 us (21%)
  Pallas kernels  42.6 us (16%)
  starting transfers between devices  30.6 us (11%)
  local copies, waits for them, and re-layouts  14.8 us (5%)
  between operations  14.3 us (5%)
    ppermute x3, waiting for transfers between devices, body(): got_down.append(lax.ppermute(pick[2], ('expert', 'context'), pair))  61.5 us
    all_to_all x1, blocking collectives, body(): lax.all_to_all(rows.reshape(ctx_count, PAIR, narrow), 'context', 0, 0, ti...  34.7 us
    all_to_all x1, blocking collectives, body(): lax.all_to_all(part.reshape(chips, tokens, 2 * HEAD_DIM), 'context', 0, 0...  21.9 us
    pallas_call x6, Pallas kernels, on_chip(): pl.pallas_call(kernel, in_specs=[pl.BlockSpec(memory_space=pltpu.SMEM)] *...  19.9 us
    all_to_all x1, waiting for transfers between devices, body(): arrived = lax.all_to_all(q.reshape(parts), 'expert', 0, 0, tiled=True)  18.5 us
    all_to_all x1, waiting for transfers between devices, body(): part = lax.all_to_all(part, 'expert', 0, 0, tiled=True)  15.3 us
    pallas_call x1, Pallas kernels, expert(): pl.pallas_call(lambda *refs: expert_kernel(rows, *refs), grid_spec=pltpu....  13.1 us
    all_to_all x1, waiting for transfers between devices, body(): lax.all_to_all(done, 'expert', 0, 0, tiled=True).reshape(tokens, wide)  12.5 us
  transfers between devices with their start and end apart: 13, of which 7 were waited for; matrix products, arithmetic and copies ran while one was open for 2% of the time, Pallas kernels for 7%

profile of v1, /device:TPU:2, one launch (start us, length us, event | category | flops | bytes accessed | tf_op | source)
XLA Modules:
  0.0 270.5 jit_solution(14880682816511557627)
XLA Ops:
  7.2 1.4 copy.17.refs_1_.refs_5_
  8.6 1.4 copy.18.refs_2_
  10.0 4.6 %route.1 = (bf16[768,2048]{1,0:T(8,128)(2,1)}, bf16[128,768]{1,0:T(8,128)(2,1)}, bf16[128,768]{1,0:T(8,128)(2,1)}, bf16[128,768]{1,0:T(8,128)(2,1)}) custom-call(s32[1]{0:T(128)} %bitcast.1.refs_0_, s32[128,8]{1,0:T(8,128)} %copy.17.refs_1_.refs_5_, bf16[128,8]{1,0:T(8,128)(2,1)} %copy.18.refs_2_, bf16[128,2048]{1,0:T(8,128)(2,1)} %refs_6_.1, ...), custom_call_target="tpu_custom_call" | custom-call | tf_op jit(solution)/shard_map/route/pallas_call | solution.py:104
  14.6 7.8 %all-to-all-start = ((bf16[32,24,2048]{2,1,0:T(8,128)(2,1)}), bf16[32,24,2048]{2,1,0:T(8,128)(2,1)S(1)}, u32[]{:S(2)}, u32[]{:S(2)}) async-start(bf16[32,24,2048]{2,1,0:T(8,128)(2,1)} %bitcast.17), calls=%async_computation | async-start | bytes 6291456 | tf_op jit(solution)/shard_map/all_to_all | solution.py:366
  22.3 0.0 all-gather.2.cloned.1.call-start
  22.5 0.6 pad_maximum_fusion.3
  23.2 2.0 constant_dynamic-slice_fusion.5
  25.2 0.1 pad_maximum_fusion.1
  25.3 5.9 %collective-permute-start.1 = (bf16[2,2048,128]{2,1,0:T(8,128)(2,1)S(1)}, bf16[2,2048,128]{2,1,0:T(8,128)(2,1)S(1)}, u32[]{:S(2)}, u32[]{:S(2)}) collective-permute-start(bf16[2,2048,128]{2,1,0:T(8,128)(2,1)S(1)} %pad_maximum_fusion.1), channel_id=1, source_target_pairs={{0,224},{32,0},{64,32},{96,64},{128,96},{160,128},{192,160},{224,1... | collective-permute-start | bytes 3145736 | tf_op jit(solution)/shard_map/ppermute | solution.py:357
  31.2 0.1 pad_maximum_fusion.2
  31.3 1.5 collective-permute-start.2
  32.9 0.1 constant_dynamic-slice_fusion.2
  33.0 1.1 collective-permute-start.3
  34.1 0.1 pad_maximum_fusion
  34.2 1.1 collective-permute-start
  35.3 2.2 collective-permute-start.4
  37.5 17.3 %collective-permute-done.3.refs_8_ = bf16[1,128,2048]{2,1,0:T(8,128)(2,1)S(1)} collective-permute-done((bf16[1,128,2048]{2,1,0:T(8,128)(2,1)S(1)}, bf16[1,128,2048]{2,1,0:T(8,128)(2,1)S(1)}, u32[]{:S(2)}, u32[]{:S(2)}) %collective-permute-start.3) | collective-permute-done | bytes 524320 | tf_op jit(solution)/shard_map/ppermute | solution.py:358
  54.8 38.6 %collective-permute-done.4.refs_9_ = bf16[1,128,2048]{2,1,0:T(8,128)(2,1)S(1)} collective-permute-done((bf16[1,128,2048]{2,1,0:T(8,128)(2,1)S(1)}, bf16[1,128,2048]{2,1,0:T(8,128)(2,1)S(1)}, u32[]{:S(2)}, u32[]{:S(2)}) %collective-permute-start.4) | collective-permute-done | bytes 524320 | tf_op jit(solution)/shard_map/ppermute | solution.py:358
  93.3 5.6 %collective-permute-done.5.refs_10_ = bf16[1,128,2048]{2,1,0:T(8,128)(2,1)S(1)} collective-permute-done((bf16[1,128,2048]{2,1,0:T(8,128)(2,1)S(1)}, bf16[1,128,2048]{2,1,0:T(8,128)(2,1)S(1)}, u32[]{:S(2)}, u32[]{:S(2)}) %collective-permute-start.5) | collective-permute-done | bytes 524320 | tf_op jit(solution)/shard_map/ppermute | solution.py:358
  99.0 0.8 copy-done.13
  99.8 0.4 copy-done.8
  100.2 1.1 copy-done.9
  101.3 1.6 copy-done
  102.9 13.1 %expert.1 = bf16[768,1152]{1,0:T(8,128)(2,1)} custom-call(s32[1]{0:T(128)} %bitcast.1.refs_0_, bf16[768,2048]{1,0:T(8,128)(2,1)} %bitcast.10, bf16[4,2048,128]{2,1,0:T(8,128)(2,1)} %refs_2_.2, bf16[4,2048,128]{2,1,0:T(8,128)(2,1)} %refs_3_.3, bf16[4,128,2048]{2,1,0:T(8,128)(2,1)} %refs_4_.3, bf16[2,2048,128]{2,1,0:T(8,128)(2,1)} %collective-permute-done.refs_5_, ...), custom_call_target="tpu_custom_call" | custom-call | tf_op jit(solution)/shard_map/expert/pallas_call | solution.py:159
  116.0 34.7 %all_to_all.30 = bf16[32,24,1152]{2,1,0:T(8,128)(2,1)} all-to-all(bf16[32,24,1152]{2,1,0:T(8,128)(2,1)} %bitcast.11), channel_id=1, replica_groups=mesh['expert'=8,'context'=32] {'context'}, dimensions={0} | all-to-all | bytes 3538944 | tf_op jit(solution)/shard_map/all_to_all | solution.py:370
  150.6 3.7 %gather_rows.1 = bf16[128,2176]{1,0:T(8,128)(2,1)} custom-call(s32[1]{0:T(128)} %bitcast.1.refs_0_, bf16[768,1152]{1,0:T(8,128)(2,1)} %bitcast.12, bf16[128,768]{1,0:T(8,128)(2,1)} %get-tuple-element.19.refs_2_, bf16[128,768]{1,0:T(8,128)(2,1)} %get-tuple-element.20.refs_3_, bf16[128,768]{1,0:T(8,128)(2,1)} %get-tuple-element.21.refs_4_, ...), custom_call_target="tpu_custom_call" | custom-call | tf_op jit(solution)/shard_map/gather_rows/pallas_call | solution.py:208
  154.3 3.7 %all-to-all-start.2 = ((bf16[8,16,2176]{2,1,0:T(8,128)(2,1)}), bf16[8,16,2176]{2,1,0:T(8,128)(2,1)S(1)}, u32[]{:S(2)}, u32[]{:S(2)}) async-start(bf16[8,16,2176]{2,1,0:T(8,128)(2,1)} %bitcast.18), calls=%async_computation.2 | async-start | bytes 1114112 | tf_op jit(solution)/shard_map/all_to_all | solution.py:379
  158.0 0.2 collective-permute-start.6
  158.3 18.5 %all-to-all-done.2.in_ref = bf16[8,16,2176]{2,1,0:T(8,128)(2,1)S(1)} async-done(((bf16[8,16,2176]{2,1,0:T(8,128)(2,1)}), bf16[8,16,2176]{2,1,0:T(8,128)(2,1)S(1)}, u32[]{:S(2)}, u32[]{:S(2)}) %all-to-all-start.2) | async-done | bytes 557088 | tf_op jit(solution)/shard_map/all_to_all | solution.py:379
  176.8 0.8 copy-done.6
  177.6 2.1 finish_hidden.1
  179.7 3.5 %all-to-all-start.3 = ((bf16[8,16,2176]{2,1,0:T(8,128)(2,1)}), bf16[8,16,2176]{2,1,0:T(8,128)(2,1)S(1)}, u32[]{:S(2)}, u32[]{:S(2)}) async-start(bf16[8,16,2176]{2,1,0:T(8,128)(2,1)} %finish_hidden.1), calls=%async_computation.3 | async-start | bytes 1114112 | tf_op jit(solution)/shard_map/all_to_all | solution.py:381
  183.2 1.0 copy-done.5
  184.2 5.1 %attention_probs.1.refs_3_ = bf16[4096,256]{1,0:T(8,128)(2,1)} custom-call(bf16[128,256]{1,0:T(8,128)(2,1)} %refs_2_.3, bf16[2048,256]{1,0:T(8,128)(2,1)} %all-gather.2.cloned.1.call-done.refs_1_.refs_4_, bf16[2048,256]{1,0:T(8,128)(2,1)} %copy-done.5), custom_call_target="tpu_custom_call" | custom-call | tf_op jit(solution)/shard_map/attention_probs/pallas_call | solution.py:285
  189.3 12.5 %all-to-all-done.3 = bf16[8,16,2176]{2,1,0:T(8,128)(2,1)S(1)} async-done(((bf16[8,16,2176]{2,1,0:T(8,128)(2,1)}), bf16[8,16,2176]{2,1,0:T(8,128)(2,1)S(1)}, u32[]{:S(2)}, u32[]{:S(2)}) %all-to-all-start.3) | async-done | bytes 557088 | tf_op jit(solution)/shard_map/all_to_all | solution.py:381
  201.8 0.8 copy-done.2
  202.6 7.4 %attention_grads.1 = (f32[128,256]{1,0:T(8,128)}, bf16[2048,256]{1,0:T(8,128)(2,1)}, bf16[2048,256]{1,0:T(8,128)(2,1)}) custom-call(bf16[128,2176]{1,0:T(8,128)(2,1)} %bitcast.13, bf16[256,2048]{1,0:T(8,128)(2,1)} %refs_1_.2, bf16[128,256]{1,0:T(8,128)(2,1)} %refs_2_.3, bf16[4096,256]{1,0:T(8,128)(2,1)} %attention_probs.1.refs_3_, ...), custom_call_target="tpu_custom_call" | custom-call | tf_op jit(solution)/shard_map/attention_grads/pallas_call | solution.py:208
  210.0 2.8 %collective-permute-done.7.b_ref = bf16[2048,256]{1,0:T(8,128)(2,1)S(1)} collective-permute-done((bf16[2048,256]{1,0:T(8,128)(2,1)}, bf16[2048,256]{1,0:T(8,128)(2,1)S(1)}, u32[]{:S(2)}, u32[]{:S(2)}) %collective-permute-start.7) | collective-permute-done | bytes 1048608 | tf_op jit(solution)/shard_map/ppermute | solution.py:396
  212.9 1.0 copy-done.10
  213.8 2.8 %add_cores.1 = bf16[2048,256]{1,0:T(8,128)(2,1)} custom-call(bf16[2048,256]{1,0:T(8,128)(2,1)} %get-tuple-element.25.a_ref, bf16[2048,256]{1,0:T(8,128)(2,1)} %copy-done.10), custom_call_target="tpu_custom_call" | custom-call | tf_op jit(solution)/shard_map/add_cores/pallas_call | solution.py:208
  216.6 21.9 %all_to_all.31.in_ref = bf16[16,128,256]{2,1,0:T(8,128)(2,1)} all-to-all(bf16[16,128,256]{2,1,0:T(8,128)(2,1)} %bitcast.16), channel_id=1, replica_groups={{0,2,4,6,8,10,12,14,16,18,20,22,24,26,28,30},{1,3,5,7,9,11,13,15,17,19,..., dimensions={0} | all-to-all | bytes 2097152 | tf_op jit(solution)/shard_map/all_to_all | solution.py:398
  238.5 2.2 sum_chips.1
  240.7 3.5 %all-to-all-start.5 = ((bf16[8,128,256]{2,1,0:T(8,128)(2,1)}), bf16[8,128,256]{2,1,0:T(8,128)(2,1)S(1)}, u32[]{:S(2)}, u32[]{:S(2)}) async-start(bf16[8,128,256]{2,1,0:T(8,128)(2,1)} %sum_chips.1), calls=%async_computation.5 | async-start | bytes 1048576 | tf_op jit(solution)/shard_map/all_to_all | solution.py:402
  244.2 0.8 slice.8
  245.1 0.7 copy.20
  245.7 15.3 %all-to-all-done.5.in_ref = bf16[8,128,256]{2,1,0:T(8,128)(2,1)S(1)} async-done(((bf16[8,128,256]{2,1,0:T(8,128)(2,1)}), bf16[8,128,256]{2,1,0:T(8,128)(2,1)S(1)}, u32[]{:S(2)}, u32[]{:S(2)}) %all-to-all-start.5) | async-done | bytes 524320 | tf_op jit(solution)/shard_map/all_to_all | solution.py:402
  261.1 0.8 copy-done.7
  261.9 1.8 sum_heads.1
  (34 shorter events, 0.1 us)
Async XLA Ops:
  14.6 7.8 %copy-start.14 = (bf16[128,256]{1,0:T(8,128)(2,1)S(1)}, bf16[128,256]{1,0:T(8,128)(2,1)}, u32[]{:S(2)}) copy-start(bf16[128,256]{1,0:T(8,128)(2,1)} %param.23) | copy-start | bytes 196612
  14.6 7.9 %copy-start.15 = (bf16[128,256]{1,0:T(8,128)(2,1)S(1)}, bf16[128,256]{1,0:T(8,128)(2,1)}, u32[]{:S(2)}) copy-start(bf16[128,256]{1,0:T(8,128)(2,1)} %param.22) | copy-start | bytes 196612
  14.6 86.7 %all-to-all-start = ((bf16[32,24,2048]{2,1,0:T(8,128)(2,1)}), bf16[32,24,2048]{2,1,0:T(8,128)(2,1)S(1)}, u32[]{:S(2)}, u32[]{:S(2)}) async-start(bf16[32,24,2048]{2,1,0:T(8,128)(2,1)} %bitcast.17), calls=%async_computation | async-start | bytes 6291456 | tf_op jit(solution)/shard_map/all_to_all | solution.py:366
  22.3 93.6 %all-gather.2.cloned.1.call-start = ((), (), s32[]{:S(2)}) async-start(), calls=%async_computation.6 | async-start | bytes 1114112 | tf_op jit(solution)/shard_map/all_gather | solution.py:363
  25.2 7.7 %copy-start.1 = (bf16[4,128,2048]{2,1,0:T(8,128)(2,1)S(1)}, bf16[4,128,2048]{2,1,0:T(8,128)(2,1)}, u32[]{:S(2)}) copy-start(bf16[4,128,2048]{2,1,0:T(8,128)(2,1)} %refs_4_.3) | copy-start | bytes 6291460
  25.3 73.6 %collective-permute-start.1 = (bf16[2,2048,128]{2,1,0:T(8,128)(2,1)S(1)}, bf16[2,2048,128]{2,1,0:T(8,128)(2,1)S(1)}, u32[]{:S(2)}, u32[]{:S(2)}) collective-permute-start(bf16[2,2048,128]{2,1,0:T(8,128)(2,1)S(1)} %pad_maximum_fusion.1), channel_id=1, source_target_pairs={{0,224},{32,0},{64,32},{96,64},{128,96},{160,128},{192,160},{224,1... | collective-permute-start | bytes 3145736 | tf_op jit(solution)/shard_map/ppermute | solution.py:357
  31.3 67.6 %collective-permute-start.2 = (bf16[2,2048,128]{2,1,0:T(8,128)(2,1)S(1)}, bf16[2,2048,128]{2,1,0:T(8,128)(2,1)S(1)}, u32[]{:S(2)}, u32[]{:S(2)}) collective-permute-start(bf16[2,2048,128]{2,1,0:T(8,128)(2,1)S(1)} %pad_maximum_fusion.2), channel_id=1, source_target_pairs={{0,192},{32,224},{64,0},{96,32},{128,64},{160,96},{192,128},{224,1... | collective-permute-start | bytes 3145736 | tf_op jit(solution)/shard_map/ppermute | solution.py:357
  33.0 21.8 %collective-permute-start.3 = (bf16[1,128,2048]{2,1,0:T(8,128)(2,1)S(1)}, bf16[1,128,2048]{2,1,0:T(8,128)(2,1)S(1)}, u32[]{:S(2)}, u32[]{:S(2)}) collective-permute-start(bf16[1,128,2048]{2,1,0:T(8,128)(2,1)S(1)} %get-tuple-element.36), channel_id=1, source_target_pairs={{0,32},{32,64},{64,96},{96,128},{128,160},{160,192},{192,224},{224... | collective-permute-start | bytes 1572872 | tf_op jit(solution)/shard_map/ppermute | solution.py:358
  34.2 67.1 %collective-permute-start = (bf16[2,2048,128]{2,1,0:T(8,128)(2,1)S(1)}, bf16[2,2048,128]{2,1,0:T(8,128)(2,1)}, u32[]{:S(2)}, u32[]{:S(2)}) collective-permute-start(bf16[2,2048,128]{2,1,0:T(8,128)(2,1)S(1)} %pad_maximum_fusion), channel_id=1, source_target_pairs={{0,32},{32,64},{64,96},{96,128},{128,160},{160,192},{192,224},{224... | collective-permute-start | bytes 3145736 | tf_op jit(solution)/shard_map/ppermute | solution.py:357
  35.3 58.1 %collective-permute-start.4 = (bf16[1,128,2048]{2,1,0:T(8,128)(2,1)S(1)}, bf16[1,128,2048]{2,1,0:T(8,128)(2,1)S(1)}, u32[]{:S(2)}, u32[]{:S(2)}) collective-permute-start(bf16[1,128,2048]{2,1,0:T(8,128)(2,1)S(1)} %get-tuple-element.35), channel_id=1, source_target_pairs={{0,224},{32,0},{64,32},{96,64},{128,96},{160,128},{192,160},{224,1... | collective-permute-start | bytes 1572872 | tf_op jit(solution)/shard_map/ppermute | solution.py:358
  54.8 44.2 %copy-start.11 = (bf16[1,128,2048]{2,1,0:T(8,128)(2,1)}, bf16[1,128,2048]{2,1,0:T(8,128)(2,1)S(1)}, u32[]{:S(2)}) copy-start(bf16[1,128,2048]{2,1,0:T(8,128)(2,1)S(1)} %collective-permute-done.3.refs_8_) | copy-start | bytes 1572868
  54.8 44.2 %collective-permute-start.5 = (bf16[1,128,2048]{2,1,0:T(8,128)(2,1)S(1)}, bf16[1,128,2048]{2,1,0:T(8,128)(2,1)S(1)}, u32[]{:S(2)}, u32[]{:S(2)}) collective-permute-start(bf16[1,128,2048]{2,1,0:T(8,128)(2,1)S(1)} %get-tuple-element.34), channel_id=1, source_target_pairs={{0,192},{32,224},{64,0},{96,32},{128,64},{160,96},{192,128},{224,1... | collective-permute-start | bytes 1572872 | tf_op jit(solution)/shard_map/ppermute | solution.py:358
  93.3 5.6 %copy-start.12 = (bf16[1,128,2048]{2,1,0:T(8,128)(2,1)}, bf16[1,128,2048]{2,1,0:T(8,128)(2,1)S(1)}, u32[]{:S(2)}) copy-start(bf16[1,128,2048]{2,1,0:T(8,128)(2,1)S(1)} %collective-permute-done.4.refs_9_) | copy-start | bytes 1572868
  99.0 0.8 copy-start.13
  99.0 1.2 copy-start.8
  100.2 1.1 copy-start.9
  101.3 1.6 copy-start
  150.6 7.4 %copy-start.4 = (bf16[2048,256]{1,0:T(8,128)(2,1)S(1)}, bf16[2048,256]{1,0:T(8,128)(2,1)}, u32[]{:S(2)}) copy-start(bf16[2048,256]{1,0:T(8,128)(2,1)} %all-gather.2.cloned.1.call-done.refs_1_.refs_4_) | copy-start | bytes 3145732
  154.3 22.4 %all-to-all-start.2 = ((bf16[8,16,2176]{2,1,0:T(8,128)(2,1)}), bf16[8,16,2176]{2,1,0:T(8,128)(2,1)S(1)}, u32[]{:S(2)}, u32[]{:S(2)}) async-start(bf16[8,16,2176]{2,1,0:T(8,128)(2,1)} %bitcast.18), calls=%async_computation.2 | async-start | bytes 1114112 | tf_op jit(solution)/shard_map/all_to_all | solution.py:379
  158.0 25.2 %collective-permute-start.6 = (bf16[2048,256]{1,0:T(8,128)(2,1)S(1)}, bf16[2048,256]{1,0:T(8,128)(2,1)S(1)}, u32[]{:S(2)}, u32[]{:S(2)}) collective-permute-start(bf16[2048,256]{1,0:T(8,128)(2,1)S(1)} %copy-done.4), channel_id=1, source_target_pairs={{0,1},{1,0},{2,3},{3,2},{4,5},{5,4},{6,7},{7,6},{8,9},{9,8},{10,11... | collective-permute-start | bytes 3145736 | tf_op jit(solution)/shard_map/ppermute | solution.py:385
  176.8 0.8 copy-start.6
  179.7 22.2 %all-to-all-start.3 = ((bf16[8,16,2176]{2,1,0:T(8,128)(2,1)}), bf16[8,16,2176]{2,1,0:T(8,128)(2,1)S(1)}, u32[]{:S(2)}, u32[]{:S(2)}) async-start(bf16[8,16,2176]{2,1,0:T(8,128)(2,1)} %finish_hidden.1), calls=%async_computation.3 | async-start | bytes 1114112 | tf_op jit(solution)/shard_map/all_to_all | solution.py:381
  183.2 1.0 copy-start.5
  201.8 0.8 copy-start.2
  210.0 2.9 %collective-permute-start.7 = (bf16[2048,256]{1,0:T(8,128)(2,1)}, bf16[2048,256]{1,0:T(8,128)(2,1)S(1)}, u32[]{:S(2)}, u32[]{:S(2)}) collective-permute-start(bf16[2048,256]{1,0:T(8,128)(2,1)} %get-tuple-element.26), channel_id=1, source_target_pairs={{0,1},{1,0},{2,3},{3,2},{4,5},{5,4},{6,7},{7,6},{8,9},{9,8},{10,11... | collective-permute-start | bytes 3145736 | tf_op jit(solution)/shard_map/ppermute | solution.py:396
  212.9 1.0 copy-start.10
  216.6 27.6 %copy-start.3 = (bf16[8,16,2176]{2,1,0:T(8,128)(2,1)S(1)}, bf16[8,16,2176]{2,1,0:T(8,128)(2,1)}, u32[]{:S(2)}) copy-start(bf16[8,16,2176]{2,1,0:T(8,128)(2,1)} %copy-done.2) | copy-start | bytes 1671172
  240.7 20.4 %all-to-all-start.5 = ((bf16[8,128,256]{2,1,0:T(8,128)(2,1)}), bf16[8,128,256]{2,1,0:T(8,128)(2,1)S(1)}, u32[]{:S(2)}, u32[]{:S(2)}) async-start(bf16[8,128,256]{2,1,0:T(8,128)(2,1)} %sum_chips.1), calls=%async_computation.5 | async-start | bytes 1048576 | tf_op jit(solution)/shard_map/all_to_all | solution.py:402
  261.1 0.8 copy-start.7
Sparse Core Ops, SparseCore 0:
  26.2 61.4 all-gather.1

commit v2 on v1

v2 whole, which is shorter than its diff:
```python
import math

import jax
import jax.numpy as jnp
from jax import lax
from jax.experimental import pallas as pl
from jax.experimental.pallas import tpu as pltpu
from jax.sharding import PartitionSpec as P

HEAD_DIM = 128
CAP = 12
PAIR = 2 * CAP
EPS = 1e-06
BF = jnp.bfloat16
F32 = jnp.float32
SCALE = 1.0 / math.sqrt(HEAD_DIM)
NT = (((1,), (1,)), ((), ()))
TN = (((0,), (0,)), ((), ()))
MB = 1 << 20
NEAR_MIB = 57
GRADS_MIB = 62
FINISH_MIB = 62
FAR_MIB = 60


def nt(a, b):
    return lax.dot_general(a, b, NT, preferred_element_type=F32)


def tn(a, b):
    return lax.dot_general(a, b, TN, preferred_element_type=F32)


def nn(a, b):
    return jnp.dot(a, b, preferred_element_type=F32)


def params(mib=60):
    return pltpu.CompilerParams(vmem_limit_bytes=mib * MB)


def whole(shape):
    return pl.BlockSpec(shape, lambda *_: (0,) * len(shape))


def row_expert(quarter, per, count, shape):
    row = lax.broadcasted_iota(jnp.int32, shape, 0)
    return jnp.where(row < count, row * per + quarter, -1)


def slot_split(shape, axis, first):
    slot = (lax.broadcasted_iota(jnp.int32, shape, axis) + first).astype(F32)
    lane = jnp.floor((slot + 0.5) * (1.0 / PAIR))
    rank = slot - PAIR * lane
    half = jnp.where(rank > CAP - 0.5, 1.0, 0.0)
    return lane, half, rank - CAP * half


def route_kernel(rows, per, count, q_ref, ids_ref, rw_ref, hid_ref, up_ref, gain_ref,
                 send_ref, s0_ref, sw0_ref, sw1_ref, m_ref, r_ref, w_ref, n_ref):
    step = pl.program_id(0)
    tokens = ids_ref.shape[1]

    @pl.when(step == 0)
    def _():
        ids = ids_ref[...]
        weights = rw_ref[...].astype(F32)
        named = row_expert(q_ref[0], per, count, (128, tokens))
        member = jnp.zeros((128, tokens), F32)
        weight = jnp.zeros((128, tokens), F32)
        for k in range(ids.shape[0]):
            hit = ids[k : k + 1] == named
            member = member + jnp.where(hit, 1.0, 0.0)
            weight = weight + jnp.where(hit, weights[k : k + 1], 0.0)
        m_ref[...] = member.astype(BF)
        w_ref[...] = weight.astype(BF)
        row = lax.broadcasted_iota(jnp.int32, (tokens, tokens), 0)
        col = lax.broadcasted_iota(jnp.int32, (tokens, tokens), 1)
        before = jnp.where(row < col, 1.0, 0.0).astype(BF)
        r_ref[...] = nn(member.astype(BF), before).astype(BF)
        wide = hid_ref[...].astype(F32)
        inv = lax.rsqrt(jnp.mean(wide * wide, axis=1, keepdims=True) + EPS)
        n_ref[:tokens] = (wide * inv * gain_ref[...]).astype(BF)
        n_ref[tokens:] = up_ref[...]

    lane_of, half_of, rank_of = slot_split((rows, 128), 0, step * rows)
    lane = lax.broadcasted_iota(jnp.int32, (rows, 128), 1).astype(F32)
    spread = jnp.where(lane == lane_of, 1.0, 0.0).astype(BF)
    chosen = (nn(spread, m_ref[...]) > 0.5) & (nn(spread, r_ref[...]) == rank_of)
    weight = nn(spread, w_ref[...])
    first, second = chosen & (half_of < 0.5), chosen & (half_of > 0.5)
    s0 = jnp.where(first, 1.0, 0.0).astype(BF)
    s1 = jnp.where(second, 1.0, 0.0).astype(BF)
    send_ref[...] = nn(jnp.concatenate([s0, s1], axis=1), n_ref[...]).astype(BF)
    s0_ref[...] = s0
    sw0_ref[...] = jnp.where(first, weight, 0.0).astype(BF)
    sw1_ref[...] = jnp.where(second, weight, 0.0).astype(BF)


def route(quarter, per, count, ids, weights, hidden, upstream, gain):
    tokens, width = hidden.shape
    rows = 256
    slots = count * PAIR
    matrix = pl.BlockSpec((rows, tokens), lambda i, p: (i, 0))
    return pl.pallas_call(
        lambda *refs: route_kernel(rows, per, count, *refs),
        grid_spec=pltpu.PrefetchScalarGridSpec(
            num_scalar_prefetch=1,
            grid=(slots // rows,),
            in_specs=[
                whole(ids.shape),
                whole(ids.shape),
                whole((tokens, width)),
                whole((tokens, width)),
                whole((1, width)),
            ],
            out_specs=[pl.BlockSpec((rows, width), lambda i, p: (i, 0)), matrix, matrix, matrix],
            scratch_shapes=[
                pltpu.VMEM((128, tokens), BF),
                pltpu.VMEM((128, tokens), BF),
                pltpu.VMEM((128, tokens), BF),
                pltpu.VMEM((2 * tokens, width), BF),
            ],
        ),
        out_shape=[jax.ShapeDtypeStruct((slots, width), BF)]
        + [jax.ShapeDtypeStruct((slots, tokens), BF)] * 3,
        compiler_params=params(),
        name="route",
    )(quarter, ids, weights, hidden, upstream, gain)


def pack_kernel(count, q_ref, g_ref, u_ref, d_ref, *refs):
    out_refs, sems = refs[:count], refs[count]
    unit = g_ref.shape[2]
    blocks = d_ref.shape[2] // unit
    copies = []
    for n, out in enumerate(out_refs):
        which = q_ref[n]
        pairs = [(g_ref.at[which], out.at[0]), (u_ref.at[which], out.at[1])]
        for k in range(blocks):
            at = pl.ds(k * unit, unit)
            pairs.append((d_ref.at[which, :, at], out.at[2, at]))
        copies += pairs
    copies = [pltpu.make_async_copy(src, dst, sems.at[k]) for k, (src, dst) in enumerate(copies)]
    for copy in copies:
        copy.start()
    for copy in copies:
        copy.wait()


def pack(which, w_gate, w_up, w_down):
    width, unit = w_gate.shape[1:]
    count = which.shape[0]
    hbm = pl.BlockSpec(memory_space=pltpu.HBM)
    return pl.pallas_call(
        lambda *refs: pack_kernel(count, *refs),
        in_specs=[pl.BlockSpec(memory_space=pltpu.SMEM), hbm, hbm, hbm],
        out_specs=[hbm] * count,
        out_shape=[jax.ShapeDtypeStruct((3, width, unit), BF)] * count,
        scratch_shapes=[pltpu.SemaphoreType.DMA((count * (2 + width // unit),))],
        compiler_params=params(),
        name="pack",
    )(which, w_gate, w_up, w_down)


def unpack(ref):
    unit = ref.shape[2]
    down = [ref[2, n * unit : (n + 1) * unit] for n in range(ref.shape[1] // unit)]
    return ref[0], ref[1], jnp.concatenate(down, axis=1)


def expert_rows(xy, w_in, w_down):
    rows, width = xy.shape
    half_width = width // 2
    ahead = nn(xy, w_in)
    gate, up = ahead[:, : w_in.shape[1] // 2], ahead[:, w_in.shape[1] // 2 :]
    proj = pltpu.roll(nt(xy, w_down), rows - CAP, 0)
    sig = 1.0 / (1.0 + jnp.exp(-gate))
    silu = gate * sig
    act = (silu * up).astype(BF).astype(F32)
    d_gate = (proj * up * (sig * (1.0 + gate * (1.0 - sig)))).astype(BF)
    d_up = (proj * silu).astype(BF)
    d_route = jnp.sum(act * proj, axis=1, keepdims=True)
    d_rows = nt(jnp.concatenate([d_gate, d_up], axis=1), w_in)
    _, half, _ = slot_split((rows, 1), 0, 0)
    out = jnp.where(half > 0.5, pltpu.roll(d_rows[:, half_width:], CAP, 0), d_rows[:, :half_width])
    return out, jnp.broadcast_to(d_route, (rows, 128))


def near_kernel(rows, q_ref, xy_ref, go_ref, uo_ref, do_ref, a_ref, b_ref, out_ref):
    width = xy_ref.shape[1]
    one, two = unpack(a_ref), unpack(b_ref)
    w_in = jnp.concatenate([go_ref[0], one[0], two[0], uo_ref[0], one[1], two[1]], axis=1)
    w_down = jnp.concatenate([do_ref[0], one[2], two[2]], axis=0)
    out, d_route = expert_rows(xy_ref[...], w_in, w_down)
    out_ref[:, : width // 2] = out
    out_ref[:, width // 2 :] = d_route


def expert_near(quarter, xy, w_gate, w_up, w_down, got_a, got_b):
    slots, width = xy.shape
    unit = w_gate.shape[2]
    rows = 384
    own = pl.BlockSpec((1, width, unit), lambda i, p: (p[0], 0, 0))
    narrow = width // 2 + 128
    return pl.pallas_call(
        lambda *refs: near_kernel(rows, *refs),
        grid_spec=pltpu.PrefetchScalarGridSpec(
            num_scalar_prefetch=1,
            grid=(slots // rows,),
            in_specs=[
                pl.BlockSpec((rows, width), lambda i, p: (i, 0)),
                own,
                own,
                pl.BlockSpec((1, unit, width), lambda i, p: (p[0], 0, 0)),
                whole(got_a.shape),
                whole(got_b.shape),
            ],
            out_specs=pl.BlockSpec((rows, narrow), lambda i, p: (i, 0)),
        ),
        out_shape=jax.ShapeDtypeStruct((slots, narrow), F32),
        compiler_params=params(NEAR_MIB),
        name="expert_near",
    )(quarter, xy, w_gate, w_up, w_down, got_a, got_b)


def far_kernel(xy_ref, far_ref, near_ref, out_ref):
    width = xy_ref.shape[1]
    w_gate, w_up, w_down = unpack(far_ref)
    out, d_route = expert_rows(xy_ref[...], jnp.concatenate([w_gate, w_up], axis=1), w_down)
    out_ref[:, : width // 2] = (near_ref[:, : width // 2] + out).astype(BF)
    out_ref[:, width // 2 :] = (near_ref[:, width // 2 :] + d_route).astype(BF)


def expert_far(xy, got, near):
    slots, width = xy.shape
    narrow = near.shape[1]
    rows = 192
    block = pl.BlockSpec((rows, narrow), lambda i: (i, 0))
    return pl.pallas_call(
        far_kernel,
        grid=(slots // rows,),
        in_specs=[pl.BlockSpec((rows, width), lambda i: (i, 0)), whole(got.shape), block],
        out_specs=block,
        out_shape=jax.ShapeDtypeStruct((slots, narrow), BF),
        compiler_params=params(FAR_MIB),
        name="expert_far",
    )(xy, got, near)


def gather_kernel(per, count, q_ref, back_ref, s0_ref, sw0_ref, sw1_ref, ids_ref, hid_ref, gain_ref, out_ref):
    tokens, width = hid_ref.shape
    half_width = width // 2
    wide = hid_ref[...].astype(F32)
    inv = lax.rsqrt(jnp.mean(wide * wide, axis=1, keepdims=True) + EPS)
    rows = back_ref[:, :half_width]
    d_normed = jnp.concatenate([tn(sw0_ref[...], rows), tn(sw1_ref[...], rows)], axis=1)
    g = d_normed * gain_ref[...]
    inner = jnp.mean(g * wide, axis=1, keepdims=True)
    out_ref[:, :width] = (inv * g - wide * (inv * inv * inv * inner)).astype(BF)
    slots = back_ref.shape[0]
    lane_of, _, _ = slot_split((slots, 128), 0, 0)
    lane = lax.broadcasted_iota(jnp.int32, (slots, 128), 1).astype(F32)
    placed = jnp.where(lane == lane_of, back_ref[:, half_width:].astype(F32), 0.0).astype(BF)
    route = tn(placed, s0_ref[...])
    named = row_expert(q_ref[0], per, count, (128, tokens))
    ids = ids_ref[...]
    row = lax.broadcasted_iota(jnp.int32, (128, tokens), 0)
    out = jnp.zeros((128, tokens), F32)
    for k in range(ids.shape[0]):
        value = jnp.sum(jnp.where(ids[k : k + 1] == named, route, 0.0), axis=0, keepdims=True)
        out = jnp.where(row == k, value, out)
    out_ref[:, width:] = out.T.astype(BF)


def on_chip(kernel, name, out_shape, scalars, arrays, scratch=(), mib=60):
    vmem = pl.BlockSpec(memory_space=pltpu.VMEM)
    many = isinstance(out_shape, list)
    return pl.pallas_call(
        kernel,
        in_specs=[pl.BlockSpec(memory_space=pltpu.SMEM)] * len(scalars) + [vmem] * len(arrays),
        out_specs=[vmem] * len(out_shape) if many else vmem,
        out_shape=out_shape,
        scratch_shapes=list(scratch),
        compiler_params=params(mib),
        name=name,
    )(*scalars, *arrays)


def sum_first(ref):
    total = ref[0].astype(F32)
    for n in range(1, ref.shape[0]):
        total = total + ref[n].astype(F32)
    return total


def finish_kernel(z_ref, in_ref, up_ref, out_ref):
    width = up_ref.shape[1]
    total = sum_first(in_ref)
    mine = up_ref[...].astype(F32)
    done = jnp.concatenate([total[:, :width] + mine, total[:, width:]], axis=1).astype(BF)
    for n in range(in_ref.shape[0]):
        out_ref[n] = done


def finish(z, arrived, upstream):
    parts, share, wide = arrived.shape
    return pl.pallas_call(
        finish_kernel,
        grid_spec=pltpu.PrefetchScalarGridSpec(
            num_scalar_prefetch=1,
            grid=(1,),
            in_specs=[
                whole((parts, share, wide)),
                pl.BlockSpec((share, upstream.shape[1]), lambda i, z: (z[0], 0)),
            ],
            out_specs=whole((parts, share, wide)),
        ),
        out_shape=jax.ShapeDtypeStruct((parts, share, wide), BF),
        compiler_params=params(FINISH_MIB),
        name="finish_hidden",
    )(z, arrived, upstream)


def spread_kernel(in_ref, out_ref):
    total = sum_first(in_ref).astype(BF)
    for n in range(out_ref.shape[0]):
        out_ref[n] = total


def last_kernel(in_ref, dk_ref, dv_ref):
    half = in_ref.shape[0] // 2
    for head in range(2):
        total = in_ref[head * half].astype(F32)
        for n in range(1, half):
            total = total + in_ref[head * half + n].astype(F32)
        at = slice(head * HEAD_DIM, (head + 1) * HEAD_DIM)
        dk_ref[:, at] = total[:, :HEAD_DIM]
        dv_ref[:, at] = total[:, HEAD_DIM:]


def heads_to_rows(x):
    return jnp.concatenate([x[:, :HEAD_DIM], x[:, HEAD_DIM:]], axis=0)


def probs_kernel(chunk, q_ref, o_ref, kv_ref, p_ref, stat_ref, s_ref):
    query = jnp.concatenate([heads_to_rows(q_ref[...]), heads_to_rows(o_ref[...])], axis=0)
    count = query.shape[0]
    steps = [slice(n, n + chunk) for n in range(0, kv_ref.shape[0], chunk)]
    top = None
    for span in steps:
        s = nt(kv_ref[span, :HEAD_DIM], query) * SCALE
        s_ref[span] = s
        most = jnp.max(s, axis=0, keepdims=True)
        top = most if top is None else jnp.maximum(top, most)
    total = jnp.zeros_like(top)
    out = jnp.zeros((HEAD_DIM, count), F32)
    for span in steps:
        e = jnp.exp(s_ref[span] - top)
        total = total + jnp.sum(e, axis=0, keepdims=True)
        p = e.astype(BF)
        p_ref[span] = p
        out = out + tn(kv_ref[span, HEAD_DIM:], p)
    stat_ref[:HEAD_DIM] = out
    row = lax.broadcasted_iota(jnp.int32, (8, count), 0)
    stat_ref[HEAD_DIM:] = jnp.where(row == 0, top, total)


def probs(queries, other, kv):
    count = kv.shape[0]
    rows = queries.shape[0] * 4
    return on_chip(
        lambda *refs: probs_kernel(512, *refs), "attention_probs",
        [jax.ShapeDtypeStruct((count, rows), BF), jax.ShapeDtypeStruct((HEAD_DIM + 8, rows), F32)],
        [], [queries, other, kv], [pltpu.VMEM((count, rows), F32)])


def grads_kernel(chunk, dh_ref, do_ref, w_ref, q_ref, o_ref, p_ref, stat_ref, far_ref, kv_ref, dq_ref, dqo_ref, dkv_ref):
    width = w_ref.shape[1]
    tokens = dh_ref.shape[0]
    d_hidden = jnp.concatenate([dh_ref[:, :width], do_ref[:, :width]], axis=0)
    d_out_w = nt(w_ref[...], d_hidden).astype(BF)
    parts = [d_out_w[h * HEAD_DIM : (h + 1) * HEAD_DIM, c * tokens : (c + 1) * tokens] for c in range(2) for h in range(2)]
    d_out_t = jnp.concatenate(parts, axis=1)
    d_out = jnp.concatenate([p.T for p in parts], axis=0)
    query = jnp.concatenate([heads_to_rows(q_ref[...]), heads_to_rows(o_ref[...])], axis=0)
    half = query.shape[0] // 2
    here = stat_ref[...]
    there = jnp.concatenate([far_ref[:, half:], far_ref[:, :half]], axis=1)
    top_here, top_there = here[HEAD_DIM : HEAD_DIM + 1], there[HEAD_DIM : HEAD_DIM + 1]
    top = jnp.maximum(top_here, top_there)
    in_here, in_there = jnp.exp(top_here - top), jnp.exp(top_there - top)
    total = here[HEAD_DIM + 1 : HEAD_DIM + 2] * in_here + there[HEAD_DIM + 1 : HEAD_DIM + 2] * in_there
    in_here, in_there = in_here / total, in_there / total
    out = here[:HEAD_DIM] * in_here + there[:HEAD_DIM] * in_there
    delta = jnp.sum(d_out_t.astype(F32) * out, axis=0, keepdims=True)
    d_query = jnp.zeros((HEAD_DIM, 2 * half), F32)
    for n in range(0, kv_ref.shape[0], chunk):
        span = slice(n, n + chunk)
        p = p_ref[span].astype(F32) * in_here
        d_probs = nn(kv_ref[span, HEAD_DIM:], d_out_t)
        ds = (p * (d_probs - delta)).astype(BF)
        dkv_ref[span, :HEAD_DIM] = (nn(ds, query) * SCALE).astype(BF)
        dkv_ref[span, HEAD_DIM:] = nn(p.astype(BF), d_out).astype(BF)
        d_query = d_query + tn(kv_ref[span, :HEAD_DIM], ds)
    d_query = (d_query * SCALE).T
    for ref, at in ((dq_ref, 0), (dqo_ref, half)):
        ref[:, :HEAD_DIM] = d_query[at : at + tokens]
        ref[:, HEAD_DIM:] = d_query[at + tokens : at + 2 * tokens]


def body(hidden, upstream, norm_gain, route_ids, route_weights, w_gate, w_up, w_down, w_out, queries, keys, values):
    ctx_count = lax.axis_size("context")
    exp_count = lax.axis_size("expert")
    tokens, width = hidden.shape
    chips = ctx_count // 2
    per = w_gate.shape[0]
    slots = ctx_count * PAIR
    z = lax.axis_index("expert")
    quarter = z % per
    q_arr = quarter.astype(jnp.int32).reshape(1)
    z_arr = z.astype(jnp.int32).reshape(1)
    gain = norm_gain.reshape(1, width)
    swap_core = [(i, i ^ 1) for i in range(ctx_count)]
    same_core = [[2 * i + k for i in range(chips)] for k in range(2)]

    def far(core):
        return -2 if core == 0 else 2

    def moves(step):
        return [
            (i * ctx_count + c, (i + step(c % 2)) % exp_count * ctx_count + c)
            for c in range(ctx_count)
            for i in range(exp_count)
        ]

    def trade(w, step):
        return lax.ppermute(w, ("expert", "context"), moves(step))

    leave = [((z + n) % per).astype(jnp.int32) for n in (1, per - 1, 2)]
    packs = pack(jnp.stack(leave[:2]), w_gate, w_up, w_down) + pack(jnp.stack(leave[2:]), w_gate, w_up, w_down)
    near_a, near_b = trade(packs[0], lambda core: 1), trade(packs[1], lambda core: -1)
    distant, near_a, near_b = lax.optimization_barrier((packs[2], near_a, near_b))
    got_far = trade(distant, far)

    ids = route_ids.T
    kv_head = z // (exp_count // 2)
    own_kv = jnp.concatenate(
        [lax.dynamic_slice_in_dim(a, kv_head * HEAD_DIM, HEAD_DIM, 1) for a in (keys, values)], axis=1)
    kv = lax.all_gather(own_kv, "context", axis=0, tiled=True, axis_index_groups=same_core)

    send, s0, sw0, sw1 = route(q_arr, per, ctx_count, ids, route_weights.T, hidden, upstream, gain)
    xy = lax.all_to_all(send.reshape(ctx_count, PAIR, width), "context", 0, 0, tiled=True)
    xy = xy.reshape(slots, width)
    narrow = width // 2 + 128
    near = expert_near(q_arr, xy, w_gate, w_up, w_down, near_a, near_b)
    rows = expert_far(xy, got_far, near)
    rows, kv = lax.optimization_barrier((rows, kv))
    rows = lax.all_to_all(rows.reshape(ctx_count, PAIR, narrow), "context", 0, 0, tiled=True)
    wide = width + 128
    q = on_chip(
        lambda *refs: gather_kernel(per, ctx_count, *refs), "gather_rows",
        jax.ShapeDtypeStruct((tokens, wide), BF),
        [q_arr], [rows.reshape(slots, narrow), s0, sw0, sw1, ids, hidden, gain])

    share = tokens // exp_count
    parts = (exp_count, share, wide)
    arrived = lax.all_to_all(q.reshape(parts), "expert", 0, 0, tiled=True)
    queries, q = lax.optimization_barrier((queries, q))
    other = lax.ppermute(queries, "context", swap_core)
    soft, stats = probs(queries, other, kv)
    far_stats = lax.ppermute(stats, "context", swap_core)
    arrived, far_stats = lax.optimization_barrier((arrived, far_stats))
    done = finish(z_arr, arrived, upstream)
    done = lax.all_to_all(done, "expert", 0, 0, tiled=True).reshape(tokens, wide)
    d_hidden = done[:, :width]
    d_route = done[:, width : width + route_ids.shape[1]].astype(F32)

    done_other = lax.ppermute(done, "context", swap_core)
    d_queries, d_other, part = on_chip(
        lambda *refs: grads_kernel(512, *refs), "attention_grads",
        [
            jax.ShapeDtypeStruct(queries.shape, F32),
            jax.ShapeDtypeStruct(queries.shape, F32),
            jax.ShapeDtypeStruct(kv.shape, BF),
        ],
        [], [done, done_other, w_out, queries, other, soft, stats, far_stats, kv], mib=GRADS_MIB)
    d_queries = d_queries + lax.ppermute(d_other, "context", swap_core)
    part = lax.all_to_all(
        part.reshape(chips, tokens, 2 * HEAD_DIM), "context", 0, 0, tiled=True, axis_index_groups=same_core)
    block = (exp_count, tokens, 2 * HEAD_DIM)
    part = on_chip(spread_kernel, "sum_chips", jax.ShapeDtypeStruct(block, BF), [], [part], mib=32)
    part = lax.all_to_all(part, "expert", 0, 0, tiled=True)
    d_keys, d_values = on_chip(
        last_kernel, "sum_heads", [jax.ShapeDtypeStruct((tokens, 2 * HEAD_DIM), F32)] * 2, [], [part], mib=32)
    return (d_hidden, d_route, d_queries, d_keys, d_values)


def solution(mesh):
    placed = (
        P("context", None),
        P("context", None),
        P(),
        P("context", None),
        P("context", None),
        P("context", None, "expert"),
        P("context", None, "expert"),
        P("context", "expert", None),
        P("expert", None),
        P("context", "expert"),
        P("context", None),
        P("context", None),
    )
    return jax.shard_map(
        body,
        mesh=mesh,
        in_specs=placed,
        out_specs=(
            P("context", None),
            P("context", None),
            P("context", "expert"),
            P("context", None),
            P("context", None),
        ),
        check_vma=False,
    )
```

time: 272 us -> 364 us (1.34)
  Pallas kernels: 42.6 us -> 190 us
  waiting for transfers between devices: 111 us -> 51 us
  blocking collectives: 56.6 us -> 75.1 us
  local copies, waits for them, and re-layouts: 14.8 us -> 5.49 us
  starting transfers between devices: 30.6 us -> 25.6 us
    pallas_call x2 -> x5, Pallas kernels: 18.2 us -> 168 us  [the longest x2 146 us: pack(): pl.pallas_call(lambda *refs: pack_kernel(count, *refs), in_specs=[pl.Bloc...]
    ppermute x8 -> x7, waiting for transfers between devices: 64.3 us -> 27 us  [the longest x3 21.5 us: trade(): return lax.ppermute(w, ('expert', 'context'), moves(step))]
    all_to_all x0 -> x1, blocking collectives: none -> 22.1 us  [body(): lax.all_to_all(done, 'expert', 0, 0, tiled=True).reshape(tokens, wide)]
    all_to_all x1 -> x0, waiting for transfers between devices: 12.5 us -> none  [body(): lax.all_to_all(done, 'expert', 0, 0, tiled=True).reshape(tokens, wide)]
    all_to_all x1, waiting for transfers between devices: 18.5 us -> 10.2 us  [body(): arrived = lax.all_to_all(q.reshape(parts), 'expert', 0, 0, tiled=True)]
    unnamed x35 -> x25, local copies, waits for them, and re-layouts: 11.7 us -> 4.63 us
    ppermute x8 -> x7, starting transfers between devices: 12.1 us -> 8.92 us  [the longest x3 8.48 us: trade(): return lax.ppermute(w, ('expert', 'context'), moves(step))]
    pallas_call x6 -> x5, Pallas kernels: 19.9 us -> 16.9 us  [on_chip(): pl.pallas_call(kernel, in_specs=[pl.BlockSpec(memory_space=pltpu.SMEM)] *...]
  transfers between devices with their start and end apart: 13 -> 11, of which waited for: 7 -> 7; matrix products, arithmetic and copies ran while one was open for 2% -> 1% of each run, Pallas kernels for 7% -> 21%
where the time goes in v2:
time: 364 us; the launch traced here: 363 us
  Pallas kernels  190 us (52%)
  blocking collectives  75.1 us (21%)
  waiting for transfers between devices  51 us (14%)
  starting transfers between devices  25.6 us (7%)
  between operations  14.2 us (4%)
  local copies, waits for them, and re-layouts  5.49 us (2%)
    pallas_call x2, Pallas kernels, pack(): pl.pallas_call(lambda *refs: pack_kernel(count, *refs), in_specs=[pl.Bloc...  146 us
    all_to_all x1, blocking collectives, body(): lax.all_to_all(rows.reshape(ctx_count, PAIR, narrow), 'context', 0, 0, ti...  32 us
    all_to_all x1, blocking collectives, body(): lax.all_to_all(done, 'expert', 0, 0, tiled=True).reshape(tokens, wide)  22.1 us
    ppermute x3, waiting for transfers between devices, trade(): return lax.ppermute(w, ('expert', 'context'), moves(step))  21.5 us
    all_to_all x1, blocking collectives, body(): lax.all_to_all(part.reshape(chips, tokens, 2 * HEAD_DIM), 'context', 0, 0...  21 us
    pallas_call x5, Pallas kernels, on_chip(): pl.pallas_call(kernel, in_specs=[pl.BlockSpec(memory_space=pltpu.SMEM)] *...  16.9 us
    all_to_all x1, waiting for transfers between devices, body(): part = lax.all_to_all(part, 'expert', 0, 0, tiled=True)  13.8 us
    pallas_call x1, Pallas kernels, expert_near(): pl.pallas_call(lambda *refs: near_kernel(rows, *refs), grid_spec=pltpu.Pr...  12.1 us
  transfers between devices with their start and end apart: 11, of which 7 were waited for; matrix products, arithmetic and copies ran while one was open for 1% of the time, Pallas kernels for 21%

profile of v2, /device:TPU:2, one launch (start us, length us, event | category | flops | bytes accessed | tf_op | source)
XLA Modules:
  0.0 362.8 jit_solution(9494375207438382062)
XLA Ops:
  7.2 0.6 pad_add_fusion.refs_0_
  7.8 97.4 %pack.3 = (bf16[3,2048,128]{2,1,0:T(8,128)(2,1)}, bf16[3,2048,128]{2,1,0:T(8,128)(2,1)}) custom-call(s32[2]{0:T(128)} %pad_add_fusion.refs_0_, bf16[4,2048,128]{2,1,0:T(8,128)(2,1)} %refs_2_.6, bf16[4,2048,128]{2,1,0:T(8,128)(2,1)} %refs_3_.7, bf16[4,128,2048]{2,1,0:T(8,128)(2,1)} %refs_4_.3), custom_call_target="tpu_custom_call" | custom-call | tf_op jit(solution)/shard_map/pack/pallas_call | solution.py:155
  105.2 2.0 collective-permute-start
  107.2 4.0 %collective-permute-start.1 = (bf16[3,2048,128]{2,1,0:T(8,128)(2,1)}, bf16[3,2048,128]{2,1,0:T(8,128)(2,1)}, u32[]{:S(2)}, u32[]{:S(2)}) collective-permute-start(bf16[3,2048,128]{2,1,0:T(8,128)(2,1)} %get-tuple-element.28), channel_id=1, source_target_pairs={{0,224},{32,0},{64,32},{96,64},{128,96},{160,128},{192,160},{224,1... | collective-permute-start | bytes 4718600 | tf_op jit(solution)/shard_map/ppermute | solution.py:438
  111.2 4.7 %route.1 = (bf16[768,2048]{1,0:T(8,128)(2,1)}, bf16[768,128]{1,0:T(8,128)(2,1)}, bf16[768,128]{1,0:T(8,128)(2,1)}, bf16[768,128]{1,0:T(8,128)(2,1)}) custom-call(s32[1]{0:T(128)} %bitcast.1.refs_0_, s32[8,128]{1,0:T(8,128)} %bitcast.28, bf16[8,128]{1,0:T(8,128)(2,1)} %bitcast.30, bf16[128,2048]{1,0:T(8,128)(2,1)} %refs_6_.1, bf16[128,2048]{1,0:T(8,128)(2,1)} %up_ref.1, ...), custom_call_target="tpu_custom_call" | custom-call | tf_op jit(solution)/shard_map/route/pallas_call | solution.py:105
  115.9 0.0 copy-start.10
  115.9 7.8 %all-to-all-start = ((bf16[32,24,2048]{2,1,0:T(8,128)(2,1)}), bf16[32,24,2048]{2,1,0:T(8,128)(2,1)S(1)}, u32[]{:S(2)}, u32[]{:S(2)}) async-start(bf16[32,24,2048]{2,1,0:T(8,128)(2,1)} %bitcast.23), calls=%async_computation | async-start | bytes 6291456 | tf_op jit(solution)/shard_map/all_to_all | solution.py:453
  123.6 0.0 all-gather.2.cloned.1.call-start
  123.8 0.6 pad_maximum_fusion
  124.4 0.0 all-gather.2.cloned.1.call-update
  124.4 48.9 %pack.2 = bf16[3,2048,128]{2,1,0:T(8,128)(2,1)} custom-call(s32[1]{0:T(128)} %bitcast.7.refs_0_, bf16[4,2048,128]{2,1,0:T(8,128)(2,1)} %refs_2_.6, bf16[4,2048,128]{2,1,0:T(8,128)(2,1)} %refs_3_.7, bf16[4,128,2048]{2,1,0:T(8,128)(2,1)} %refs_4_.3), custom_call_target="tpu_custom_call" | custom-call | tf_op jit(solution)/shard_map/pack/pallas_call | solution.py:155
  173.3 0.0 collective-permute-done.refs_5_
  173.4 0.0 collective-permute-done.1.refs_6_
  173.4 2.5 collective-permute-start.2
  175.8 0.0 all-to-all-done
  175.8 1.7 copy-done
  177.5 12.1 %expert_near.1.near_ref = f32[768,1152]{1,0:T(8,128)} custom-call(s32[1]{0:T(128)} %bitcast.1.refs_0_, bf16[768,2048]{1,0:T(8,128)(2,1)} %bitcast.15, bf16[4,2048,128]{2,1,0:T(8,128)(2,1)} %refs_2_.6, bf16[4,2048,128]{2,1,0:T(8,128)(2,1)} %refs_3_.7, bf16[4,128,2048]{2,1,0:T(8,128)(2,1)} %refs_4_.3, bf16[3,2048,128]{2,1,0:T(8,128)(2,1)} %collective-permute-done.refs_5_, ...), custom_call_target="tpu_custom_call" | custom-call | tf_op jit(solution)/shard_map/expert_near/pallas_call | solution.py:206
  189.6 21.5 %collective-permute-done.2.far_ref = bf16[3,2048,128]{2,1,0:T(8,128)(2,1)} collective-permute-done((bf16[3,2048,128]{2,1,0:T(8,128)(2,1)}, bf16[3,2048,128]{2,1,0:T(8,128)(2,1)}, u32[]{:S(2)}, u32[]{:S(2)}) %collective-permute-start.2) | collective-permute-done | bytes 1572896 | tf_op jit(solution)/shard_map/ppermute | solution.py:438
  211.1 7.7 %expert_far.1 = bf16[768,1152]{1,0:T(8,128)(2,1)} custom-call(bf16[768,2048]{1,0:T(8,128)(2,1)} %bitcast.16, bf16[3,2048,128]{2,1,0:T(8,128)(2,1)} %collective-permute-done.2.far_ref, f32[768,1152]{1,0:T(8,128)} %expert_near.1.near_ref), custom_call_target="tpu_custom_call" | custom-call | tf_op jit(solution)/shard_map/expert_far/pallas_call | solution.py:240
  218.8 32.0 %all_to_all.30 = bf16[32,24,1152]{2,1,0:T(8,128)(2,1)} all-to-all(bf16[32,24,1152]{2,1,0:T(8,128)(2,1)} %bitcast.17), channel_id=1, replica_groups=mesh['expert'=8,'context'=32] {'context'}, dimensions={0} | all-to-all | bytes 3538944 | tf_op jit(solution)/shard_map/all_to_all | solution.py:459
  250.8 3.6 %gather_rows.1 = bf16[128,2176]{1,0:T(8,128)(2,1)} custom-call(s32[1]{0:T(128)} %bitcast.1.refs_0_, bf16[768,1152]{1,0:T(8,128)(2,1)} %bitcast.18, bf16[768,128]{1,0:T(8,128)(2,1)} %get-tuple-element.33.refs_2_, bf16[768,128]{1,0:T(8,128)(2,1)} %get-tuple-element.34.refs_3_, bf16[768,128]{1,0:T(8,128)(2,1)} %get-tuple-element.35.refs_4_, s32[8,128]{1,0:T(8,128)} %bitcast.29, ...), custom_call_target="tpu_custom_call" | custom-call | tf_op jit(solution)/shard_map/gather_rows/pallas_call | solution.py:279
  254.4 5.4 %all-to-all-start.2 = ((bf16[8,16,2176]{2,1,0:T(8,128)(2,1)}), bf16[8,16,2176]{2,1,0:T(8,128)(2,1)S(1)}, u32[]{:S(2)}, u32[]{:S(2)}) async-start(bf16[8,16,2176]{2,1,0:T(8,128)(2,1)} %bitcast.24), calls=%async_computation.2 | async-start | bytes 1114112 | tf_op jit(solution)/shard_map/all_to_all | solution.py:468
  259.8 0.3 collective-permute-start.3
  260.1 1.2 collective-permute-done.3.refs_1_.refs_4_
  261.3 0.6 copy-done.7
  261.9 4.6 %attention_probs.1 = (bf16[2048,512]{1,0:T(8,128)(2,1)}, f32[136,512]{1,0:T(8,128)}) custom-call(bf16[128,256]{1,0:T(8,128)(2,1)} %refs_3_.8, bf16[128,256]{1,0:T(8,128)(2,1)} %copy-done.7, bf16[2048,256]{1,0:T(8,128)(2,1)} %all-gather.2.cloned.1.call-done.refs_2_.refs_8_), custom_call_target="tpu_custom_call" | custom-call | tf_op jit(solution)/shard_map/attention_probs/pallas_call | solution.py:279
  266.5 0.2 collective-permute-start.4
  266.7 1.6 collective-permute-done.4.refs_7_
  268.3 10.2 %all-to-all-done.2.in_ref = bf16[8,16,2176]{2,1,0:T(8,128)(2,1)S(1)} async-done(((bf16[8,16,2176]{2,1,0:T(8,128)(2,1)}), bf16[8,16,2176]{2,1,0:T(8,128)(2,1)S(1)}, u32[]{:S(2)}, u32[]{:S(2)}) %all-to-all-start.2) | async-done | bytes 557088 | tf_op jit(solution)/shard_map/all_to_all | solution.py:468
  278.5 0.8 copy-done.3
  279.3 1.9 finish_hidden.1
  281.2 22.1 %all_to_all.31 = bf16[8,16,2176]{2,1,0:T(8,128)(2,1)S(1)} all-to-all(bf16[8,16,2176]{2,1,0:T(8,128)(2,1)} %finish_hidden.1), channel_id=1, replica_groups=mesh['expert'=8,'context'=32] {'expert'}, dimensions={0} | all-to-all | bytes 1114112 | tf_op jit(solution)/shard_map/all_to_all | solution.py:475
  303.3 0.0 collective-permute-start.5
  303.3 2.0 collective-permute-done.5.refs_1_
  305.3 0.0 copy-done.5
  305.3 0.8 copy-done.4
  306.1 7.0 %attention_grads.1 = (f32[128,256]{1,0:T(8,128)}, f32[128,256]{1,0:T(8,128)}, bf16[2048,256]{1,0:T(8,128)(2,1)}) custom-call(bf16[128,2176]{1,0:T(8,128)(2,1)} %bitcast.20, bf16[128,2176]{1,0:T(8,128)(2,1)} %copy-done.4, bf16[256,2048]{1,0:T(8,128)(2,1)} %refs_2_.7, bf16[128,256]{1,0:T(8,128)(2,1)} %refs_3_.8, bf16[128,256]{1,0:T(8,128)(2,1)} %copy-done.7, ...), custom_call_target="tpu_custom_call" | custom-call | tf_op jit(solution)/shard_map/attention_grads/pallas_call | solution.py:279
  313.1 21.0 %all_to_all.32.in_ref = bf16[16,128,256]{2,1,0:T(8,128)(2,1)S(1)} all-to-all(bf16[16,128,256]{2,1,0:T(8,128)(2,1)} %bitcast.25), channel_id=1, replica_groups={{0,2,4,6,8,10,12,14,16,18,20,22,24,26,28,30},{1,3,5,7,9,11,13,15,17,19,..., dimensions={0} | all-to-all | bytes 2097152 | tf_op jit(solution)/shard_map/all_to_all | solution.py:489
  334.1 0.9 sum_chips.1
  335.0 3.5 all-to-all-start.5
  338.5 0.0 copy-done.2
  338.5 0.8 slice.8
  339.4 0.0 collective-permute-start.6
  339.4 0.7 copy.17
  340.1 0.7 collective-permute-done.6
  340.7 0.7 add.38
  341.4 13.8 %all-to-all-done.5.in_ref = bf16[8,128,256]{2,1,0:T(8,128)(2,1)S(1)} async-done(((bf16[8,128,256]{2,1,0:T(8,128)(2,1)}), bf16[8,128,256]{2,1,0:T(8,128)(2,1)S(1)}, u32[]{:S(2)}, u32[]{:S(2)}) %all-to-all-start.5) | async-done | bytes 524320 | tf_op jit(solution)/shard_map/all_to_all | solution.py:493
  355.2 0.7 sum_heads.1
  (20 shorter events, 0.1 us)
Async XLA Ops:
  105.2 68.2 %collective-permute-start = (bf16[3,2048,128]{2,1,0:T(8,128)(2,1)}, bf16[3,2048,128]{2,1,0:T(8,128)(2,1)}, u32[]{:S(2)}, u32[]{:S(2)}) collective-permute-start(bf16[3,2048,128]{2,1,0:T(8,128)(2,1)} %get-tuple-element.27), channel_id=1, source_target_pairs={{0,32},{32,64},{64,96},{96,128},{128,160},{160,192},{192,224},{224... | collective-permute-start | bytes 4718600 | tf_op jit(solution)/shard_map/ppermute | solution.py:438
  107.2 66.2 %collective-permute-start.1 = (bf16[3,2048,128]{2,1,0:T(8,128)(2,1)}, bf16[3,2048,128]{2,1,0:T(8,128)(2,1)}, u32[]{:S(2)}, u32[]{:S(2)}) collective-permute-start(bf16[3,2048,128]{2,1,0:T(8,128)(2,1)} %get-tuple-element.28), channel_id=1, source_target_pairs={{0,224},{32,0},{64,32},{96,64},{128,96},{160,128},{192,160},{224,1... | collective-permute-start | bytes 4718600 | tf_op jit(solution)/shard_map/ppermute | solution.py:438
  115.9 7.9 %copy-start.9 = (bf16[128,256]{1,0:T(8,128)(2,1)S(1)}, bf16[128,256]{1,0:T(8,128)(2,1)}, u32[]{:S(2)}) copy-start(bf16[128,256]{1,0:T(8,128)(2,1)} %param.23) | copy-start | bytes 196612
  115.9 7.9 %copy-start.10 = (bf16[128,256]{1,0:T(8,128)(2,1)S(1)}, bf16[128,256]{1,0:T(8,128)(2,1)}, u32[]{:S(2)}) copy-start(bf16[128,256]{1,0:T(8,128)(2,1)} %param.22) | copy-start | bytes 196612
  115.9 60.0 %all-to-all-start = ((bf16[32,24,2048]{2,1,0:T(8,128)(2,1)}), bf16[32,24,2048]{2,1,0:T(8,128)(2,1)S(1)}, u32[]{:S(2)}, u32[]{:S(2)}) async-start(bf16[32,24,2048]{2,1,0:T(8,128)(2,1)} %bitcast.23), calls=%async_computation | async-start | bytes 6291456 | tf_op jit(solution)/shard_map/all_to_all | solution.py:453
  123.6 95.1 %all-gather.2.cloned.1.call-start = ((), (), s32[]{:S(2)}) async-start(), calls=%async_computation.6 | async-start | bytes 1114112 | tf_op jit(solution)/shard_map/all_gather | solution.py:450
  173.4 37.7 %collective-permute-start.2 = (bf16[3,2048,128]{2,1,0:T(8,128)(2,1)}, bf16[3,2048,128]{2,1,0:T(8,128)(2,1)}, u32[]{:S(2)}, u32[]{:S(2)}) collective-permute-start(bf16[3,2048,128]{2,1,0:T(8,128)(2,1)} %pack.2), channel_id=1, source_target_pairs={{0,192},{32,224},{64,0},{96,32},{128,64},{160,96},{192,128},{224,1... | collective-permute-start | bytes 4718600 | tf_op jit(solution)/shard_map/ppermute | solution.py:438
  175.8 1.7 copy-start
  250.7 9.0 %copy-start.6 = (bf16[128,256]{1,0:T(8,128)(2,1)S(1)}, bf16[128,256]{1,0:T(8,128)(2,1)}, u32[]{:S(2)}) copy-start(bf16[128,256]{1,0:T(8,128)(2,1)} %refs_3_.8) | copy-start | bytes 196612
  254.4 24.1 %all-to-all-start.2 = ((bf16[8,16,2176]{2,1,0:T(8,128)(2,1)}), bf16[8,16,2176]{2,1,0:T(8,128)(2,1)S(1)}, u32[]{:S(2)}, u32[]{:S(2)}) async-start(bf16[8,16,2176]{2,1,0:T(8,128)(2,1)} %bitcast.24), calls=%async_computation.2 | async-start | bytes 1114112 | tf_op jit(solution)/shard_map/all_to_all | solution.py:468
  259.8 1.5 collective-permute-start.3
  261.3 0.6 copy-start.7
  266.5 1.8 collective-permute-start.4
  268.3 37.0 %copy-start.5 = (f32[136,512]{1,0:T(8,128)}, f32[136,512]{1,0:T(8,128)S(1)}, u32[]{:S(2)}) copy-start(f32[136,512]{1,0:T(8,128)S(1)} %collective-permute-done.4.refs_7_) | copy-start | bytes 835588
  278.5 0.8 copy-start.3
  303.3 2.0 copy-start.1
  303.3 2.0 collective-permute-start.5
  305.3 0.8 copy-start.4
  334.1 4.4 %copy-start.2 = (bf16[8,16,2176]{2,1,0:T(8,128)(2,1)S(1)}, bf16[8,16,2176]{2,1,0:T(8,128)(2,1)}, u32[]{:S(2)}) copy-start(bf16[8,16,2176]{2,1,0:T(8,128)(2,1)} %copy-done.1) | copy-start | bytes 1671172
  334.1 5.3 %copy-start.11 = (f32[128,256]{1,0:T(8,128)S(1)}, f32[128,256]{1,0:T(8,128)}, u32[]{:S(2)}) copy-start(f32[128,256]{1,0:T(8,128)} %get-tuple-element.43) | copy-start | bytes 393220
  334.1 6.6 %copy-start.8 = (f32[128,256]{1,0:T(8,128)S(1)}, f32[128,256]{1,0:T(8,128)}, u32[]{:S(2)}) copy-start(f32[128,256]{1,0:T(8,128)} %get-tuple-element.42) | copy-start | bytes 393220
  335.0 20.2 %all-to-all-start.5 = ((bf16[8,128,256]{2,1,0:T(8,128)(2,1)}), bf16[8,128,256]{2,1,0:T(8,128)(2,1)S(1)}, u32[]{:S(2)}, u32[]{:S(2)}) async-start(bf16[8,128,256]{2,1,0:T(8,128)(2,1)} %sum_chips.1), calls=%async_computation.5 | async-start | bytes 1048576 | tf_op jit(solution)/shard_map/all_to_all | solution.py:493
  339.4 1.3 collective-permute-start.6
Sparse Core Ops, SparseCore 0:
  127.5 58.8 all-gather.1

commit v3 on v2

--- a/solution.py
+++ b/solution.py
@@ -9,17 +9,21 @@
 
 HEAD_DIM = 128
 CAP = 12
+BF = jnp.bfloat16
+F32 = jnp.float32
 PAIR = 2 * CAP
 EPS = 1e-06
-BF = jnp.bfloat16
-F32 = jnp.float32
 SCALE = 1.0 / math.sqrt(HEAD_DIM)
 NT = (((1,), (1,)), ((), ()))
 TN = (((0,), (0,)), ((), ()))
 MB = 1 << 20
-NEAR_MIB = 57
+NEAR_MIB = 60
+PACK_ROWS = 1024
+NEAR_TYPE = BF
+NEAR_ROWS = 384
+FAR_ROWS = 384
 GRADS_MIB = 62
-FINISH_MIB = 62
+FINISH_MIB = 32
 FAR_MIB = 60
 
 
@@ -129,38 +133,38 @@
     )(quarter, ids, weights, hidden, upstream, gain)
 
 
-def pack_kernel(count, q_ref, g_ref, u_ref, d_ref, *refs):
-    out_refs, sems = refs[:count], refs[count]
-    unit = g_ref.shape[2]
-    blocks = d_ref.shape[2] // unit
-    copies = []
-    for n, out in enumerate(out_refs):
-        which = q_ref[n]
-        pairs = [(g_ref.at[which], out.at[0]), (u_ref.at[which], out.at[1])]
-        for k in range(blocks):
-            at = pl.ds(k * unit, unit)
-            pairs.append((d_ref.at[which, :, at], out.at[2, at]))
-        copies += pairs
-    copies = [pltpu.make_async_copy(src, dst, sems.at[k]) for k, (src, dst) in enumerate(copies)]
-    for copy in copies:
-        copy.start()
-    for copy in copies:
-        copy.wait()
+def pack_kernel(count, q_ref, *refs):
+    for n in range(count):
+        g_ref, u_ref, d_ref = refs[3 * n : 3 * n + 3]
+        out_ref = refs[3 * count + n]
+        unit = g_ref.shape[2]
+        out_ref[0] = g_ref[0]
+        out_ref[1] = u_ref[0]
+        for k in range(d_ref.shape[2] // unit):
+            out_ref[2, k * unit : (k + 1) * unit] = d_ref[0, :, k * unit : (k + 1) * unit]
 
 
 def pack(which, w_gate, w_up, w_down):
     width, unit = w_gate.shape[1:]
     count = which.shape[0]
-    hbm = pl.BlockSpec(memory_space=pltpu.HBM)
+    rows = PACK_ROWS
+
+    def at(n):
+        tall = pl.BlockSpec((1, rows, unit), lambda i, q: (q[n], i, 0))
+        return [tall, tall, pl.BlockSpec((1, unit, rows), lambda i, q: (q[n], 0, i))]
+
     return pl.pallas_call(
         lambda *refs: pack_kernel(count, *refs),
-        in_specs=[pl.BlockSpec(memory_space=pltpu.SMEM), hbm, hbm, hbm],
-        out_specs=[hbm] * count,
+        grid_spec=pltpu.PrefetchScalarGridSpec(
+            num_scalar_prefetch=1,
+            grid=(width // rows,),
+            in_specs=sum([at(n) for n in range(count)], []),
+            out_specs=[pl.BlockSpec((3, rows, unit), lambda i, q: (0, i, 0))] * count,
+        ),
         out_shape=[jax.ShapeDtypeStruct((3, width, unit), BF)] * count,
-        scratch_shapes=[pltpu.SemaphoreType.DMA((count * (2 + width // unit),))],
         compiler_params=params(),
         name="pack",
-    )(which, w_gate, w_up, w_down)
+    )(which, *[w_gate, w_up, w_down] * count)
 
 
 def unpack(ref):
@@ -193,14 +197,14 @@
     w_in = jnp.concatenate([go_ref[0], one[0], two[0], uo_ref[0], one[1], two[1]], axis=1)
     w_down = jnp.concatenate([do_ref[0], one[2], two[2]], axis=0)
     out, d_route = expert_rows(xy_ref[...], w_in, w_down)
-    out_ref[:, : width // 2] = out
-    out_ref[:, width // 2 :] = d_route
+    out_ref[:, : width // 2] = out.astype(NEAR_TYPE)
+    out_ref[:, width // 2 :] = d_route.astype(NEAR_TYPE)
 
 
 def expert_near(quarter, xy, w_gate, w_up, w_down, got_a, got_b):
     slots, width = xy.shape
     unit = w_gate.shape[2]
-    rows = 384
+    rows = NEAR_ROWS
     own = pl.BlockSpec((1, width, unit), lambda i, p: (p[0], 0, 0))
     narrow = width // 2 + 128
     return pl.pallas_call(
@@ -218,7 +222,7 @@
             ],
             out_specs=pl.BlockSpec((rows, narrow), lambda i, p: (i, 0)),
         ),
-        out_shape=jax.ShapeDtypeStruct((slots, narrow), F32),
+        out_shape=jax.ShapeDtypeStruct((slots, narrow), NEAR_TYPE),
         compiler_params=params(NEAR_MIB),
         name="expert_near",
     )(quarter, xy, w_gate, w_up, w_down, got_a, got_b)
@@ -235,7 +239,7 @@
 def expert_far(xy, got, near):
     slots, width = xy.shape
     narrow = near.shape[1]
-    rows = 192
+    rows = FAR_ROWS
     block = pl.BlockSpec((rows, narrow), lambda i: (i, 0))
     return pl.pallas_call(
         far_kernel,

time: 364 us -> 239 us (0.66)
  Pallas kernels: 190 us -> 46 us
  waiting for transfers between devices: 51 us -> 70.3 us
    pallas_call x2, Pallas kernels: 146 us -> 6.29 us  [pack(): pl.pallas_call(lambda *refs: pack_kernel(count, *refs), grid_spec=pltpu.P...]
    all_to_all x1, waiting for transfers between devices: 0.01 us -> 15.6 us  [body(): lax.all_to_all(send.reshape(ctx_count, PAIR, width), 'context', 0, 0, til...]
    ppermute x3, waiting for transfers between devices: 21.5 us -> 25.2 us  [trade(): return lax.ppermute(w, ('expert', 'context'), moves(step))]
  transfers between devices with their start and end apart: 11 -> 11, of which waited for: 7 -> 9; matrix products, arithmetic and copies ran while one was open for 1% -> 1% of each run, Pallas kernels for 21% -> 12%
where the time goes in v3:
time: 239 us
  blocking collectives  73.6 us (31%)
  waiting for transfers between devices  70.3 us (29%)
  Pallas kernels  46 us (19%)
  starting transfers between devices  28.1 us (12%)
  between operations  14.2 us (6%)
  local copies, waits for them, and re-layouts  4.63 us (2%)
    all_to_all x1, blocking collectives, body(): lax.all_to_all(rows.reshape(ctx_count, PAIR, narrow), 'context', 0, 0, ti...  31.6 us
    ppermute x3, waiting for transfers between devices, trade(): return lax.ppermute(w, ('expert', 'context'), moves(step))  25.2 us
    all_to_all x1, blocking collectives, body(): lax.all_to_all(done, 'expert', 0, 0, tiled=True).reshape(tokens, wide)  21 us
    all_to_all x1, blocking collectives, body(): lax.all_to_all(part.reshape(chips, tokens, 2 * HEAD_DIM), 'context', 0, 0...  21 us
    pallas_call x5, Pallas kernels, on_chip(): pl.pallas_call(kernel, in_specs=[pl.BlockSpec(memory_space=pltpu.SMEM)] *...  16.9 us
    all_to_all x1, waiting for transfers between devices, body(): lax.all_to_all(send.reshape(ctx_count, PAIR, width), 'context', 0, 0, til...  15.6 us
    all_to_all x1, waiting for transfers between devices, body(): part = lax.all_to_all(part, 'expert', 0, 0, tiled=True)  13.8 us
    pallas_call x1, Pallas kernels, expert_near(): pl.pallas_call(lambda *refs: near_kernel(rows, *refs), grid_spec=pltpu.Pr...  11.7 us
  transfers between devices with their start and end apart: 11, of which 9 were waited for; matrix products, arithmetic and copies ran while one was open for 1% of the time, Pallas kernels for 12%

profile of v3, /device:TPU:2, one launch (start us, length us, event | category | flops | bytes accessed | tf_op | source)
XLA Modules:
  0.0 238.7 jit_solution(7517862712818652706)
XLA Ops:
  7.2 0.6 pad_add_fusion.refs_0_
  7.8 3.9 %pack.3 = (bf16[3,2048,128]{2,1,0:T(8,128)(2,1)}, bf16[3,2048,128]{2,1,0:T(8,128)(2,1)}) custom-call(s32[2]{0:T(128)} %pad_add_fusion.refs_0_, bf16[4,2048,128]{2,1,0:T(8,128)(2,1)} %refs_2_.6, bf16[4,2048,128]{2,1,0:T(8,128)(2,1)} %refs_3_.7, bf16[4,128,2048]{2,1,0:T(8,128)(2,1)} %refs_4_.5, bf16[4,2048,128]{2,1,0:T(8,128)(2,1)} %refs_2_.6, ...), custom_call_target="tpu_custom_call" | custom-call | tf_op jit(solution)/shard_map/pack/pallas_call | solution.py:156
  11.6 1.9 collective-permute-start
  13.6 4.0 %collective-permute-start.1 = (bf16[3,2048,128]{2,1,0:T(8,128)(2,1)}, bf16[3,2048,128]{2,1,0:T(8,128)(2,1)}, u32[]{:S(2)}, u32[]{:S(2)}) collective-permute-start(bf16[3,2048,128]{2,1,0:T(8,128)(2,1)} %get-tuple-element.28), channel_id=1, source_target_pairs={{0,224},{32,0},{64,32},{96,64},{128,96},{160,128},{192,160},{224,1... | collective-permute-start | bytes 4718600 | tf_op jit(solution)/shard_map/ppermute | solution.py:442
  17.6 4.6 %route.1 = (bf16[768,2048]{1,0:T(8,128)(2,1)}, bf16[768,128]{1,0:T(8,128)(2,1)}, bf16[768,128]{1,0:T(8,128)(2,1)}, bf16[768,128]{1,0:T(8,128)(2,1)}) custom-call(s32[1]{0:T(128)} %bitcast.1.refs_0_, s32[8,128]{1,0:T(8,128)} %bitcast.28, bf16[8,128]{1,0:T(8,128)(2,1)} %bitcast.30, bf16[128,2048]{1,0:T(8,128)(2,1)} %refs_6_.3, bf16[128,2048]{1,0:T(8,128)(2,1)} %up_ref.1, ...), custom_call_target="tpu_custom_call" | custom-call | tf_op jit(solution)/shard_map/route/pallas_call | solution.py:109
  22.2 0.0 copy-start.10
  22.3 7.8 %all-to-all-start = ((bf16[32,24,2048]{2,1,0:T(8,128)(2,1)}), bf16[32,24,2048]{2,1,0:T(8,128)(2,1)S(1)}, u32[]{:S(2)}, u32[]{:S(2)}) async-start(bf16[32,24,2048]{2,1,0:T(8,128)(2,1)} %bitcast.23), calls=%async_computation | async-start | bytes 6291456 | tf_op jit(solution)/shard_map/all_to_all | solution.py:457
  30.0 0.0 all-gather.2.cloned.1.call-start
  30.1 0.6 pad_maximum_fusion
  30.8 0.0 all-gather.2.cloned.1.call-update
  30.8 2.4 %pack.2 = bf16[3,2048,128]{2,1,0:T(8,128)(2,1)} custom-call(s32[1]{0:T(128)} %bitcast.7.refs_0_, bf16[4,2048,128]{2,1,0:T(8,128)(2,1)} %refs_2_.6, bf16[4,2048,128]{2,1,0:T(8,128)(2,1)} %refs_3_.7, bf16[4,128,2048]{2,1,0:T(8,128)(2,1)} %refs_4_.5), custom_call_target="tpu_custom_call" | custom-call | tf_op jit(solution)/shard_map/pack/pallas_call | solution.py:156
  33.2 19.0 %collective-permute-done.refs_5_ = bf16[3,2048,128]{2,1,0:T(8,128)(2,1)} collective-permute-done((bf16[3,2048,128]{2,1,0:T(8,128)(2,1)}, bf16[3,2048,128]{2,1,0:T(8,128)(2,1)}, u32[]{:S(2)}, u32[]{:S(2)}) %collective-permute-start) | collective-permute-done | bytes 1572896 | tf_op jit(solution)/shard_map/ppermute | solution.py:442
  52.2 0.0 collective-permute-done.1.refs_6_
  52.2 2.9 %collective-permute-start.2 = (bf16[3,2048,128]{2,1,0:T(8,128)(2,1)}, bf16[3,2048,128]{2,1,0:T(8,128)(2,1)}, u32[]{:S(2)}, u32[]{:S(2)}) collective-permute-start(bf16[3,2048,128]{2,1,0:T(8,128)(2,1)} %pack.2), channel_id=1, source_target_pairs={{0,192},{32,224},{64,0},{96,32},{128,64},{160,96},{192,128},{224,1... | collective-permute-start | bytes 4718600 | tf_op jit(solution)/shard_map/ppermute | solution.py:442
  55.1 15.6 %all-to-all-done = bf16[32,24,2048]{2,1,0:T(8,128)(2,1)S(1)} async-done(((bf16[32,24,2048]{2,1,0:T(8,128)(2,1)}), bf16[32,24,2048]{2,1,0:T(8,128)(2,1)S(1)}, u32[]{:S(2)}, u32[]{:S(2)}) %all-to-all-start) | async-done | bytes 3145760 | tf_op jit(solution)/shard_map/all_to_all | solution.py:457
  70.7 1.6 copy-done.1
  72.4 11.7 %expert_near.1.near_ref = bf16[768,1152]{1,0:T(8,128)(2,1)} custom-call(s32[1]{0:T(128)} %bitcast.1.refs_0_, bf16[768,2048]{1,0:T(8,128)(2,1)} %bitcast.15, bf16[4,2048,128]{2,1,0:T(8,128)(2,1)} %refs_2_.6, bf16[4,2048,128]{2,1,0:T(8,128)(2,1)} %refs_3_.7, bf16[4,128,2048]{2,1,0:T(8,128)(2,1)} %refs_4_.5, ...), custom_call_target="tpu_custom_call" | custom-call | tf_op jit(solution)/shard_map/expert_near/pallas_call | solution.py:210
  84.1 6.2 %collective-permute-done.2.far_ref = bf16[3,2048,128]{2,1,0:T(8,128)(2,1)} collective-permute-done((bf16[3,2048,128]{2,1,0:T(8,128)(2,1)}, bf16[3,2048,128]{2,1,0:T(8,128)(2,1)}, u32[]{:S(2)}, u32[]{:S(2)}) %collective-permute-start.2) | collective-permute-done | bytes 1572896 | tf_op jit(solution)/shard_map/ppermute | solution.py:442
  90.3 6.4 %expert_far.1 = bf16[768,1152]{1,0:T(8,128)(2,1)} custom-call(bf16[768,2048]{1,0:T(8,128)(2,1)} %bitcast.16, bf16[3,2048,128]{2,1,0:T(8,128)(2,1)} %collective-permute-done.2.far_ref, bf16[768,1152]{1,0:T(8,128)(2,1)} %expert_near.1.near_ref), custom_call_target="tpu_custom_call" | custom-call | tf_op jit(solution)/shard_map/expert_far/pallas_call | solution.py:244
  96.7 31.6 %all_to_all.30 = bf16[32,24,1152]{2,1,0:T(8,128)(2,1)} all-to-all(bf16[32,24,1152]{2,1,0:T(8,128)(2,1)} %bitcast.18), channel_id=1, replica_groups=mesh['expert'=8,'context'=32] {'context'}, dimensions={0} | all-to-all | bytes 3538944 | tf_op jit(solution)/shard_map/all_to_all | solution.py:463
  128.2 3.7 %gather_rows.1 = bf16[128,2176]{1,0:T(8,128)(2,1)} custom-call(s32[1]{0:T(128)} %bitcast.1.refs_0_, bf16[768,1152]{1,0:T(8,128)(2,1)} %bitcast.17, bf16[768,128]{1,0:T(8,128)(2,1)} %get-tuple-element.33.refs_2_, bf16[768,128]{1,0:T(8,128)(2,1)} %get-tuple-element.34.refs_3_, bf16[768,128]{1,0:T(8,128)(2,1)} %get-tuple-element.35.refs_4_, s32[8,128]{1,0:T(8,128)} %bitcast.29, ...), custom_call_target="tpu_custom_call" | custom-call | tf_op jit(solution)/shard_map/gather_rows/pallas_call | solution.py:283
  131.9 7.5 %all-to-all-start.2 = ((bf16[8,16,2176]{2,1,0:T(8,128)(2,1)}), bf16[8,16,2176]{2,1,0:T(8,128)(2,1)S(1)}, u32[]{:S(2)}, u32[]{:S(2)}) async-start(bf16[8,16,2176]{2,1,0:T(8,128)(2,1)} %bitcast.24), calls=%async_computation.2 | async-start | bytes 1114112 | tf_op jit(solution)/shard_map/all_to_all | solution.py:472
  139.4 0.0 copy-done.6
  139.4 0.3 collective-permute-start.3
  139.7 1.2 collective-permute-done.3.refs_1_.refs_4_
  140.9 0.6 copy-done.7
  141.5 4.6 %attention_probs.1 = (bf16[2048,512]{1,0:T(8,128)(2,1)}, f32[136,512]{1,0:T(8,128)}) custom-call(bf16[128,256]{1,0:T(8,128)(2,1)} %refs_3_.8, bf16[128,256]{1,0:T(8,128)(2,1)} %copy-done.7, bf16[2048,256]{1,0:T(8,128)(2,1)} %all-gather.2.cloned.1.call-done.refs_2_.refs_8_), custom_call_target="tpu_custom_call" | custom-call | tf_op jit(solution)/shard_map/attention_probs/pallas_call | solution.py:283
  146.1 0.2 collective-permute-start.4
  146.3 1.6 collective-permute-done.4.refs_7_
  147.9 10.2 %all-to-all-done.2.in_ref = bf16[8,16,2176]{2,1,0:T(8,128)(2,1)S(1)} async-done(((bf16[8,16,2176]{2,1,0:T(8,128)(2,1)}), bf16[8,16,2176]{2,1,0:T(8,128)(2,1)S(1)}, u32[]{:S(2)}, u32[]{:S(2)}) %all-to-all-start.2) | async-done | bytes 557088 | tf_op jit(solution)/shard_map/all_to_all | solution.py:472
  158.1 0.0 copy-done
  158.1 0.1 finish_hidden.1
  158.2 21.0 %all_to_all.31 = bf16[8,16,2176]{2,1,0:T(8,128)(2,1)S(1)} all-to-all(bf16[8,16,2176]{2,1,0:T(8,128)(2,1)S(1)} %finish_hidden.1), channel_id=1, replica_groups=mesh['expert'=8,'context'=32] {'expert'}, dimensions={0} | all-to-all | bytes 1114112 | tf_op jit(solution)/shard_map/all_to_all | solution.py:479
  179.2 0.0 collective-permute-start.5
  179.2 2.0 collective-permute-done.5.refs_1_
  181.2 0.0 copy-done.5
  181.2 0.8 copy-done.4
  182.0 7.0 %attention_grads.1 = (f32[128,256]{1,0:T(8,128)}, f32[128,256]{1,0:T(8,128)}, bf16[2048,256]{1,0:T(8,128)(2,1)}) custom-call(bf16[128,2176]{1,0:T(8,128)(2,1)} %bitcast.20, bf16[128,2176]{1,0:T(8,128)(2,1)} %copy-done.4, bf16[256,2048]{1,0:T(8,128)(2,1)} %refs_2_.7, bf16[128,256]{1,0:T(8,128)(2,1)} %refs_3_.8, bf16[128,256]{1,0:T(8,128)(2,1)} %copy-done.7, ...), custom_call_target="tpu_custom_call" | custom-call | tf_op jit(solution)/shard_map/attention_grads/pallas_call | solution.py:283
  189.0 21.0 %all_to_all.32.in_ref = bf16[16,128,256]{2,1,0:T(8,128)(2,1)S(1)} all-to-all(bf16[16,128,256]{2,1,0:T(8,128)(2,1)} %bitcast.25), channel_id=1, replica_groups={{0,2,4,6,8,10,12,14,16,18,20,22,24,26,28,30},{1,3,5,7,9,11,13,15,17,19,..., dimensions={0} | all-to-all | bytes 2097152 | tf_op jit(solution)/shard_map/all_to_all | solution.py:493
  210.0 0.9 sum_chips.1
  210.9 3.5 %all-to-all-start.5 = ((bf16[8,128,256]{2,1,0:T(8,128)(2,1)}), bf16[8,128,256]{2,1,0:T(8,128)(2,1)S(1)}, u32[]{:S(2)}, u32[]{:S(2)}) async-start(bf16[8,128,256]{2,1,0:T(8,128)(2,1)} %sum_chips.1), calls=%async_computation.5 | async-start | bytes 1048576 | tf_op jit(solution)/shard_map/all_to_all | solution.py:497
  214.4 0.8 slice.8
  215.3 0.0 collective-permute-start.6
  215.3 0.7 copy.17
  215.9 0.7 collective-permute-done.6
  216.6 0.7 add.38
  217.3 13.8 %all-to-all-done.5.in_ref = bf16[8,128,256]{2,1,0:T(8,128)(2,1)S(1)} async-done(((bf16[8,128,256]{2,1,0:T(8,128)(2,1)}), bf16[8,128,256]{2,1,0:T(8,128)(2,1)S(1)}, u32[]{:S(2)}, u32[]{:S(2)}) %all-to-all-start.5) | async-done | bytes 524320 | tf_op jit(solution)/shard_map/all_to_all | solution.py:497
  231.1 0.7 sum_heads.1
  (20 shorter events, 0.1 us)
Async XLA Ops:
  11.6 40.6 %collective-permute-start = (bf16[3,2048,128]{2,1,0:T(8,128)(2,1)}, bf16[3,2048,128]{2,1,0:T(8,128)(2,1)}, u32[]{:S(2)}, u32[]{:S(2)}) collective-permute-start(bf16[3,2048,128]{2,1,0:T(8,128)(2,1)} %get-tuple-element.27), channel_id=1, source_target_pairs={{0,32},{32,64},{64,96},{96,128},{128,160},{160,192},{192,224},{224... | collective-permute-start | bytes 4718600 | tf_op jit(solution)/shard_map/ppermute | solution.py:442
  13.6 38.6 %collective-permute-start.1 = (bf16[3,2048,128]{2,1,0:T(8,128)(2,1)}, bf16[3,2048,128]{2,1,0:T(8,128)(2,1)}, u32[]{:S(2)}, u32[]{:S(2)}) collective-permute-start(bf16[3,2048,128]{2,1,0:T(8,128)(2,1)} %get-tuple-element.28), channel_id=1, source_target_pairs={{0,224},{32,0},{64,32},{96,64},{128,96},{160,128},{192,160},{224,1... | collective-permute-start | bytes 4718600 | tf_op jit(solution)/shard_map/ppermute | solution.py:442
  22.2 7.9 %copy-start.9 = (bf16[128,256]{1,0:T(8,128)(2,1)S(1)}, bf16[128,256]{1,0:T(8,128)(2,1)}, u32[]{:S(2)}) copy-start(bf16[128,256]{1,0:T(8,128)(2,1)} %param.23) | copy-start | bytes 196612
  22.2 7.9 %copy-start.10 = (bf16[128,256]{1,0:T(8,128)(2,1)S(1)}, bf16[128,256]{1,0:T(8,128)(2,1)}, u32[]{:S(2)}) copy-start(bf16[128,256]{1,0:T(8,128)(2,1)} %param.22) | copy-start | bytes 196612
  22.3 48.5 %all-to-all-start = ((bf16[32,24,2048]{2,1,0:T(8,128)(2,1)}), bf16[32,24,2048]{2,1,0:T(8,128)(2,1)S(1)}, u32[]{:S(2)}, u32[]{:S(2)}) async-start(bf16[32,24,2048]{2,1,0:T(8,128)(2,1)} %bitcast.23), calls=%async_computation | async-start | bytes 6291456 | tf_op jit(solution)/shard_map/all_to_all | solution.py:457
  30.0 66.6 %all-gather.2.cloned.1.call-start = ((), (), s32[]{:S(2)}) async-start(), calls=%async_computation.6 | async-start | bytes 1114112 | tf_op jit(solution)/shard_map/all_gather | solution.py:454
  52.2 38.1 %collective-permute-start.2 = (bf16[3,2048,128]{2,1,0:T(8,128)(2,1)}, bf16[3,2048,128]{2,1,0:T(8,128)(2,1)}, u32[]{:S(2)}, u32[]{:S(2)}) collective-permute-start(bf16[3,2048,128]{2,1,0:T(8,128)(2,1)} %pack.2), channel_id=1, source_target_pairs={{0,192},{32,224},{64,0},{96,32},{128,64},{160,96},{192,128},{224,1... | collective-permute-start | bytes 4718600 | tf_op jit(solution)/shard_map/ppermute | solution.py:442
  70.7 1.6 copy-start.1
  128.2 11.2 %copy-start.6 = (bf16[128,256]{1,0:T(8,128)(2,1)S(1)}, bf16[128,256]{1,0:T(8,128)(2,1)}, u32[]{:S(2)}) copy-start(bf16[128,256]{1,0:T(8,128)(2,1)} %refs_3_.8) | copy-start | bytes 196612
  131.9 26.2 %copy-start = (bf16[128,2048]{1,0:T(8,128)(2,1)S(1)}, bf16[128,2048]{1,0:T(8,128)(2,1)}, u32[]{:S(2)}) copy-start(bf16[128,2048]{1,0:T(8,128)(2,1)} %up_ref.1) | copy-start | bytes 1572868
  131.9 26.2 %all-to-all-start.2 = ((bf16[8,16,2176]{2,1,0:T(8,128)(2,1)}), bf16[8,16,2176]{2,1,0:T(8,128)(2,1)S(1)}, u32[]{:S(2)}, u32[]{:S(2)}) async-start(bf16[8,16,2176]{2,1,0:T(8,128)(2,1)} %bitcast.24), calls=%async_computation.2 | async-start | bytes 1114112 | tf_op jit(solution)/shard_map/all_to_all | solution.py:472
  139.4 1.5 collective-permute-start.3
  140.9 0.6 copy-start.7
  146.1 1.8 collective-permute-start.4
  147.9 33.3 %copy-start.5 = (f32[136,512]{1,0:T(8,128)}, f32[136,512]{1,0:T(8,128)S(1)}, u32[]{:S(2)}) copy-start(f32[136,512]{1,0:T(8,128)S(1)} %collective-permute-done.4.refs_7_) | copy-start | bytes 835588
  179.2 2.0 copy-start.2
  179.2 2.0 collective-permute-start.5
  181.2 0.8 copy-start.4
  210.0 4.4 %copy-start.3 = (bf16[8,16,2176]{2,1,0:T(8,128)(2,1)S(1)}, bf16[8,16,2176]{2,1,0:T(8,128)(2,1)}, u32[]{:S(2)}) copy-start(bf16[8,16,2176]{2,1,0:T(8,128)(2,1)} %copy-done.2) | copy-start | bytes 1671172
  210.0 5.3 %copy-start.11 = (f32[128,256]{1,0:T(8,128)S(1)}, f32[128,256]{1,0:T(8,128)}, u32[]{:S(2)}) copy-start(f32[128,256]{1,0:T(8,128)} %get-tuple-element.43) | copy-start | bytes 393220
  210.0 6.6 %copy-start.8 = (f32[128,256]{1,0:T(8,128)S(1)}, f32[128,256]{1,0:T(8,128)}, u32[]{:S(2)}) copy-start(f32[128,256]{1,0:T(8,128)} %get-tuple-element.42) | copy-start | bytes 393220
  210.9 20.2 %all-to-all-start.5 = ((bf16[8,128,256]{2,1,0:T(8,128)(2,1)}), bf16[8,128,256]{2,1,0:T(8,128)(2,1)S(1)}, u32[]{:S(2)}, u32[]{:S(2)}) async-start(bf16[8,128,256]{2,1,0:T(8,128)(2,1)} %sum_chips.1), calls=%async_computation.5 | async-start | bytes 1048576 | tf_op jit(solution)/shard_map/all_to_all | solution.py:497
  215.3 1.3 collective-permute-start.6
Sparse Core Ops, SparseCore 0:
  33.9 58.8 all-gather.1

commit v4 on v3

--- a/solution.py
+++ b/solution.py
@@ -19,6 +19,8 @@
 MB = 1 << 20
 NEAR_MIB = 60
 PACK_ROWS = 1024
+PICK_COST = 30000000000
+GRADS_ROWS = 1024
 NEAR_TYPE = BF
 NEAR_ROWS = 384
 FAR_ROWS = 384
@@ -167,6 +169,27 @@
     )(which, *[w_gate, w_up, w_down] * count)
 
 
+def pick_kernel(q_ref, w_ref, out_ref):
+    out_ref[...] = w_ref[...]
+
+
+def pick(which, w):
+    _, unit, width = w.shape
+    return pl.pallas_call(
+        pick_kernel,
+        grid_spec=pltpu.PrefetchScalarGridSpec(
+            num_scalar_prefetch=1,
+            grid=(1,),
+            in_specs=[pl.BlockSpec((1, unit, width), lambda i, q: (q[0], 0, 0))],
+            out_specs=whole((1, unit, width)),
+        ),
+        out_shape=jax.ShapeDtypeStruct((1, unit, width), BF),
+        cost_estimate=pl.CostEstimate(flops=PICK_COST, bytes_accessed=2 * unit * width * 2, transcendentals=0),
+        compiler_params=params(),
+        name="pick",
+    )(which, w)
+
+
 def unpack(ref):
     unit = ref.shape[2]
     down = [ref[2, n * unit : (n + 1) * unit] for n in range(ref.shape[1] // unit)]
@@ -228,15 +251,14 @@
     )(quarter, xy, w_gate, w_up, w_down, got_a, got_b)
 
 
-def far_kernel(xy_ref, far_ref, near_ref, out_ref):
+def far_kernel(xy_ref, in_ref, down_ref, near_ref, out_ref):
     width = xy_ref.shape[1]
-    w_gate, w_up, w_down = unpack(far_ref)
-    out, d_route = expert_rows(xy_ref[...], jnp.concatenate([w_gate, w_up], axis=1), w_down)
+    out, d_route = expert_rows(xy_ref[...], jnp.concatenate([in_ref[0], in_ref[1]], axis=1), down_ref[0])
     out_ref[:, : width // 2] = (near_ref[:, : width // 2] + out).astype(BF)
     out_ref[:, width // 2 :] = (near_ref[:, width // 2 :] + d_route).astype(BF)
 
 
-def expert_far(xy, got, near):
+def expert_far(xy, w_in, w_down, near):
     slots, width = xy.shape
     narrow = near.shape[1]
     rows = FAR_ROWS
@@ -244,12 +266,12 @@
     return pl.pallas_call(
         far_kernel,
         grid=(slots // rows,),
-        in_specs=[pl.BlockSpec((rows, width), lambda i: (i, 0)), whole(got.shape), block],
+        in_specs=[pl.BlockSpec((rows, width), lambda i: (i, 0)), whole(w_in.shape), whole(w_down.shape), block],
         out_specs=block,
         out_shape=jax.ShapeDtypeStruct((slots, narrow), BF),
         compiler_params=params(FAR_MIB),
         name="expert_far",
-    )(xy, got, near)
+    )(xy, w_in, w_down, near)
 
 
 def gather_kernel(per, count, q_ref, back_ref, s0_ref, sw0_ref, sw1_ref, ids_ref, hid_ref, gain_ref, out_ref):
@@ -379,38 +401,74 @@
         [], [queries, other, kv], [pltpu.VMEM((count, rows), F32)])
 
 
-def grads_kernel(chunk, dh_ref, do_ref, w_ref, q_ref, o_ref, p_ref, stat_ref, far_ref, kv_ref, dq_ref, dqo_ref, dkv_ref):
+def grads_kernel(dh_ref, do_ref, w_ref, q_ref, o_ref, stat_ref, far_ref, p_ref, kv_ref,
+                 dq_ref, dqo_ref, dkv_ref, t_ref, d_ref, row_ref, query_ref, sum_ref):
+    step = pl.program_id(0)
     width = w_ref.shape[1]
     tokens = dh_ref.shape[0]
-    d_hidden = jnp.concatenate([dh_ref[:, :width], do_ref[:, :width]], axis=0)
-    d_out_w = nt(w_ref[...], d_hidden).astype(BF)
-    parts = [d_out_w[h * HEAD_DIM : (h + 1) * HEAD_DIM, c * tokens : (c + 1) * tokens] for c in range(2) for h in range(2)]
-    d_out_t = jnp.concatenate(parts, axis=1)
-    d_out = jnp.concatenate([p.T for p in parts], axis=0)
-    query = jnp.concatenate([heads_to_rows(q_ref[...]), heads_to_rows(o_ref[...])], axis=0)
-    half = query.shape[0] // 2
-    here = stat_ref[...]
-    there = jnp.concatenate([far_ref[:, half:], far_ref[:, :half]], axis=1)
-    top_here, top_there = here[HEAD_DIM : HEAD_DIM + 1], there[HEAD_DIM : HEAD_DIM + 1]
-    top = jnp.maximum(top_here, top_there)
-    in_here, in_there = jnp.exp(top_here - top), jnp.exp(top_there - top)
-    total = here[HEAD_DIM + 1 : HEAD_DIM + 2] * in_here + there[HEAD_DIM + 1 : HEAD_DIM + 2] * in_there
-    in_here, in_there = in_here / total, in_there / total
-    out = here[:HEAD_DIM] * in_here + there[:HEAD_DIM] * in_there
-    delta = jnp.sum(d_out_t.astype(F32) * out, axis=0, keepdims=True)
-    d_query = jnp.zeros((HEAD_DIM, 2 * half), F32)
-    for n in range(0, kv_ref.shape[0], chunk):
-        span = slice(n, n + chunk)
-        p = p_ref[span].astype(F32) * in_here
-        d_probs = nn(kv_ref[span, HEAD_DIM:], d_out_t)
-        ds = (p * (d_probs - delta)).astype(BF)
-        dkv_ref[span, :HEAD_DIM] = (nn(ds, query) * SCALE).astype(BF)
-        dkv_ref[span, HEAD_DIM:] = nn(p.astype(BF), d_out).astype(BF)
-        d_query = d_query + tn(kv_ref[span, :HEAD_DIM], ds)
-    d_query = (d_query * SCALE).T
-    for ref, at in ((dq_ref, 0), (dqo_ref, half)):
-        ref[:, :HEAD_DIM] = d_query[at : at + tokens]
-        ref[:, HEAD_DIM:] = d_query[at + tokens : at + 2 * tokens]
+    half = sum_ref.shape[1] // 2
+
+    @pl.when(step == 0)
+    def _():
+        d_hidden = jnp.concatenate([dh_ref[:, :width], do_ref[:, :width]], axis=0)
+        d_out_w = nt(w_ref[...], d_hidden).astype(BF)
+        parts = [d_out_w[h * HEAD_DIM : (h + 1) * HEAD_DIM, c * tokens : (c + 1) * tokens] for c in range(2) for h in range(2)]
+        d_out_t = jnp.concatenate(parts, axis=1)
+        t_ref[...] = d_out_t
+        d_ref[...] = jnp.concatenate([p.T for p in parts], axis=0)
+        query_ref[...] = jnp.concatenate([heads_to_rows(q_ref[...]), heads_to_rows(o_ref[...])], axis=0)
+        here = stat_ref[...]
+        there = jnp.concatenate([far_ref[:, half:], far_ref[:, :half]], axis=1)
+        top_here, top_there = here[HEAD_DIM : HEAD_DIM + 1], there[HEAD_DIM : HEAD_DIM + 1]
+        top = jnp.maximum(top_here, top_there)
+        in_here, in_there = jnp.exp(top_here - top), jnp.exp(top_there - top)
+        total = here[HEAD_DIM + 1 : HEAD_DIM + 2] * in_here + there[HEAD_DIM + 1 : HEAD_DIM + 2] * in_there
+        in_here, in_there = in_here / total, in_there / total
+        out = here[:HEAD_DIM] * in_here + there[:HEAD_DIM] * in_there
+        row_ref[0:1] = in_here
+        row_ref[1:2] = jnp.sum(d_out_t.astype(F32) * out, axis=0, keepdims=True)
+        sum_ref[...] = jnp.zeros_like(sum_ref)
+
+    p = p_ref[...].astype(F32) * row_ref[0:1]
+    d_probs = nn(kv_ref[:, HEAD_DIM:], t_ref[...])
+    ds = (p * (d_probs - row_ref[1:2])).astype(BF)
+    dkv_ref[:, :HEAD_DIM] = (nn(ds, query_ref[...]) * SCALE).astype(BF)
+    dkv_ref[:, HEAD_DIM:] = nn(p.astype(BF), d_ref[...]).astype(BF)
+    sum_ref[...] += tn(kv_ref[:, :HEAD_DIM], ds)
+
+    @pl.when(step == pl.num_programs(0) - 1)
+    def _():
+        d_query = (sum_ref[...] * SCALE).T
+        for ref, at in ((dq_ref, 0), (dqo_ref, half)):
+            ref[:, :HEAD_DIM] = d_query[at : at + tokens]
+            ref[:, HEAD_DIM:] = d_query[at + tokens : at + 2 * tokens]
+
+
+def grads(done, done_other, w_out, queries, other, stats, far_stats, soft, kv):
+    chunk = GRADS_ROWS
+    count, rows = soft.shape
+    fixed = [done, done_other, w_out, queries, other, stats, far_stats]
+    return pl.pallas_call(
+        grads_kernel,
+        grid=(count // chunk,),
+        in_specs=[whole(a.shape) for a in fixed]
+        + [pl.BlockSpec((chunk, rows), lambda i: (i, 0)), pl.BlockSpec((chunk, kv.shape[1]), lambda i: (i, 0))],
+        out_specs=[whole(queries.shape)] * 2 + [pl.BlockSpec((chunk, kv.shape[1]), lambda i: (i, 0))],
+        out_shape=[
+            jax.ShapeDtypeStruct(queries.shape, F32),
+            jax.ShapeDtypeStruct(queries.shape, F32),
+            jax.ShapeDtypeStruct(kv.shape, BF),
+        ],
+        scratch_shapes=[
+            pltpu.VMEM((HEAD_DIM, rows), BF),
+            pltpu.VMEM((rows, HEAD_DIM), BF),
+            pltpu.VMEM((8, rows), F32),
+            pltpu.VMEM((rows, HEAD_DIM), BF),
+            pltpu.VMEM((HEAD_DIM, rows), F32),
+        ],
+        compiler_params=params(GRADS_MIB),
+        name="attention_grads",
+    )(*fixed, soft, kv)
 
 
 def body(hidden, upstream, norm_gain, route_ids, route_weights, w_gate, w_up, w_down, w_out, queries, keys, values):
@@ -441,11 +499,13 @@
     def trade(w, step):
         return lax.ppermute(w, ("expert", "context"), moves(step))
 
-    leave = [((z + n) % per).astype(jnp.int32) for n in (1, per - 1, 2)]
-    packs = pack(jnp.stack(leave[:2]), w_gate, w_up, w_down) + pack(jnp.stack(leave[2:]), w_gate, w_up, w_down)
-    near_a, near_b = trade(packs[0], lambda core: 1), trade(packs[1], lambda core: -1)
-    distant, near_a, near_b = lax.optimization_barrier((packs[2], near_a, near_b))
-    got_far = trade(distant, far)
+    leave = jnp.stack([((z + n) % per).astype(jnp.int32) for n in (1, per - 1)])
+    near_a, near_b = pack(leave, w_gate, w_up, w_down)
+    near_a, near_b = trade(near_a, lambda core: 1), trade(near_b, lambda core: -1)
+    which = ((z + 2) % per).astype(jnp.int32)
+    far_in = trade(jnp.concatenate([lax.dynamic_slice_in_dim(w, which, 1, 0) for w in (w_gate, w_up)], axis=0), far)
+    which, near_a, near_b = lax.optimization_barrier((which, near_a, near_b))
+    far_down = trade(pick(which.reshape(1), w_down), far)
 
     ids = route_ids.T
     kv_head = z // (exp_count // 2)
@@ -458,7 +518,7 @@
     xy = xy.reshape(slots, width)
     narrow = width // 2 + 128
     near = expert_near(q_arr, xy, w_gate, w_up, w_down, near_a, near_b)
-    rows = expert_far(xy, got_far, near)
+    rows = expert_far(xy, far_in, far_down, near)
     rows, kv = lax.optimization_barrier((rows, kv))
     rows = lax.all_to_all(rows.reshape(ctx_count, PAIR, narrow), "context", 0, 0, tiled=True)
     wide = width + 128
@@ -481,14 +541,7 @@
     d_route = done[:, width : width + route_ids.shape[1]].astype(F32)
 
     done_other = lax.ppermute(done, "context", swap_core)
-    d_queries, d_other, part = on_chip(
-        lambda *refs: grads_kernel(512, *refs), "attention_grads",
-        [
-            jax.ShapeDtypeStruct(queries.shape, F32),
-            jax.ShapeDtypeStruct(queries.shape, F32),
-            jax.ShapeDtypeStruct(kv.shape, BF),
-        ],
-        [], [done, done_other, w_out, queries, other, soft, stats, far_stats, kv], mib=GRADS_MIB)
+    d_queries, d_other, part = grads(done, done_other, w_out, queries, other, stats, far_stats, soft, kv)
     d_queries = d_queries + lax.ppermute(d_other, "context", swap_core)
     part = lax.all_to_all(
         part.reshape(chips, tokens, 2 * HEAD_DIM), "context", 0, 0, tiled=True, axis_index_groups=same_core)

time: 239 us -> 235 us (0.983)
  waiting for transfers between devices: 70.3 us -> 53.2 us
  starting transfers between devices: 28.1 us -> 40.3 us
    all_to_all x1, waiting for transfers between devices: 15.6 us -> 3.45 us  [body(): lax.all_to_all(send.reshape(ctx_count, PAIR, width), 'context', 0, 0, til...]
    ppermute x3 -> x4, starting transfers between devices: 8.86 us -> 20.1 us  [trade(): return lax.ppermute(w, ('expert', 'context'), moves(step))]
    pallas_call x0 -> x2, Pallas kernels: none -> 8.06 us  [the longest x1 6.19 us: grads(): pl.pallas_call(grads_kernel, grid=(count // chunk,), in_specs=[whole(a.sh...]
    pallas_call x5 -> x4, Pallas kernels: 16.9 us -> 9.92 us  [on_chip(): pl.pallas_call(kernel, in_specs=[pl.BlockSpec(memory_space=pltpu.SMEM)] *...]
    ppermute x3 -> x4, waiting for transfers between devices: 25.2 us -> 19.2 us  [trade(): return lax.ppermute(w, ('expert', 'context'), moves(step))]
    pallas_call x2 -> x1, Pallas kernels: 6.29 us -> 3.86 us  [pack(): pl.pallas_call(lambda *refs: pack_kernel(count, *refs), grid_spec=pltpu.P...]
  transfers between devices with their start and end apart: 11 -> 12, of which waited for: 9 -> 10; matrix products, arithmetic and copies ran while one was open for 1% -> 2% of each run, Pallas kernels for 12% -> 13%
where the time goes in v4:
time: 235 us; the launch traced here: 234 us
  blocking collectives  72.8 us (31%)
  waiting for transfers between devices  53.2 us (23%)
  Pallas kernels  44.8 us (19%)
  starting transfers between devices  40.3 us (17%)
  between operations  14.2 us (6%)
  local copies, waits for them, and re-layouts  6.04 us (3%)
  other arithmetic  2.96 us (1%)
    all_to_all x1, blocking collectives, body(): lax.all_to_all(rows.reshape(ctx_count, PAIR, narrow), 'context', 0, 0, ti...  30.6 us
    all_to_all x1, blocking collectives, body(): lax.all_to_all(part.reshape(chips, tokens, 2 * HEAD_DIM), 'context', 0, 0...  21.1 us
    all_to_all x1, blocking collectives, body(): lax.all_to_all(done, 'expert', 0, 0, tiled=True).reshape(tokens, wide)  21 us
    ppermute x4, starting transfers between devices, trade(): return lax.ppermute(w, ('expert', 'context'), moves(step))  20.1 us
    ppermute x4, waiting for transfers between devices, trade(): return lax.ppermute(w, ('expert', 'context'), moves(step))  19.2 us
    all_to_all x1, waiting for transfers between devices, body(): part = lax.all_to_all(part, 'expert', 0, 0, tiled=True)  13.8 us
    pallas_call x1, Pallas kernels, expert_near(): pl.pallas_call(lambda *refs: near_kernel(rows, *refs), grid_spec=pltpu.Pr...  11.8 us
    all_to_all x1, waiting for transfers between devices, body(): arrived = lax.all_to_all(q.reshape(parts), 'expert', 0, 0, tiled=True)  10.2 us
  transfers between devices with their start and end apart: 12, of which 10 were waited for; matrix products, arithmetic and copies ran while one was open for 2% of the time, Pallas kernels for 13%

profile of v4, /device:TPU:2, one launch (start us, length us, event | category | flops | bytes accessed | tf_op | source)
XLA Modules:
  0.0 234.1 jit_solution(16369674830917637172)
XLA Ops:
  7.2 0.6 pad_add_fusion.refs_0_
  7.8 3.9 %pack.1 = (bf16[3,2048,128]{2,1,0:T(8,128)(2,1)}, bf16[3,2048,128]{2,1,0:T(8,128)(2,1)}) custom-call(s32[2]{0:T(128)} %pad_add_fusion.refs_0_, bf16[4,2048,128]{2,1,0:T(8,128)(2,1)} %refs_2_.3, bf16[4,2048,128]{2,1,0:T(8,128)(2,1)} %refs_3_.5, bf16[4,128,2048]{2,1,0:T(8,128)(2,1)} %refs_4_.5, bf16[4,2048,128]{2,1,0:T(8,128)(2,1)} %refs_2_.3, ...), custom_call_target="tpu_custom_call" | custom-call | tf_op jit(solution)/shard_map/pack/pallas_call | solution.py:158
  11.6 1.9 collective-permute-start.1
  13.5 4.0 %collective-permute-start.2 = (bf16[3,2048,128]{2,1,0:T(8,128)(2,1)}, bf16[3,2048,128]{2,1,0:T(8,128)(2,1)}, u32[]{:S(2)}, u32[]{:S(2)}) collective-permute-start(bf16[3,2048,128]{2,1,0:T(8,128)(2,1)} %get-tuple-element.28), channel_id=1, source_target_pairs={{0,224},{32,0},{64,32},{96,64},{128,96},{160,128},{192,160},{224,1... | collective-permute-start | bytes 4718600 | tf_op jit(solution)/shard_map/ppermute | solution.py:500
  17.6 4.7 %route.1 = (bf16[768,2048]{1,0:T(8,128)(2,1)}, bf16[768,128]{1,0:T(8,128)(2,1)}, bf16[768,128]{1,0:T(8,128)(2,1)}, bf16[768,128]{1,0:T(8,128)(2,1)}) custom-call(s32[1]{0:T(128)} %bitcast.1.refs_0_, s32[8,128]{1,0:T(8,128)} %bitcast.28, bf16[8,128]{1,0:T(8,128)(2,1)} %bitcast.30, bf16[128,2048]{1,0:T(8,128)(2,1)} %refs_6_.3, bf16[128,2048]{1,0:T(8,128)(2,1)} %up_ref.1, ...), custom_call_target="tpu_custom_call" | custom-call | tf_op jit(solution)/shard_map/route/pallas_call | solution.py:111
  22.3 7.6 %all-to-all-start = ((bf16[32,24,2048]{2,1,0:T(8,128)(2,1)}), bf16[32,24,2048]{2,1,0:T(8,128)(2,1)S(1)}, u32[]{:S(2)}, u32[]{:S(2)}) async-start(bf16[32,24,2048]{2,1,0:T(8,128)(2,1)} %bitcast.23), calls=%async_computation | async-start | bytes 6291456 | tf_op jit(solution)/shard_map/all_to_all | solution.py:517
  29.9 0.0 all-gather.2.cloned.1.call-start
  30.0 0.0 copy-start.9
  30.0 0.0 copy-start.10
  30.0 1.3 constant_dynamic-slice_fusion.2
  31.3 1.1 pad_maximum_fusion
  32.4 2.4 %collective-permute-start = (bf16[2,2048,128]{2,1,0:T(8,128)(2,1)}, bf16[2,2048,128]{2,1,0:T(8,128)(2,1)}, u32[]{:S(2)}, u32[]{:S(2)}) collective-permute-start(bf16[2,2048,128]{2,1,0:T(8,128)(2,1)} %pad_maximum_fusion), channel_id=1, source_target_pairs={{0,192},{32,224},{64,0},{96,32},{128,64},{160,96},{192,128},{224,1... | collective-permute-start | bytes 3145736 | tf_op jit(solution)/shard_map/ppermute | solution.py:500
  34.8 0.6 pad_maximum_fusion.1
  35.4 0.0 all-gather.2.cloned.1.call-update
  35.4 18.1 %collective-permute-done.1.refs_5_ = bf16[3,2048,128]{2,1,0:T(8,128)(2,1)} collective-permute-done((bf16[3,2048,128]{2,1,0:T(8,128)(2,1)}, bf16[3,2048,128]{2,1,0:T(8,128)(2,1)}, u32[]{:S(2)}, u32[]{:S(2)}) %collective-permute-start.1) | collective-permute-done | bytes 1572896 | tf_op jit(solution)/shard_map/ppermute | solution.py:500
  53.5 0.0 collective-permute-done.2.refs_6_
  53.5 1.9 pick.1
  55.4 11.8 %collective-permute-start.3 = (bf16[1,128,2048]{2,1,0:T(8,128)(2,1)}, bf16[1,128,2048]{2,1,0:T(8,128)(2,1)}, u32[]{:S(2)}, u32[]{:S(2)}) collective-permute-start(bf16[1,128,2048]{2,1,0:T(8,128)(2,1)} %pick.1), channel_id=1, source_target_pairs={{0,192},{32,224},{64,0},{96,32},{128,64},{160,96},{192,128},{224,1... | collective-permute-start | bytes 1572872 | tf_op jit(solution)/shard_map/ppermute | solution.py:500
  67.2 3.4 %all-to-all-done = bf16[32,24,2048]{2,1,0:T(8,128)(2,1)S(1)} async-done(((bf16[32,24,2048]{2,1,0:T(8,128)(2,1)}), bf16[32,24,2048]{2,1,0:T(8,128)(2,1)S(1)}, u32[]{:S(2)}, u32[]{:S(2)}) %all-to-all-start) | async-done | bytes 3145760 | tf_op jit(solution)/shard_map/all_to_all | solution.py:517
  70.6 1.7 copy-done.1
  72.4 11.8 %expert_near.1.near_ref = bf16[768,1152]{1,0:T(8,128)(2,1)} custom-call(s32[1]{0:T(128)} %bitcast.1.refs_0_, bf16[768,2048]{1,0:T(8,128)(2,1)} %bitcast.15, bf16[4,2048,128]{2,1,0:T(8,128)(2,1)} %refs_2_.3, bf16[4,2048,128]{2,1,0:T(8,128)(2,1)} %refs_3_.5, bf16[4,128,2048]{2,1,0:T(8,128)(2,1)} %refs_4_.5, ...), custom_call_target="tpu_custom_call" | custom-call | tf_op jit(solution)/shard_map/expert_near/pallas_call | solution.py:233
  84.2 1.1 collective-permute-done.3.down_ref
  85.3 6.3 %expert_far.1 = bf16[768,1152]{1,0:T(8,128)(2,1)} custom-call(bf16[768,2048]{1,0:T(8,128)(2,1)} %bitcast.16, bf16[2,2048,128]{2,1,0:T(8,128)(2,1)} %collective-permute-done.in_ref, bf16[1,128,2048]{2,1,0:T(8,128)(2,1)} %collective-permute-done.3.down_ref, bf16[768,1152]{1,0:T(8,128)(2,1)} %expert_near.1.near_ref), custom_call_target="tpu_custom_call" | custom-call | tf_op jit(solution)/shard_map/expert_far/pallas_call | solution.py:266
  91.6 1.0 all-gather.2.cloned.1.call-done.refs_2_.kv_ref
  92.6 30.6 %all_to_all.30 = bf16[32,24,1152]{2,1,0:T(8,128)(2,1)} all-to-all(bf16[32,24,1152]{2,1,0:T(8,128)(2,1)} %bitcast.18), channel_id=1, replica_groups=mesh['expert'=8,'context'=32] {'context'}, dimensions={0} | all-to-all | bytes 3538944 | tf_op jit(solution)/shard_map/all_to_all | solution.py:523
  123.2 3.7 %gather_rows.1 = bf16[128,2176]{1,0:T(8,128)(2,1)} custom-call(s32[1]{0:T(128)} %bitcast.1.refs_0_, bf16[768,1152]{1,0:T(8,128)(2,1)} %bitcast.17, bf16[768,128]{1,0:T(8,128)(2,1)} %get-tuple-element.33.refs_2_, bf16[768,128]{1,0:T(8,128)(2,1)} %get-tuple-element.34.refs_3_, bf16[768,128]{1,0:T(8,128)(2,1)} %get-tuple-element.35.refs_4_, s32[8,128]{1,0:T(8,128)} %bitcast.29, ...), custom_call_target="tpu_custom_call" | custom-call | tf_op jit(solution)/shard_map/gather_rows/pallas_call | solution.py:305
  126.9 8.6 %all-to-all-start.2 = ((bf16[8,16,2176]{2,1,0:T(8,128)(2,1)}), bf16[8,16,2176]{2,1,0:T(8,128)(2,1)S(1)}, u32[]{:S(2)}, u32[]{:S(2)}) async-start(bf16[8,16,2176]{2,1,0:T(8,128)(2,1)} %bitcast.24), calls=%async_computation.2 | async-start | bytes 1114112 | tf_op jit(solution)/shard_map/all_to_all | solution.py:532
  135.4 0.3 collective-permute-start.4
  135.7 1.2 collective-permute-done.4.refs_1_.o_ref
  137.0 0.6 copy-done.7
  137.6 4.6 %attention_probs.1 = (bf16[2048,512]{1,0:T(8,128)(2,1)}, f32[136,512]{1,0:T(8,128)}) custom-call(bf16[128,256]{1,0:T(8,128)(2,1)} %q_ref, bf16[128,256]{1,0:T(8,128)(2,1)} %copy-done.7, bf16[2048,256]{1,0:T(8,128)(2,1)} %all-gather.2.cloned.1.call-done.refs_2_.kv_ref), custom_call_target="tpu_custom_call" | custom-call | tf_op jit(solution)/shard_map/attention_probs/pallas_call | solution.py:305
  142.2 0.2 collective-permute-start.5
  142.3 1.6 collective-permute-done.5.far_ref
  143.9 10.2 %all-to-all-done.2.in_ref = bf16[8,16,2176]{2,1,0:T(8,128)(2,1)S(1)} async-done(((bf16[8,16,2176]{2,1,0:T(8,128)(2,1)}), bf16[8,16,2176]{2,1,0:T(8,128)(2,1)S(1)}, u32[]{:S(2)}, u32[]{:S(2)}) %all-to-all-start.2) | async-done | bytes 557088 | tf_op jit(solution)/shard_map/all_to_all | solution.py:532
  154.1 0.1 finish_hidden.1
  154.2 21.0 %all_to_all.31 = bf16[8,16,2176]{2,1,0:T(8,128)(2,1)S(1)} all-to-all(bf16[8,16,2176]{2,1,0:T(8,128)(2,1)S(1)} %finish_hidden.1), channel_id=1, replica_groups=mesh['expert'=8,'context'=32] {'expert'}, dimensions={0} | all-to-all | bytes 1114112 | tf_op jit(solution)/shard_map/all_to_all | solution.py:539
  175.3 2.0 collective-permute-done.6.do_ref
  177.2 0.8 copy-done.4
  178.0 6.2 %attention_grads.1 = (f32[128,256]{1,0:T(8,128)}, f32[128,256]{1,0:T(8,128)}, bf16[2048,256]{1,0:T(8,128)(2,1)}) custom-call(bf16[128,2176]{1,0:T(8,128)(2,1)} %bitcast.20, bf16[128,2176]{1,0:T(8,128)(2,1)} %copy-done.4, bf16[256,2048]{1,0:T(8,128)(2,1)} %w_ref.3, bf16[128,256]{1,0:T(8,128)(2,1)} %q_ref, bf16[128,256]{1,0:T(8,128)(2,1)} %copy-done.7, ...), custom_call_target="tpu_custom_call" | custom-call | tf_op jit(solution)/shard_map/attention_grads/pallas_call | solution.py:451
  184.2 21.1 %all_to_all.32.in_ref = bf16[16,128,256]{2,1,0:T(8,128)(2,1)S(1)} all-to-all(bf16[16,128,256]{2,1,0:T(8,128)(2,1)} %bitcast.25), channel_id=1, replica_groups={{0,2,4,6,8,10,12,14,16,18,20,22,24,26,28,30},{1,3,5,7,9,11,13,15,17,19,..., dimensions={0} | all-to-all | bytes 2097152 | tf_op jit(solution)/shard_map/all_to_all | solution.py:546
  205.4 0.9 sum_chips.1
  206.3 3.5 %all-to-all-start.5 = ((bf16[8,128,256]{2,1,0:T(8,128)(2,1)}), bf16[8,128,256]{2,1,0:T(8,128)(2,1)S(1)}, u32[]{:S(2)}, u32[]{:S(2)}) async-start(bf16[8,128,256]{2,1,0:T(8,128)(2,1)} %sum_chips.1), calls=%async_computation.5 | async-start | bytes 1048576 | tf_op jit(solution)/shard_map/all_to_all | solution.py:550
  209.8 0.8 slice.8
  210.7 0.7 copy.17
  211.3 0.7 collective-permute-done.7
  212.0 0.7 add.43
  212.7 13.8 %all-to-all-done.5.in_ref = bf16[8,128,256]{2,1,0:T(8,128)(2,1)S(1)} async-done(((bf16[8,128,256]{2,1,0:T(8,128)(2,1)}), bf16[8,128,256]{2,1,0:T(8,128)(2,1)S(1)}, u32[]{:S(2)}, u32[]{:S(2)}) %all-to-all-start.5) | async-done | bytes 524320 | tf_op jit(solution)/shard_map/all_to_all | solution.py:550
  226.5 0.7 sum_heads.1
  (24 shorter events, 0.1 us)
Async XLA Ops:
  11.6 41.9 %collective-permute-start.1 = (bf16[3,2048,128]{2,1,0:T(8,128)(2,1)}, bf16[3,2048,128]{2,1,0:T(8,128)(2,1)}, u32[]{:S(2)}, u32[]{:S(2)}) collective-permute-start(bf16[3,2048,128]{2,1,0:T(8,128)(2,1)} %get-tuple-element.27), channel_id=1, source_target_pairs={{0,32},{32,64},{64,96},{96,128},{128,160},{160,192},{192,224},{224... | collective-permute-start | bytes 4718600 | tf_op jit(solution)/shard_map/ppermute | solution.py:500
  13.5 39.9 %collective-permute-start.2 = (bf16[3,2048,128]{2,1,0:T(8,128)(2,1)}, bf16[3,2048,128]{2,1,0:T(8,128)(2,1)}, u32[]{:S(2)}, u32[]{:S(2)}) collective-permute-start(bf16[3,2048,128]{2,1,0:T(8,128)(2,1)} %get-tuple-element.28), channel_id=1, source_target_pairs={{0,224},{32,0},{64,32},{96,64},{128,96},{160,128},{192,160},{224,1... | collective-permute-start | bytes 4718600 | tf_op jit(solution)/shard_map/ppermute | solution.py:500
  22.3 48.3 %all-to-all-start = ((bf16[32,24,2048]{2,1,0:T(8,128)(2,1)}), bf16[32,24,2048]{2,1,0:T(8,128)(2,1)S(1)}, u32[]{:S(2)}, u32[]{:S(2)}) async-start(bf16[32,24,2048]{2,1,0:T(8,128)(2,1)} %bitcast.23), calls=%async_computation | async-start | bytes 6291456 | tf_op jit(solution)/shard_map/all_to_all | solution.py:517
  29.9 62.7 %all-gather.2.cloned.1.call-start = ((), (), s32[]{:S(2)}) async-start(), calls=%async_computation.6 | async-start | bytes 1114112 | tf_op jit(solution)/shard_map/all_gather | solution.py:514
  30.0 4.8 %copy-start.9 = (bf16[128,256]{1,0:T(8,128)(2,1)S(1)}, bf16[128,256]{1,0:T(8,128)(2,1)}, u32[]{:S(2)}) copy-start(bf16[128,256]{1,0:T(8,128)(2,1)} %param.23) | copy-start | bytes 196612
  30.0 4.7 %copy-start.10 = (bf16[128,256]{1,0:T(8,128)(2,1)S(1)}, bf16[128,256]{1,0:T(8,128)(2,1)}, u32[]{:S(2)}) copy-start(bf16[128,256]{1,0:T(8,128)(2,1)} %param.22) | copy-start | bytes 196612
  32.4 51.8 %collective-permute-start = (bf16[2,2048,128]{2,1,0:T(8,128)(2,1)}, bf16[2,2048,128]{2,1,0:T(8,128)(2,1)}, u32[]{:S(2)}, u32[]{:S(2)}) collective-permute-start(bf16[2,2048,128]{2,1,0:T(8,128)(2,1)} %pad_maximum_fusion), channel_id=1, source_target_pairs={{0,192},{32,224},{64,0},{96,32},{128,64},{160,96},{192,128},{224,1... | collective-permute-start | bytes 3145736 | tf_op jit(solution)/shard_map/ppermute | solution.py:500
  55.4 29.9 %collective-permute-start.3 = (bf16[1,128,2048]{2,1,0:T(8,128)(2,1)}, bf16[1,128,2048]{2,1,0:T(8,128)(2,1)}, u32[]{:S(2)}, u32[]{:S(2)}) collective-permute-start(bf16[1,128,2048]{2,1,0:T(8,128)(2,1)} %pick.1), channel_id=1, source_target_pairs={{0,192},{32,224},{64,0},{96,32},{128,64},{160,96},{192,128},{224,1... | collective-permute-start | bytes 1572872 | tf_op jit(solution)/shard_map/ppermute | solution.py:500
  70.6 1.7 copy-start.1
  123.2 12.2 %copy-start.6 = (bf16[128,256]{1,0:T(8,128)(2,1)S(1)}, bf16[128,256]{1,0:T(8,128)(2,1)}, u32[]{:S(2)}) copy-start(bf16[128,256]{1,0:T(8,128)(2,1)} %q_ref) | copy-start | bytes 196612
  123.2 30.9 %copy-start = (bf16[128,2048]{1,0:T(8,128)(2,1)S(1)}, bf16[128,2048]{1,0:T(8,128)(2,1)}, u32[]{:S(2)}) copy-start(bf16[128,2048]{1,0:T(8,128)(2,1)} %up_ref.1) | copy-start | bytes 1572868
  126.9 27.3 %all-to-all-start.2 = ((bf16[8,16,2176]{2,1,0:T(8,128)(2,1)}), bf16[8,16,2176]{2,1,0:T(8,128)(2,1)S(1)}, u32[]{:S(2)}, u32[]{:S(2)}) async-start(bf16[8,16,2176]{2,1,0:T(8,128)(2,1)} %bitcast.24), calls=%async_computation.2 | async-start | bytes 1114112 | tf_op jit(solution)/shard_map/all_to_all | solution.py:532
  135.4 1.5 collective-permute-start.4
  137.0 0.6 copy-start.7
  142.2 1.8 collective-permute-start.5
  143.9 33.3 %copy-start.5 = (f32[136,512]{1,0:T(8,128)}, f32[136,512]{1,0:T(8,128)S(1)}, u32[]{:S(2)}) copy-start(f32[136,512]{1,0:T(8,128)S(1)} %collective-permute-done.5.far_ref) | copy-start | bytes 835588
  175.3 2.0 copy-start.2
  175.3 2.0 collective-permute-start.6
  177.2 0.8 copy-start.4
  184.2 25.6 %copy-start.3 = (bf16[8,16,2176]{2,1,0:T(8,128)(2,1)S(1)}, bf16[8,16,2176]{2,1,0:T(8,128)(2,1)}, u32[]{:S(2)}) copy-start(bf16[8,16,2176]{2,1,0:T(8,128)(2,1)} %copy-done.2) | copy-start | bytes 1671172
  205.4 5.3 %copy-start.11 = (f32[128,256]{1,0:T(8,128)S(1)}, f32[128,256]{1,0:T(8,128)}, u32[]{:S(2)}) copy-start(f32[128,256]{1,0:T(8,128)} %get-tuple-element.43) | copy-start | bytes 393220
  205.4 6.6 %copy-start.8 = (f32[128,256]{1,0:T(8,128)S(1)}, f32[128,256]{1,0:T(8,128)}, u32[]{:S(2)}) copy-start(f32[128,256]{1,0:T(8,128)} %get-tuple-element.42) | copy-start | bytes 393220
  206.3 20.2 %all-to-all-start.5 = ((bf16[8,128,256]{2,1,0:T(8,128)(2,1)}), bf16[8,128,256]{2,1,0:T(8,128)(2,1)S(1)}, u32[]{:S(2)}, u32[]{:S(2)}) async-start(bf16[8,128,256]{2,1,0:T(8,128)(2,1)} %sum_chips.1), calls=%async_computation.5 | async-start | bytes 1048576 | tf_op jit(solution)/shard_map/all_to_all | solution.py:550
  210.7 1.3 collective-permute-start.7
Sparse Core Ops, SparseCore 0:
  35.6 57.0 all-gather.1

commit v5 on v3

--- a/solution.py
+++ b/solution.py
@@ -19,10 +19,11 @@
 MB = 1 << 20
 NEAR_MIB = 60
 PACK_ROWS = 1024
+PICK_COST = 30000000000
 NEAR_TYPE = BF
 NEAR_ROWS = 384
 FAR_ROWS = 384
-GRADS_MIB = 62
+GRADS_MIB = 36
 FINISH_MIB = 32
 FAR_MIB = 60
 
@@ -61,7 +62,7 @@
 
 
 def route_kernel(rows, per, count, q_ref, ids_ref, rw_ref, hid_ref, up_ref, gain_ref,
-                 send_ref, s0_ref, sw0_ref, sw1_ref, m_ref, r_ref, w_ref, n_ref):
+                 send_ref, picks_ref, m_ref, r_ref, w_ref, n_ref):
     step = pl.program_id(0)
     tokens = ids_ref.shape[1]
 
@@ -96,16 +97,15 @@
     s0 = jnp.where(first, 1.0, 0.0).astype(BF)
     s1 = jnp.where(second, 1.0, 0.0).astype(BF)
     send_ref[...] = nn(jnp.concatenate([s0, s1], axis=1), n_ref[...]).astype(BF)
-    s0_ref[...] = s0
-    sw0_ref[...] = jnp.where(first, weight, 0.0).astype(BF)
-    sw1_ref[...] = jnp.where(second, weight, 0.0).astype(BF)
+    picks_ref[:, :128] = jnp.where(first, weight, 0.0).astype(BF)
+    picks_ref[:, 128:256] = jnp.where(second, weight, 0.0).astype(BF)
+    picks_ref[:, 256:] = s0
 
 
 def route(quarter, per, count, ids, weights, hidden, upstream, gain):
     tokens, width = hidden.shape
     rows = 256
     slots = count * PAIR
-    matrix = pl.BlockSpec((rows, tokens), lambda i, p: (i, 0))
     return pl.pallas_call(
         lambda *refs: route_kernel(rows, per, count, *refs),
         grid_spec=pltpu.PrefetchScalarGridSpec(
@@ -118,7 +118,10 @@
                 whole((tokens, width)),
                 whole((1, width)),
             ],
-            out_specs=[pl.BlockSpec((rows, width), lambda i, p: (i, 0)), matrix, matrix, matrix],
+            out_specs=[
+                pl.BlockSpec((rows, width), lambda i, p: (i, 0)),
+                pl.BlockSpec((rows, 3 * tokens), lambda i, p: (i, 0)),
+            ],
             scratch_shapes=[
                 pltpu.VMEM((128, tokens), BF),
                 pltpu.VMEM((128, tokens), BF),
@@ -126,8 +129,7 @@
                 pltpu.VMEM((2 * tokens, width), BF),
             ],
         ),
-        out_shape=[jax.ShapeDtypeStruct((slots, width), BF)]
-        + [jax.ShapeDtypeStruct((slots, tokens), BF)] * 3,
+        out_shape=[jax.ShapeDtypeStruct((slots, width), BF), jax.ShapeDtypeStruct((slots, 3 * tokens), BF)],
         compiler_params=params(),
         name="route",
     )(quarter, ids, weights, hidden, upstream, gain)
@@ -165,6 +167,27 @@
         compiler_params=params(),
         name="pack",
     )(which, *[w_gate, w_up, w_down] * count)
+
+
+def pick_kernel(q_ref, w_ref, out_ref):
+    out_ref[...] = w_ref[...]
+
+
+def pick(which, w):
+    _, unit, width = w.shape
+    return pl.pallas_call(
+        pick_kernel,
+        grid_spec=pltpu.PrefetchScalarGridSpec(
+            num_scalar_prefetch=1,
+            grid=(1,),
+            in_specs=[pl.BlockSpec((1, unit, width), lambda i, q: (q[0], 0, 0))],
+            out_specs=whole((1, unit, width)),
+        ),
+        out_shape=jax.ShapeDtypeStruct((1, unit, width), BF),
+        cost_estimate=pl.CostEstimate(flops=PICK_COST, bytes_accessed=2 * unit * width * 2, transcendentals=0),
+        compiler_params=params(),
+        name="pick",
+    )(which, w)
 
 
 def unpack(ref):
@@ -228,15 +251,14 @@
     )(quarter, xy, w_gate, w_up, w_down, got_a, got_b)
 
 
-def far_kernel(xy_ref, far_ref, near_ref, out_ref):
+def far_kernel(xy_ref, in_ref, down_ref, near_ref, out_ref):
     width = xy_ref.shape[1]
-    w_gate, w_up, w_down = unpack(far_ref)
-    out, d_route = expert_rows(xy_ref[...], jnp.concatenate([w_gate, w_up], axis=1), w_down)
+    out, d_route = expert_rows(xy_ref[...], jnp.concatenate([in_ref[0], in_ref[1]], axis=1), down_ref[0])
     out_ref[:, : width // 2] = (near_ref[:, : width // 2] + out).astype(BF)
     out_ref[:, width // 2 :] = (near_ref[:, width // 2 :] + d_route).astype(BF)
 
 
-def expert_far(xy, got, near):
+def expert_far(xy, w_in, w_down, near):
     slots, width = xy.shape
     narrow = near.shape[1]
     rows = FAR_ROWS
@@ -244,21 +266,22 @@
     return pl.pallas_call(
         far_kernel,
         grid=(slots // rows,),
-        in_specs=[pl.BlockSpec((rows, width), lambda i: (i, 0)), whole(got.shape), block],
+        in_specs=[pl.BlockSpec((rows, width), lambda i: (i, 0)), whole(w_in.shape), whole(w_down.shape), block],
         out_specs=block,
         out_shape=jax.ShapeDtypeStruct((slots, narrow), BF),
         compiler_params=params(FAR_MIB),
         name="expert_far",
-    )(xy, got, near)
-
-
-def gather_kernel(per, count, q_ref, back_ref, s0_ref, sw0_ref, sw1_ref, ids_ref, hid_ref, gain_ref, out_ref):
+    )(xy, w_in, w_down, near)
+
+
+def gather_kernel(per, count, q_ref, back_ref, picks_ref, ids_ref, hid_ref, gain_ref, out_ref):
     tokens, width = hid_ref.shape
     half_width = width // 2
     wide = hid_ref[...].astype(F32)
     inv = lax.rsqrt(jnp.mean(wide * wide, axis=1, keepdims=True) + EPS)
     rows = back_ref[:, :half_width]
-    d_normed = jnp.concatenate([tn(sw0_ref[...], rows), tn(sw1_ref[...], rows)], axis=1)
+    halves = tn(picks_ref[:, : 2 * tokens], rows)
+    d_normed = jnp.concatenate([halves[:tokens], halves[tokens:]], axis=1)
     g = d_normed * gain_ref[...]
     inner = jnp.mean(g * wide, axis=1, keepdims=True)
     out_ref[:, :width] = (inv * g - wide * (inv * inv * inv * inner)).astype(BF)
@@ -266,7 +289,7 @@
     lane_of, _, _ = slot_split((slots, 128), 0, 0)
     lane = lax.broadcasted_iota(jnp.int32, (slots, 128), 1).astype(F32)
     placed = jnp.where(lane == lane_of, back_ref[:, half_width:].astype(F32), 0.0).astype(BF)
-    route = tn(placed, s0_ref[...])
+    route = tn(placed, picks_ref[:, 2 * tokens :])
     named = row_expert(q_ref[0], per, count, (128, tokens))
     ids = ids_ref[...]
     row = lax.broadcasted_iota(jnp.int32, (128, tokens), 0)
@@ -376,7 +399,7 @@
     return on_chip(
         lambda *refs: probs_kernel(512, *refs), "attention_probs",
         [jax.ShapeDtypeStruct((count, rows), BF), jax.ShapeDtypeStruct((HEAD_DIM + 8, rows), F32)],
-        [], [queries, other, kv], [pltpu.VMEM((count, rows), F32)])
+        [], [queries, other, kv], [pltpu.VMEM((count, rows), F32)], mib=60)
 
 
 def grads_kernel(chunk, dh_ref, do_ref, w_ref, q_ref, o_ref, p_ref, stat_ref, far_ref, kv_ref, dq_ref, dqo_ref, dkv_ref):
@@ -441,11 +464,13 @@
     def trade(w, step):
         return lax.ppermute(w, ("expert", "context"), moves(step))
 
-    leave = [((z + n) % per).astype(jnp.int32) for n in (1, per - 1, 2)]
-    packs = pack(jnp.stack(leave[:2]), w_gate, w_up, w_down) + pack(jnp.stack(leave[2:]), w_gate, w_up, w_down)
-    near_a, near_b = trade(packs[0], lambda core: 1), trade(packs[1], lambda core: -1)
-    distant, near_a, near_b = lax.optimization_barrier((packs[2], near_a, near_b))
-    got_far = trade(distant, far)
+    leave = jnp.stack([((z + n) % per).astype(jnp.int32) for n in (1, per - 1)])
+    near_a, near_b = pack(leave, w_gate, w_up, w_down)
+    near_a, near_b = trade(near_a, lambda core: 1), trade(near_b, lambda core: -1)
+    which = ((z + 2) % per).astype(jnp.int32)
+    far_in = trade(jnp.concatenate([lax.dynamic_slice_in_dim(w, which, 1, 0) for w in (w_gate, w_up)], axis=0), far)
+    which, near_a, near_b = lax.optimization_barrier((which, near_a, near_b))
+    far_down = trade(pick(which.reshape(1), w_down), far)
 
     ids = route_ids.T
     kv_head = z // (exp_count // 2)
@@ -453,19 +478,19 @@
         [lax.dynamic_slice_in_dim(a, kv_head * HEAD_DIM, HEAD_DIM, 1) for a in (keys, values)], axis=1)
     kv = lax.all_gather(own_kv, "context", axis=0, tiled=True, axis_index_groups=same_core)
 
-    send, s0, sw0, sw1 = route(q_arr, per, ctx_count, ids, route_weights.T, hidden, upstream, gain)
+    send, picks = route(q_arr, per, ctx_count, ids, route_weights.T, hidden, upstream, gain)
     xy = lax.all_to_all(send.reshape(ctx_count, PAIR, width), "context", 0, 0, tiled=True)
     xy = xy.reshape(slots, width)
     narrow = width // 2 + 128
     near = expert_near(q_arr, xy, w_gate, w_up, w_down, near_a, near_b)
-    rows = expert_far(xy, got_far, near)
+    rows = expert_far(xy, far_in, far_down, near)
     rows, kv = lax.optimization_barrier((rows, kv))
     rows = lax.all_to_all(rows.reshape(ctx_count, PAIR, narrow), "context", 0, 0, tiled=True)
     wide = width + 128
     q = on_chip(
         lambda *refs: gather_kernel(per, ctx_count, *refs), "gather_rows",
         jax.ShapeDtypeStruct((tokens, wide), BF),
-        [q_arr], [rows.reshape(slots, narrow), s0, sw0, sw1, ids, hidden, gain])
+        [q_arr], [rows.reshape(slots, narrow), picks, ids, hidden, gain], mib=36)
 
     share = tokens // exp_count
     parts = (exp_count, share, wide)

time: 239 us -> 230 us (0.962)
  waiting for transfers between devices: 70.3 us -> 52.2 us
  starting transfers between devices: 28.1 us -> 40.4 us
  Pallas kernels: 46 us -> 40.6 us
    all_to_all x1, waiting for transfers between devices: 15.6 us -> 3.47 us  [body(): lax.all_to_all(send.reshape(ctx_count, PAIR, width), 'context', 0, 0, til...]
    ppermute x3 -> x4, starting transfers between devices: 8.86 us -> 20.1 us  [trade(): return lax.ppermute(w, ('expert', 'context'), moves(step))]
    ppermute x3 -> x4, waiting for transfers between devices: 25.2 us -> 19.1 us  [trade(): return lax.ppermute(w, ('expert', 'context'), moves(step))]
    pallas_call x5, Pallas kernels: 16.9 us -> 12 us  [on_chip(): pl.pallas_call(kernel, in_specs=[pl.BlockSpec(memory_space=pltpu.SMEM)] *...]
    pallas_call x2 -> x1, Pallas kernels: 6.29 us -> 3.88 us  [pack(): pl.pallas_call(lambda *refs: pack_kernel(count, *refs), grid_spec=pltpu.P...]
  transfers between devices with their start and end apart: 11 -> 12, of which waited for: 9 -> 10; matrix products, arithmetic and copies ran while one was open for 1% -> 2% of each run, Pallas kernels for 12% -> 13%
where the time goes in v5:
time: 230 us; the launch traced here: 229 us
  blocking collectives  72.6 us (32%)
  waiting for transfers between devices  52.2 us (23%)
  Pallas kernels  40.6 us (18%)
  starting transfers between devices  40.4 us (18%)
  between operations  14.2 us (6%)
  local copies, waits for them, and re-layouts  5.96 us (3%)
  other arithmetic  2.99 us (1%)
    all_to_all x1, blocking collectives, body(): lax.all_to_all(rows.reshape(ctx_count, PAIR, narrow), 'context', 0, 0, ti...  30.8 us
    all_to_all x1, blocking collectives, body(): lax.all_to_all(done, 'expert', 0, 0, tiled=True).reshape(tokens, wide)  21.2 us
    all_to_all x1, blocking collectives, body(): lax.all_to_all(part.reshape(chips, tokens, 2 * HEAD_DIM), 'context', 0, 0...  20.7 us
    ppermute x4, starting transfers between devices, trade(): return lax.ppermute(w, ('expert', 'context'), moves(step))  20.1 us
    ppermute x4, waiting for transfers between devices, trade(): return lax.ppermute(w, ('expert', 'context'), moves(step))  19.1 us
    all_to_all x1, waiting for transfers between devices, body(): part = lax.all_to_all(part, 'expert', 0, 0, tiled=True)  13.7 us
    pallas_call x5, Pallas kernels, on_chip(): pl.pallas_call(kernel, in_specs=[pl.BlockSpec(memory_space=pltpu.SMEM)] *...  12 us
    pallas_call x1, Pallas kernels, expert_near(): pl.pallas_call(lambda *refs: near_kernel(rows, *refs), grid_spec=pltpu.Pr...  11.7 us
  transfers between devices with their start and end apart: 12, of which 10 were waited for; matrix products, arithmetic and copies ran while one was open for 2% of the time, Pallas kernels for 13%

profile of v5, /device:TPU:2, one launch (start us, length us, event | category | flops | bytes accessed | tf_op | source)
XLA Modules:
  0.0 229.0 jit_solution(11658722218996490283)
XLA Ops:
  7.2 0.6 pad_add_fusion.refs_0_
  7.8 3.9 %pack.1 = (bf16[3,2048,128]{2,1,0:T(8,128)(2,1)}, bf16[3,2048,128]{2,1,0:T(8,128)(2,1)}) custom-call(s32[2]{0:T(128)} %pad_add_fusion.refs_0_, bf16[4,2048,128]{2,1,0:T(8,128)(2,1)} %refs_2_.4, bf16[4,2048,128]{2,1,0:T(8,128)(2,1)} %refs_3_.5, bf16[4,128,2048]{2,1,0:T(8,128)(2,1)} %refs_4_.6, bf16[4,2048,128]{2,1,0:T(8,128)(2,1)} %refs_2_.4, ...), custom_call_target="tpu_custom_call" | custom-call | tf_op jit(solution)/shard_map/pack/pallas_call | solution.py:158
  11.7 1.9 collective-permute-start.1
  13.6 4.0 %collective-permute-start.2 = (bf16[3,2048,128]{2,1,0:T(8,128)(2,1)}, bf16[3,2048,128]{2,1,0:T(8,128)(2,1)}, u32[]{:S(2)}, u32[]{:S(2)}) collective-permute-start(bf16[3,2048,128]{2,1,0:T(8,128)(2,1)} %get-tuple-element.26), channel_id=1, source_target_pairs={{0,224},{32,0},{64,32},{96,64},{128,96},{160,128},{192,160},{224,1... | collective-permute-start | bytes 4718600 | tf_op jit(solution)/shard_map/ppermute | solution.py:465
  17.6 4.8 %route.1 = (bf16[768,2048]{1,0:T(8,128)(2,1)}, bf16[768,384]{1,0:T(8,128)(2,1)}) custom-call(s32[1]{0:T(128)} %bitcast.1.refs_0_, s32[8,128]{1,0:T(8,128)} %bitcast.23, bf16[8,128]{1,0:T(8,128)(2,1)} %bitcast.29, bf16[128,2048]{1,0:T(8,128)(2,1)} %refs_4_.7, bf16[128,2048]{1,0:T(8,128)(2,1)} %up_ref.1, f32[1,2048]{1,0:T(1,128)} %bitcast.21), custom_call_target="tpu_custom_call" | custom-call | tf_op jit(solution)/shard_map/route/pallas_call | solution.py:109
  22.3 7.6 %all-to-all-start = ((bf16[32,24,2048]{2,1,0:T(8,128)(2,1)}), bf16[32,24,2048]{2,1,0:T(8,128)(2,1)S(1)}, u32[]{:S(2)}, u32[]{:S(2)}) async-start(bf16[32,24,2048]{2,1,0:T(8,128)(2,1)} %bitcast.28), calls=%async_computation | async-start | bytes 6291456 | tf_op jit(solution)/shard_map/all_to_all | solution.py:482
  30.0 0.0 all-gather.2.cloned.1.call-start
  30.0 0.0 copy-start.14
  30.1 0.0 copy-start.15
  30.1 1.3 constant_dynamic-slice_fusion.2
  31.4 1.1 pad_maximum_fusion
  32.5 2.4 %collective-permute-start = (bf16[2,2048,128]{2,1,0:T(8,128)(2,1)}, bf16[2,2048,128]{2,1,0:T(8,128)(2,1)}, u32[]{:S(2)}, u32[]{:S(2)}) collective-permute-start(bf16[2,2048,128]{2,1,0:T(8,128)(2,1)} %pad_maximum_fusion), channel_id=1, source_target_pairs={{0,192},{32,224},{64,0},{96,32},{128,64},{160,96},{192,128},{224,1... | collective-permute-start | bytes 3145736 | tf_op jit(solution)/shard_map/ppermute | solution.py:465
  34.8 0.6 pad_maximum_fusion.1
  35.5 0.0 all-gather.2.cloned.1.call-update
  35.5 18.0 %collective-permute-done.1.refs_5_ = bf16[3,2048,128]{2,1,0:T(8,128)(2,1)} collective-permute-done((bf16[3,2048,128]{2,1,0:T(8,128)(2,1)}, bf16[3,2048,128]{2,1,0:T(8,128)(2,1)}, u32[]{:S(2)}, u32[]{:S(2)}) %collective-permute-start.1) | collective-permute-done | bytes 1572896 | tf_op jit(solution)/shard_map/ppermute | solution.py:465
  53.5 1.9 pick.1
  55.4 11.8 %collective-permute-start.3 = (bf16[1,128,2048]{2,1,0:T(8,128)(2,1)}, bf16[1,128,2048]{2,1,0:T(8,128)(2,1)}, u32[]{:S(2)}, u32[]{:S(2)}) collective-permute-start(bf16[1,128,2048]{2,1,0:T(8,128)(2,1)} %pick.1), channel_id=1, source_target_pairs={{0,192},{32,224},{64,0},{96,32},{128,64},{160,96},{192,128},{224,1... | collective-permute-start | bytes 1572872 | tf_op jit(solution)/shard_map/ppermute | solution.py:465
  67.2 3.5 %all-to-all-done = bf16[32,24,2048]{2,1,0:T(8,128)(2,1)S(1)} async-done(((bf16[32,24,2048]{2,1,0:T(8,128)(2,1)}), bf16[32,24,2048]{2,1,0:T(8,128)(2,1)S(1)}, u32[]{:S(2)}, u32[]{:S(2)}) %all-to-all-start) | async-done | bytes 3145760 | tf_op jit(solution)/shard_map/all_to_all | solution.py:482
  70.7 1.8 copy-done.13
  72.4 11.7 %expert_near.1.near_ref = bf16[768,1152]{1,0:T(8,128)(2,1)} custom-call(s32[1]{0:T(128)} %bitcast.1.refs_0_, bf16[768,2048]{1,0:T(8,128)(2,1)} %bitcast.25, bf16[4,2048,128]{2,1,0:T(8,128)(2,1)} %refs_2_.4, bf16[4,2048,128]{2,1,0:T(8,128)(2,1)} %refs_3_.5, bf16[4,128,2048]{2,1,0:T(8,128)(2,1)} %refs_4_.6, ...), custom_call_target="tpu_custom_call" | custom-call | tf_op jit(solution)/shard_map/expert_near/pallas_call | solution.py:233
  84.2 1.1 collective-permute-done.3.down_ref
  85.3 6.3 %expert_far.1 = bf16[768,1152]{1,0:T(8,128)(2,1)} custom-call(bf16[768,2048]{1,0:T(8,128)(2,1)} %bitcast.26, bf16[2,2048,128]{2,1,0:T(8,128)(2,1)} %collective-permute-done.in_ref, bf16[1,128,2048]{2,1,0:T(8,128)(2,1)} %collective-permute-done.3.down_ref, bf16[768,1152]{1,0:T(8,128)(2,1)} %expert_near.1.near_ref), custom_call_target="tpu_custom_call" | custom-call | tf_op jit(solution)/shard_map/expert_far/pallas_call | solution.py:266
  91.6 0.0 copy-start.12
  91.6 0.9 all-gather.2.cloned.1.call-done.refs_2_.refs_8_
  92.5 30.8 %all_to_all.30 = bf16[32,24,1152]{2,1,0:T(8,128)(2,1)S(1)} all-to-all(bf16[32,24,1152]{2,1,0:T(8,128)(2,1)} %bitcast.27), channel_id=1, replica_groups=mesh['expert'=8,'context'=32] {'context'}, dimensions={0} | all-to-all | bytes 3538944 | tf_op jit(solution)/shard_map/all_to_all | solution.py:488
  123.3 1.7 gather_rows.1
  125.0 8.7 %all-to-all-start.2 = ((bf16[8,16,2176]{2,1,0:T(8,128)(2,1)}), bf16[8,16,2176]{2,1,0:T(8,128)(2,1)S(1)}, u32[]{:S(2)}, u32[]{:S(2)}) async-start(bf16[8,16,2176]{2,1,0:T(8,128)(2,1)} %bitcast.12), calls=%async_computation.2 | async-start | bytes 1114112 | tf_op jit(solution)/shard_map/all_to_all | solution.py:497
  133.7 0.3 collective-permute-start.4
  134.0 1.4 collective-permute-done.4.refs_1_.refs_4_
  135.4 0.6 copy-done.9
  136.1 4.6 %attention_probs.1 = (bf16[2048,512]{1,0:T(8,128)(2,1)}, f32[136,512]{1,0:T(8,128)}) custom-call(bf16[128,256]{1,0:T(8,128)(2,1)} %refs_3_.6, bf16[128,256]{1,0:T(8,128)(2,1)} %copy-done.9, bf16[2048,256]{1,0:T(8,128)(2,1)} %all-gather.2.cloned.1.call-done.refs_2_.refs_8_), custom_call_target="tpu_custom_call" | custom-call | tf_op jit(solution)/shard_map/attention_probs/pallas_call | solution.py:306
  140.6 0.2 collective-permute-start.5
  140.8 1.6 collective-permute-done.5.refs_7_
  142.4 0.7 copy-done.7
  143.1 9.3 %all-to-all-done.2.in_ref = bf16[8,16,2176]{2,1,0:T(8,128)(2,1)S(1)} async-done(((bf16[8,16,2176]{2,1,0:T(8,128)(2,1)}), bf16[8,16,2176]{2,1,0:T(8,128)(2,1)S(1)}, u32[]{:S(2)}, u32[]{:S(2)}) %all-to-all-start.2) | async-done | bytes 557088 | tf_op jit(solution)/shard_map/all_to_all | solution.py:497
  152.4 0.1 finish_hidden.1
  152.5 21.2 %all_to_all.31 = bf16[8,16,2176]{2,1,0:T(8,128)(2,1)S(1)} all-to-all(bf16[8,16,2176]{2,1,0:T(8,128)(2,1)S(1)} %finish_hidden.1), channel_id=1, replica_groups=mesh['expert'=8,'context'=32] {'expert'}, dimensions={0} | all-to-all | bytes 1114112 | tf_op jit(solution)/shard_map/all_to_all | solution.py:504
  173.7 2.0 collective-permute-done.6.refs_1_
  175.6 4.0 %attention_grads.1 = (f32[128,256]{1,0:T(8,128)S(1)}, f32[128,256]{1,0:T(8,128)S(1)}, bf16[2048,256]{1,0:T(8,128)(2,1)S(1)}) custom-call(bf16[128,2176]{1,0:T(8,128)(2,1)S(1)} %bitcast.17, bf16[128,2176]{1,0:T(8,128)(2,1)S(1)} %collective-permute-done.6.refs_1_, bf16[256,2048]{1,0:T(8,128)(2,1)S(1)} %copy-done.4, bf16[128,256]{1,0:T(8,128)(2,1)} %refs_3_.6, ...), custom_call_target="tpu_custom_call" | custom-call | tf_op jit(solution)/shard_map/attention_grads/pallas_call | solution.py:306
  179.7 20.7 %all_to_all.32.in_ref = bf16[16,128,256]{2,1,0:T(8,128)(2,1)S(1)} all-to-all(bf16[16,128,256]{2,1,0:T(8,128)(2,1)S(1)} %bitcast.20), channel_id=1, replica_groups={{0,2,4,6,8,10,12,14,16,18,20,22,24,26,28,30},{1,3,5,7,9,11,13,15,17,19,..., dimensions={0} | all-to-all | bytes 2097152 | tf_op jit(solution)/shard_map/all_to_all | solution.py:518
  200.4 0.9 sum_chips.1
  201.3 3.5 %all-to-all-start.5 = ((bf16[8,128,256]{2,1,0:T(8,128)(2,1)}), bf16[8,128,256]{2,1,0:T(8,128)(2,1)S(1)}, u32[]{:S(2)}, u32[]{:S(2)}) async-start(bf16[8,128,256]{2,1,0:T(8,128)(2,1)} %sum_chips.1), calls=%async_computation.5 | async-start | bytes 1048576 | tf_op jit(solution)/shard_map/all_to_all | solution.py:522
  204.8 0.8 slice.8
  205.7 0.7 copy.17
  206.3 0.7 collective-permute-done.7
  207.0 0.7 add.43
  207.7 13.7 %all-to-all-done.5.in_ref = bf16[8,128,256]{2,1,0:T(8,128)(2,1)S(1)} async-done(((bf16[8,128,256]{2,1,0:T(8,128)(2,1)}), bf16[8,128,256]{2,1,0:T(8,128)(2,1)S(1)}, u32[]{:S(2)}, u32[]{:S(2)}) %all-to-all-start.5) | async-done | bytes 524320 | tf_op jit(solution)/shard_map/all_to_all | solution.py:522
  221.4 0.7 sum_heads.1
  (32 shorter events, 0.1 us)
Async XLA Ops:
  11.7 41.9 %collective-permute-start.1 = (bf16[3,2048,128]{2,1,0:T(8,128)(2,1)}, bf16[3,2048,128]{2,1,0:T(8,128)(2,1)}, u32[]{:S(2)}, u32[]{:S(2)}) collective-permute-start(bf16[3,2048,128]{2,1,0:T(8,128)(2,1)} %get-tuple-element.25), channel_id=1, source_target_pairs={{0,32},{32,64},{64,96},{96,128},{128,160},{160,192},{192,224},{224... | collective-permute-start | bytes 4718600 | tf_op jit(solution)/shard_map/ppermute | solution.py:465
  13.6 39.9 %collective-permute-start.2 = (bf16[3,2048,128]{2,1,0:T(8,128)(2,1)}, bf16[3,2048,128]{2,1,0:T(8,128)(2,1)}, u32[]{:S(2)}, u32[]{:S(2)}) collective-permute-start(bf16[3,2048,128]{2,1,0:T(8,128)(2,1)} %get-tuple-element.26), channel_id=1, source_target_pairs={{0,224},{32,0},{64,32},{96,64},{128,96},{160,128},{192,160},{224,1... | collective-permute-start | bytes 4718600 | tf_op jit(solution)/shard_map/ppermute | solution.py:465
  22.3 48.3 %all-to-all-start = ((bf16[32,24,2048]{2,1,0:T(8,128)(2,1)}), bf16[32,24,2048]{2,1,0:T(8,128)(2,1)S(1)}, u32[]{:S(2)}, u32[]{:S(2)}) async-start(bf16[32,24,2048]{2,1,0:T(8,128)(2,1)} %bitcast.28), calls=%async_computation | async-start | bytes 6291456 | tf_op jit(solution)/shard_map/all_to_all | solution.py:482
  30.0 62.6 %all-gather.2.cloned.1.call-start = ((), (), s32[]{:S(2)}) async-start(), calls=%async_computation.6 | async-start | bytes 1114112 | tf_op jit(solution)/shard_map/all_gather | solution.py:479
  30.0 4.8 %copy-start.14 = (bf16[128,256]{1,0:T(8,128)(2,1)S(1)}, bf16[128,256]{1,0:T(8,128)(2,1)}, u32[]{:S(2)}) copy-start(bf16[128,256]{1,0:T(8,128)(2,1)} %param.23) | copy-start | bytes 196612
  30.1 4.8 %copy-start.15 = (bf16[128,256]{1,0:T(8,128)(2,1)S(1)}, bf16[128,256]{1,0:T(8,128)(2,1)}, u32[]{:S(2)}) copy-start(bf16[128,256]{1,0:T(8,128)(2,1)} %param.22) | copy-start | bytes 196612
  32.5 51.7 %collective-permute-start = (bf16[2,2048,128]{2,1,0:T(8,128)(2,1)}, bf16[2,2048,128]{2,1,0:T(8,128)(2,1)}, u32[]{:S(2)}, u32[]{:S(2)}) collective-permute-start(bf16[2,2048,128]{2,1,0:T(8,128)(2,1)} %pad_maximum_fusion), channel_id=1, source_target_pairs={{0,192},{32,224},{64,0},{96,32},{128,64},{160,96},{192,128},{224,1... | collective-permute-start | bytes 3145736 | tf_op jit(solution)/shard_map/ppermute | solution.py:465
  55.4 29.9 %collective-permute-start.3 = (bf16[1,128,2048]{2,1,0:T(8,128)(2,1)}, bf16[1,128,2048]{2,1,0:T(8,128)(2,1)}, u32[]{:S(2)}, u32[]{:S(2)}) collective-permute-start(bf16[1,128,2048]{2,1,0:T(8,128)(2,1)} %pick.1), channel_id=1, source_target_pairs={{0,192},{32,224},{64,0},{96,32},{128,64},{160,96},{192,128},{224,1... | collective-permute-start | bytes 1572872 | tf_op jit(solution)/shard_map/ppermute | solution.py:465
  70.7 1.8 copy-start.13
  91.6 31.7 %copy-start.3 = (bf16[128,2048]{1,0:T(8,128)(2,1)S(1)}, bf16[128,2048]{1,0:T(8,128)(2,1)}, u32[]{:S(2)}) copy-start(bf16[128,2048]{1,0:T(8,128)(2,1)} %refs_4_.7) | copy-start | bytes 1572868
  91.6 31.7 %copy-start.5 = (bf16[768,384]{1,0:T(8,128)(2,1)S(1)}, bf16[768,384]{1,0:T(8,128)(2,1)}, u32[]{:S(2)}) copy-start(bf16[768,384]{1,0:T(8,128)(2,1)} %get-tuple-element.31.refs_2_) | copy-start | bytes 1769476
  91.6 31.7 %copy-start.11 = (f32[2048]{0:T(1024)S(1)}, f32[2048]{0:T(1024)}, u32[]{:S(2)}) copy-start(f32[2048]{0:T(1024)} %param.14) | copy-start | bytes 24580
  91.6 31.7 %copy-start.12 = (s32[128,8]{0,1:T(8,128)S(1)}, s32[128,8]{0,1:T(8,128)}, u32[]{:S(2)}) copy-start(s32[128,8]{0,1:T(8,128)} %param.15) | copy-start | bytes 12292
  123.3 29.1 %copy-start.2 = (bf16[128,2048]{1,0:T(8,128)(2,1)S(1)}, bf16[128,2048]{1,0:T(8,128)(2,1)}, u32[]{:S(2)}) copy-start(bf16[128,2048]{1,0:T(8,128)(2,1)} %up_ref.1) | copy-start | bytes 1572868
  125.0 50.6 %copy-start.4 = (bf16[256,2048]{1,0:T(8,128)(2,1)S(1)}, bf16[256,2048]{1,0:T(8,128)(2,1)}, u32[]{:S(2)}) copy-start(bf16[256,2048]{1,0:T(8,128)(2,1)} %refs_2_.5) | copy-start | bytes 3145732
  125.0 27.4 %all-to-all-start.2 = ((bf16[8,16,2176]{2,1,0:T(8,128)(2,1)}), bf16[8,16,2176]{2,1,0:T(8,128)(2,1)S(1)}, u32[]{:S(2)}, u32[]{:S(2)}) async-start(bf16[8,16,2176]{2,1,0:T(8,128)(2,1)} %bitcast.12), calls=%async_computation.2 | async-start | bytes 1114112 | tf_op jit(solution)/shard_map/all_to_all | solution.py:497
  133.7 41.9 %copy-start = (bf16[2048,256]{1,0:T(8,128)(2,1)S(1)}, bf16[2048,256]{1,0:T(8,128)(2,1)}, u32[]{:S(2)}) copy-start(bf16[2048,256]{1,0:T(8,128)(2,1)} %all-gather.2.cloned.1.call-done.refs_2_.refs_8_) | copy-start | bytes 3145732
  133.7 1.7 collective-permute-start.4
  135.4 0.6 copy-start.9
  140.6 35.0 %copy-start.6 = (f32[136,512]{1,0:T(8,128)S(1)}, f32[136,512]{1,0:T(8,128)}, u32[]{:S(2)}) copy-start(f32[136,512]{1,0:T(8,128)} %get-tuple-element.34.refs_6_) | copy-start | bytes 835588
  140.6 35.0 %copy-start.10 = (bf16[128,256]{1,0:T(8,128)(2,1)S(1)}, bf16[128,256]{1,0:T(8,128)(2,1)}, u32[]{:S(2)}) copy-start(bf16[128,256]{1,0:T(8,128)(2,1)} %copy-done.9) | copy-start | bytes 196612
  140.6 1.8 collective-permute-start.5
  142.4 0.7 copy-start.7
  152.4 23.2 %copy-start.1 = (bf16[2048,512]{1,0:T(8,128)(2,1)S(1)}, bf16[2048,512]{1,0:T(8,128)(2,1)}, u32[]{:S(2)}) copy-start(bf16[2048,512]{1,0:T(8,128)(2,1)} %get-tuple-element.36.refs_5_) | copy-start | bytes 6291460
  152.4 23.3 %copy-start.8 = (f32[136,512]{1,0:T(8,128)S(1)}, f32[136,512]{1,0:T(8,128)}, u32[]{:S(2)}) copy-start(f32[136,512]{1,0:T(8,128)} %copy-done.7) | copy-start | bytes 835588
  173.7 2.0 collective-permute-start.6
  201.3 20.1 %all-to-all-start.5 = ((bf16[8,128,256]{2,1,0:T(8,128)(2,1)}), bf16[8,128,256]{2,1,0:T(8,128)(2,1)S(1)}, u32[]{:S(2)}, u32[]{:S(2)}) async-start(bf16[8,128,256]{2,1,0:T(8,128)(2,1)} %sum_chips.1), calls=%async_computation.5 | async-start | bytes 1048576 | tf_op jit(solution)/shard_map/all_to_all | solution.py:522
  205.7 1.3 collective-permute-start.7
Sparse Core Ops, SparseCore 0:
  35.6 56.8 all-gather.1

commit v6 on v5

--- a/solution.py
+++ b/solution.py
@@ -224,7 +224,7 @@
     out_ref[:, width // 2 :] = d_route.astype(NEAR_TYPE)
 
 
-def expert_near(quarter, xy, w_gate, w_up, w_down, got_a, got_b):
+def expert_near(quarter, xy, w_gate, w_up, own_down, got_a, got_b):
     slots, width = xy.shape
     unit = w_gate.shape[2]
     rows = NEAR_ROWS
@@ -239,7 +239,7 @@
                 pl.BlockSpec((rows, width), lambda i, p: (i, 0)),
                 own,
                 own,
-                pl.BlockSpec((1, unit, width), lambda i, p: (p[0], 0, 0)),
+                whole((1, unit, width)),
                 whole(got_a.shape),
                 whole(got_b.shape),
             ],
@@ -248,7 +248,7 @@
         out_shape=jax.ShapeDtypeStruct((slots, narrow), NEAR_TYPE),
         compiler_params=params(NEAR_MIB),
         name="expert_near",
-    )(quarter, xy, w_gate, w_up, w_down, got_a, got_b)
+    )(quarter, xy, w_gate, w_up, own_down, got_a, got_b)
 
 
 def far_kernel(xy_ref, in_ref, down_ref, near_ref, out_ref):
@@ -467,10 +467,11 @@
     leave = jnp.stack([((z + n) % per).astype(jnp.int32) for n in (1, per - 1)])
     near_a, near_b = pack(leave, w_gate, w_up, w_down)
     near_a, near_b = trade(near_a, lambda core: 1), trade(near_b, lambda core: -1)
-    which = ((z + 2) % per).astype(jnp.int32)
-    far_in = trade(jnp.concatenate([lax.dynamic_slice_in_dim(w, which, 1, 0) for w in (w_gate, w_up)], axis=0), far)
-    which, near_a, near_b = lax.optimization_barrier((which, near_a, near_b))
-    far_down = trade(pick(which.reshape(1), w_down), far)
+    far_gate, far_up, far_down = [lax.dynamic_slice_in_dim(w, (z + 2) % per, 1, 0) for w in (w_gate, w_up, w_down)]
+    far_in = trade(jnp.concatenate([far_gate, far_up], axis=0), far)
+    far_down = trade(far_down, far)
+    mine, near_a, near_b = lax.optimization_barrier((q_arr, near_a, near_b))
+    own_down = pick(mine, w_down)
 
     ids = route_ids.T
     kv_head = z // (exp_count // 2)
@@ -482,7 +483,7 @@
     xy = lax.all_to_all(send.reshape(ctx_count, PAIR, width), "context", 0, 0, tiled=True)
     xy = xy.reshape(slots, width)
     narrow = width // 2 + 128
-    near = expert_near(q_arr, xy, w_gate, w_up, w_down, near_a, near_b)
+    near = expert_near(q_arr, xy, w_gate, w_up, own_down, near_a, near_b)
     rows = expert_far(xy, far_in, far_down, near)
     rows, kv = lax.optimization_barrier((rows, kv))
     rows = lax.all_to_all(rows.reshape(ctx_count, PAIR, narrow), "context", 0, 0, tiled=True)

time: 230 us -> 229 us (level)
  starting transfers between devices: 40.4 us -> 29.7 us
  waiting for transfers between devices: 52.2 us -> 61.3 us
    all_to_all x1, waiting for transfers between devices: 3.47 us -> 14.9 us  [body(): lax.all_to_all(send.reshape(ctx_count, PAIR, width), 'context', 0, 0, til...]
    ppermute x4, starting transfers between devices: 20.1 us -> 11 us  [trade(): return lax.ppermute(w, ('expert', 'context'), moves(step))]
    ppermute x4, waiting for transfers between devices: 19.1 us -> 15.1 us  [trade(): return lax.ppermute(w, ('expert', 'context'), moves(step))]
  transfers between devices with their start and end apart: 12 -> 12, of which waited for: 10 -> 10; matrix products, arithmetic and copies ran while one was open for 2% -> 3% of each run, Pallas kernels for 13% -> 13%
where the time goes in v6:
time: 229 us; the launch traced here: 228 us
  blocking collectives  71.5 us (31%)
  waiting for transfers between devices  61.3 us (27%)
  Pallas kernels  40.7 us (18%)
  starting transfers between devices  29.7 us (13%)
  between operations  14.2 us (6%)
  local copies, waits for them, and re-layouts  7.68 us (3%)
  other arithmetic  3.03 us (1%)
    all_to_all x1, blocking collectives, body(): lax.all_to_all(rows.reshape(ctx_count, PAIR, narrow), 'context', 0, 0, ti...  29.7 us
    all_to_all x1, blocking collectives, body(): lax.all_to_all(done, 'expert', 0, 0, tiled=True).reshape(tokens, wide)  21.2 us
    all_to_all x1, blocking collectives, body(): lax.all_to_all(part.reshape(chips, tokens, 2 * HEAD_DIM), 'context', 0, 0...  20.7 us
    ppermute x4, waiting for transfers between devices, trade(): return lax.ppermute(w, ('expert', 'context'), moves(step))  15.1 us
    all_to_all x1, waiting for transfers between devices, body(): lax.all_to_all(send.reshape(ctx_count, PAIR, width), 'context', 0, 0, til...  14.9 us
    all_to_all x1, waiting for transfers between devices, body(): part = lax.all_to_all(part, 'expert', 0, 0, tiled=True)  13.7 us
    pallas_call x5, Pallas kernels, on_chip(): pl.pallas_call(kernel, in_specs=[pl.BlockSpec(memory_space=pltpu.SMEM)] *...  12 us
    pallas_call x1, Pallas kernels, expert_near(): pl.pallas_call(lambda *refs: near_kernel(rows, *refs), grid_spec=pltpu.Pr...  11.7 us
  transfers between devices with their start and end apart: 12, of which 10 were waited for; matrix products, arithmetic and copies ran while one was open for 3% of the time, Pallas kernels for 13%

profile of v6, /device:TPU:2, one launch (start us, length us, event | category | flops | bytes accessed | tf_op | source)
XLA Modules:
  0.0 228.2 jit_solution(12898997785914614487)
XLA Ops:
  7.2 0.6 pad_add_fusion.refs_0_
  7.8 4.0 %pack.1 = (bf16[3,2048,128]{2,1,0:T(8,128)(2,1)}, bf16[3,2048,128]{2,1,0:T(8,128)(2,1)}) custom-call(s32[2]{0:T(128)} %pad_add_fusion.refs_0_, bf16[4,2048,128]{2,1,0:T(8,128)(2,1)} %refs_2_.4, bf16[4,2048,128]{2,1,0:T(8,128)(2,1)} %refs_3_.5, bf16[4,128,2048]{2,1,0:T(8,128)(2,1)} %w_ref.1, bf16[4,2048,128]{2,1,0:T(8,128)(2,1)} %refs_2_.4, ...), custom_call_target="tpu_custom_call" | custom-call | tf_op jit(solution)/shard_map/pack/pallas_call | solution.py:158
  11.8 1.9 collective-permute-start.2
  13.7 4.0 %collective-permute-start.3 = (bf16[3,2048,128]{2,1,0:T(8,128)(2,1)}, bf16[3,2048,128]{2,1,0:T(8,128)(2,1)}, u32[]{:S(2)}, u32[]{:S(2)}) collective-permute-start(bf16[3,2048,128]{2,1,0:T(8,128)(2,1)} %get-tuple-element.26), channel_id=1, source_target_pairs={{0,224},{32,0},{64,32},{96,64},{128,96},{160,128},{192,160},{224,1... | collective-permute-start | bytes 4718600 | tf_op jit(solution)/shard_map/ppermute | solution.py:465
  17.7 4.7 %route.1 = (bf16[768,2048]{1,0:T(8,128)(2,1)}, bf16[768,384]{1,0:T(8,128)(2,1)}) custom-call(s32[1]{0:T(128)} %bitcast.1.refs_0_.q_ref, s32[8,128]{1,0:T(8,128)} %bitcast.22, bf16[8,128]{1,0:T(8,128)(2,1)} %bitcast.28, bf16[128,2048]{1,0:T(8,128)(2,1)} %refs_4_.5, bf16[128,2048]{1,0:T(8,128)(2,1)} %up_ref.1, f32[1,2048]{1,0:T(1,128)} %bitcast.20), custom_call_target="tpu_custom_call" | custom-call | tf_op jit(solution)/shard_map/route/pallas_call | solution.py:109
  22.4 7.6 %all-to-all-start = ((bf16[32,24,2048]{2,1,0:T(8,128)(2,1)}), bf16[32,24,2048]{2,1,0:T(8,128)(2,1)S(1)}, u32[]{:S(2)}, u32[]{:S(2)}) async-start(bf16[32,24,2048]{2,1,0:T(8,128)(2,1)} %bitcast.27), calls=%async_computation | async-start | bytes 6291456 | tf_op jit(solution)/shard_map/all_to_all | solution.py:483
  30.0 0.0 all-gather.2.cloned.1.call-start
  30.1 1.3 constant_dynamic-slice_fusion.3
  31.3 0.0 copy-start.14
  31.3 0.0 copy-start.15
  31.4 1.1 pad_maximum_fusion
  32.5 2.4 %collective-permute-start = (bf16[2,2048,128]{2,1,0:T(8,128)(2,1)}, bf16[2,2048,128]{2,1,0:T(8,128)(2,1)}, u32[]{:S(2)}, u32[]{:S(2)}) collective-permute-start(bf16[2,2048,128]{2,1,0:T(8,128)(2,1)} %pad_maximum_fusion), channel_id=1, source_target_pairs={{0,192},{32,224},{64,0},{96,32},{128,64},{160,96},{192,128},{224,1... | collective-permute-start | bytes 3145736 | tf_op jit(solution)/shard_map/ppermute | solution.py:465
  34.9 1.9 constant_dynamic-slice_fusion.2
  36.8 2.6 %collective-permute-start.1 = (bf16[1,128,2048]{2,1,0:T(8,128)(2,1)}, bf16[1,128,2048]{2,1,0:T(8,128)(2,1)}, u32[]{:S(2)}, u32[]{:S(2)}) collective-permute-start(bf16[1,128,2048]{2,1,0:T(8,128)(2,1)} %constant_dynamic-slice_fusion.2), channel_id=1, source_target_pairs={{0,192},{32,224},{64,0},{96,32},{128,64},{160,96},{192,128},{224,1... | collective-permute-start | bytes 1572872 | tf_op jit(solution)/shard_map/ppermute | solution.py:465
  39.4 0.6 pad_maximum_fusion.1
  40.1 0.0 all-gather.2.cloned.1.call-update
  40.1 13.5 %collective-permute-done.2.refs_5_ = bf16[3,2048,128]{2,1,0:T(8,128)(2,1)} collective-permute-done((bf16[3,2048,128]{2,1,0:T(8,128)(2,1)}, bf16[3,2048,128]{2,1,0:T(8,128)(2,1)}, u32[]{:S(2)}, u32[]{:S(2)}) %collective-permute-start.2) | collective-permute-done | bytes 1572896 | tf_op jit(solution)/shard_map/ppermute | solution.py:465
  53.6 1.9 pick.1.refs_4_
  55.5 14.9 %all-to-all-done = bf16[32,24,2048]{2,1,0:T(8,128)(2,1)S(1)} async-done(((bf16[32,24,2048]{2,1,0:T(8,128)(2,1)}), bf16[32,24,2048]{2,1,0:T(8,128)(2,1)S(1)}, u32[]{:S(2)}, u32[]{:S(2)}) %all-to-all-start) | async-done | bytes 3145760 | tf_op jit(solution)/shard_map/all_to_all | solution.py:483
  70.4 1.6 copy-done.13
  72.1 11.7 %expert_near.1.near_ref = bf16[768,1152]{1,0:T(8,128)(2,1)} custom-call(s32[1]{0:T(128)} %bitcast.1.refs_0_.q_ref, bf16[768,2048]{1,0:T(8,128)(2,1)} %bitcast.24, bf16[4,2048,128]{2,1,0:T(8,128)(2,1)} %refs_2_.4, bf16[4,2048,128]{2,1,0:T(8,128)(2,1)} %refs_3_.5, bf16[1,128,2048]{2,1,0:T(8,128)(2,1)} %pick.1.refs_4_, ...), custom_call_target="tpu_custom_call" | custom-call | tf_op jit(solution)/shard_map/expert_near/pallas_call | solution.py:233
  83.8 1.6 collective-permute-done.1.down_ref
  85.4 6.4 %expert_far.1 = bf16[768,1152]{1,0:T(8,128)(2,1)} custom-call(bf16[768,2048]{1,0:T(8,128)(2,1)} %bitcast.25, bf16[2,2048,128]{2,1,0:T(8,128)(2,1)} %collective-permute-done.in_ref, bf16[1,128,2048]{2,1,0:T(8,128)(2,1)} %collective-permute-done.1.down_ref, bf16[768,1152]{1,0:T(8,128)(2,1)} %expert_near.1.near_ref), custom_call_target="tpu_custom_call" | custom-call | tf_op jit(solution)/shard_map/expert_far/pallas_call | solution.py:266
  91.8 2.6 %all-gather.2.cloned.1.call-done.refs_2_.refs_8_ = bf16[2048,256]{1,0:T(8,128)(2,1)} async-done(((bf16[128,256]{1,0:T(8,128)(2,1)}), bf16[2048,256]{1,0:T(8,128)(2,1)}) %all-gather.2.cloned.1.call-update) | async-done | bytes 1048592 | tf_op jit(solution)/shard_map/all_gather | solution.py:480
  94.3 29.7 %all_to_all.30 = bf16[32,24,1152]{2,1,0:T(8,128)(2,1)S(1)} all-to-all(bf16[32,24,1152]{2,1,0:T(8,128)(2,1)} %bitcast.26), channel_id=1, replica_groups=mesh['expert'=8,'context'=32] {'context'}, dimensions={0} | all-to-all | bytes 3538944 | tf_op jit(solution)/shard_map/all_to_all | solution.py:489
  124.1 1.7 gather_rows.1
  125.7 7.1 %all-to-all-start.2 = ((bf16[8,16,2176]{2,1,0:T(8,128)(2,1)}), bf16[8,16,2176]{2,1,0:T(8,128)(2,1)S(1)}, u32[]{:S(2)}, u32[]{:S(2)}) async-start(bf16[8,16,2176]{2,1,0:T(8,128)(2,1)} %bitcast.11), calls=%async_computation.2 | async-start | bytes 1114112 | tf_op jit(solution)/shard_map/all_to_all | solution.py:498
  132.9 0.3 collective-permute-start.4
  133.2 1.4 collective-permute-done.4.refs_1_.refs_4_
  134.6 0.6 copy-done.9
  135.3 4.6 %attention_probs.1 = (bf16[2048,512]{1,0:T(8,128)(2,1)}, f32[136,512]{1,0:T(8,128)}) custom-call(bf16[128,256]{1,0:T(8,128)(2,1)} %refs_3_.6, bf16[128,256]{1,0:T(8,128)(2,1)} %copy-done.9, bf16[2048,256]{1,0:T(8,128)(2,1)} %all-gather.2.cloned.1.call-done.refs_2_.refs_8_), custom_call_target="tpu_custom_call" | custom-call | tf_op jit(solution)/shard_map/attention_probs/pallas_call | solution.py:306
  139.8 0.2 collective-permute-start.5
  140.0 1.6 collective-permute-done.5.refs_7_
  141.6 0.7 copy-done.7
  142.3 9.3 %all-to-all-done.2.in_ref = bf16[8,16,2176]{2,1,0:T(8,128)(2,1)S(1)} async-done(((bf16[8,16,2176]{2,1,0:T(8,128)(2,1)}), bf16[8,16,2176]{2,1,0:T(8,128)(2,1)S(1)}, u32[]{:S(2)}, u32[]{:S(2)}) %all-to-all-start.2) | async-done | bytes 557088 | tf_op jit(solution)/shard_map/all_to_all | solution.py:498
  151.6 0.1 finish_hidden.1
  151.7 21.2 %all_to_all.31 = bf16[8,16,2176]{2,1,0:T(8,128)(2,1)S(1)} all-to-all(bf16[8,16,2176]{2,1,0:T(8,128)(2,1)S(1)} %finish_hidden.1), channel_id=1, replica_groups=mesh['expert'=8,'context'=32] {'expert'}, dimensions={0} | all-to-all | bytes 1114112 | tf_op jit(solution)/shard_map/all_to_all | solution.py:505
  172.9 2.0 collective-permute-done.6.refs_1_
  174.9 4.0 %attention_grads.1 = (f32[128,256]{1,0:T(8,128)S(1)}, f32[128,256]{1,0:T(8,128)S(1)}, bf16[2048,256]{1,0:T(8,128)(2,1)S(1)}) custom-call(bf16[128,2176]{1,0:T(8,128)(2,1)S(1)} %bitcast.16, bf16[128,2176]{1,0:T(8,128)(2,1)S(1)} %collective-permute-done.6.refs_1_, bf16[256,2048]{1,0:T(8,128)(2,1)S(1)} %copy-done.4, bf16[128,256]{1,0:T(8,128)(2,1)} %refs_3_.6, ...), custom_call_target="tpu_custom_call" | custom-call | tf_op jit(solution)/shard_map/attention_grads/pallas_call | solution.py:306
  178.9 20.7 %all_to_all.32.in_ref = bf16[16,128,256]{2,1,0:T(8,128)(2,1)S(1)} all-to-all(bf16[16,128,256]{2,1,0:T(8,128)(2,1)S(1)} %bitcast.19), channel_id=1, replica_groups={{0,2,4,6,8,10,12,14,16,18,20,22,24,26,28,30},{1,3,5,7,9,11,13,15,17,19,..., dimensions={0} | all-to-all | bytes 2097152 | tf_op jit(solution)/shard_map/all_to_all | solution.py:519
  199.6 0.9 sum_chips.1
  200.5 3.5 %all-to-all-start.5 = ((bf16[8,128,256]{2,1,0:T(8,128)(2,1)}), bf16[8,128,256]{2,1,0:T(8,128)(2,1)S(1)}, u32[]{:S(2)}, u32[]{:S(2)}) async-start(bf16[8,128,256]{2,1,0:T(8,128)(2,1)} %sum_chips.1), calls=%async_computation.5 | async-start | bytes 1048576 | tf_op jit(solution)/shard_map/all_to_all | solution.py:523
  204.0 0.8 slice.8
  204.9 0.7 copy.17
  205.5 0.7 collective-permute-done.7
  206.2 0.7 add.48
  206.9 13.7 %all-to-all-done.5.in_ref = bf16[8,128,256]{2,1,0:T(8,128)(2,1)S(1)} async-done(((bf16[8,128,256]{2,1,0:T(8,128)(2,1)}), bf16[8,128,256]{2,1,0:T(8,128)(2,1)S(1)}, u32[]{:S(2)}, u32[]{:S(2)}) %all-to-all-start.5) | async-done | bytes 524320 | tf_op jit(solution)/shard_map/all_to_all | solution.py:523
  220.6 0.7 sum_heads.1
  (33 shorter events, 0.1 us)
Async XLA Ops:
  11.8 41.9 %collective-permute-start.2 = (bf16[3,2048,128]{2,1,0:T(8,128)(2,1)}, bf16[3,2048,128]{2,1,0:T(8,128)(2,1)}, u32[]{:S(2)}, u32[]{:S(2)}) collective-permute-start(bf16[3,2048,128]{2,1,0:T(8,128)(2,1)} %get-tuple-element.25), channel_id=1, source_target_pairs={{0,32},{32,64},{64,96},{96,128},{128,160},{160,192},{192,224},{224... | collective-permute-start | bytes 4718600 | tf_op jit(solution)/shard_map/ppermute | solution.py:465
  13.7 39.9 %collective-permute-start.3 = (bf16[3,2048,128]{2,1,0:T(8,128)(2,1)}, bf16[3,2048,128]{2,1,0:T(8,128)(2,1)}, u32[]{:S(2)}, u32[]{:S(2)}) collective-permute-start(bf16[3,2048,128]{2,1,0:T(8,128)(2,1)} %get-tuple-element.26), channel_id=1, source_target_pairs={{0,224},{32,0},{64,32},{96,64},{128,96},{160,128},{192,160},{224,1... | collective-permute-start | bytes 4718600 | tf_op jit(solution)/shard_map/ppermute | solution.py:465
  22.4 48.1 %all-to-all-start = ((bf16[32,24,2048]{2,1,0:T(8,128)(2,1)}), bf16[32,24,2048]{2,1,0:T(8,128)(2,1)S(1)}, u32[]{:S(2)}, u32[]{:S(2)}) async-start(bf16[32,24,2048]{2,1,0:T(8,128)(2,1)} %bitcast.27), calls=%async_computation | async-start | bytes 6291456 | tf_op jit(solution)/shard_map/all_to_all | solution.py:483
  30.0 64.3 %all-gather.2.cloned.1.call-start = ((), (), s32[]{:S(2)}) async-start(), calls=%async_computation.6 | async-start | bytes 1114112 | tf_op jit(solution)/shard_map/all_gather | solution.py:480
  31.3 8.1 %copy-start.14 = (bf16[128,256]{1,0:T(8,128)(2,1)S(1)}, bf16[128,256]{1,0:T(8,128)(2,1)}, u32[]{:S(2)}) copy-start(bf16[128,256]{1,0:T(8,128)(2,1)} %param.23) | copy-start | bytes 196612
  31.3 8.1 %copy-start.15 = (bf16[128,256]{1,0:T(8,128)(2,1)S(1)}, bf16[128,256]{1,0:T(8,128)(2,1)}, u32[]{:S(2)}) copy-start(bf16[128,256]{1,0:T(8,128)(2,1)} %param.22) | copy-start | bytes 196612
  32.5 52.9 %collective-permute-start = (bf16[2,2048,128]{2,1,0:T(8,128)(2,1)}, bf16[2,2048,128]{2,1,0:T(8,128)(2,1)}, u32[]{:S(2)}, u32[]{:S(2)}) collective-permute-start(bf16[2,2048,128]{2,1,0:T(8,128)(2,1)} %pad_maximum_fusion), channel_id=1, source_target_pairs={{0,192},{32,224},{64,0},{96,32},{128,64},{160,96},{192,128},{224,1... | collective-permute-start | bytes 3145736 | tf_op jit(solution)/shard_map/ppermute | solution.py:465
  36.8 48.6 %collective-permute-start.1 = (bf16[1,128,2048]{2,1,0:T(8,128)(2,1)}, bf16[1,128,2048]{2,1,0:T(8,128)(2,1)}, u32[]{:S(2)}, u32[]{:S(2)}) collective-permute-start(bf16[1,128,2048]{2,1,0:T(8,128)(2,1)} %constant_dynamic-slice_fusion.2), channel_id=1, source_target_pairs={{0,192},{32,224},{64,0},{96,32},{128,64},{160,96},{192,128},{224,1... | collective-permute-start | bytes 1572872 | tf_op jit(solution)/shard_map/ppermute | solution.py:465
  70.4 1.6 copy-start.13
  91.7 32.3 %copy-start.3 = (bf16[128,2048]{1,0:T(8,128)(2,1)S(1)}, bf16[128,2048]{1,0:T(8,128)(2,1)}, u32[]{:S(2)}) copy-start(bf16[128,2048]{1,0:T(8,128)(2,1)} %refs_4_.5) | copy-start | bytes 1572868
  91.7 32.3 %copy-start.5 = (bf16[768,384]{1,0:T(8,128)(2,1)S(1)}, bf16[768,384]{1,0:T(8,128)(2,1)}, u32[]{:S(2)}) copy-start(bf16[768,384]{1,0:T(8,128)(2,1)} %get-tuple-element.31.refs_2_) | copy-start | bytes 1769476
  91.7 32.3 %copy-start.11 = (f32[2048]{0:T(1024)S(1)}, f32[2048]{0:T(1024)}, u32[]{:S(2)}) copy-start(f32[2048]{0:T(1024)} %param.14) | copy-start | bytes 24580
  91.7 32.3 %copy-start.12 = (s32[128,8]{0,1:T(8,128)S(1)}, s32[128,8]{0,1:T(8,128)}, u32[]{:S(2)}) copy-start(s32[128,8]{0,1:T(8,128)} %param.15) | copy-start | bytes 12292
  124.0 27.6 %copy-start.2 = (bf16[128,2048]{1,0:T(8,128)(2,1)S(1)}, bf16[128,2048]{1,0:T(8,128)(2,1)}, u32[]{:S(2)}) copy-start(bf16[128,2048]{1,0:T(8,128)(2,1)} %up_ref.1) | copy-start | bytes 1572868
  125.7 49.1 %copy-start.4 = (bf16[256,2048]{1,0:T(8,128)(2,1)S(1)}, bf16[256,2048]{1,0:T(8,128)(2,1)}, u32[]{:S(2)}) copy-start(bf16[256,2048]{1,0:T(8,128)(2,1)} %refs_2_.5) | copy-start | bytes 3145732
  125.7 25.9 %all-to-all-start.2 = ((bf16[8,16,2176]{2,1,0:T(8,128)(2,1)}), bf16[8,16,2176]{2,1,0:T(8,128)(2,1)S(1)}, u32[]{:S(2)}, u32[]{:S(2)}) async-start(bf16[8,16,2176]{2,1,0:T(8,128)(2,1)} %bitcast.11), calls=%async_computation.2 | async-start | bytes 1114112 | tf_op jit(solution)/shard_map/all_to_all | solution.py:498
  132.9 41.9 %copy-start = (bf16[2048,256]{1,0:T(8,128)(2,1)S(1)}, bf16[2048,256]{1,0:T(8,128)(2,1)}, u32[]{:S(2)}) copy-start(bf16[2048,256]{1,0:T(8,128)(2,1)} %all-gather.2.cloned.1.call-done.refs_2_.refs_8_) | copy-start | bytes 3145732
  132.9 1.7 collective-permute-start.4
  134.6 0.6 copy-start.9
  139.8 35.0 %copy-start.6 = (f32[136,512]{1,0:T(8,128)S(1)}, f32[136,512]{1,0:T(8,128)}, u32[]{:S(2)}) copy-start(f32[136,512]{1,0:T(8,128)} %get-tuple-element.34.refs_6_) | copy-start | bytes 835588
  139.8 35.0 %copy-start.10 = (bf16[128,256]{1,0:T(8,128)(2,1)S(1)}, bf16[128,256]{1,0:T(8,128)(2,1)}, u32[]{:S(2)}) copy-start(bf16[128,256]{1,0:T(8,128)(2,1)} %copy-done.9) | copy-start | bytes 196612
  139.8 1.8 collective-permute-start.5
  141.6 0.7 copy-start.7
  151.6 23.2 %copy-start.1 = (bf16[2048,512]{1,0:T(8,128)(2,1)S(1)}, bf16[2048,512]{1,0:T(8,128)(2,1)}, u32[]{:S(2)}) copy-start(bf16[2048,512]{1,0:T(8,128)(2,1)} %get-tuple-element.36.refs_5_) | copy-start | bytes 6291460
  151.6 23.3 %copy-start.8 = (f32[136,512]{1,0:T(8,128)S(1)}, f32[136,512]{1,0:T(8,128)}, u32[]{:S(2)}) copy-start(f32[136,512]{1,0:T(8,128)} %copy-done.7) | copy-start | bytes 835588
  172.9 2.0 collective-permute-start.6
  200.5 20.1 %all-to-all-start.5 = ((bf16[8,128,256]{2,1,0:T(8,128)(2,1)}), bf16[8,128,256]{2,1,0:T(8,128)(2,1)S(1)}, u32[]{:S(2)}, u32[]{:S(2)}) async-start(bf16[8,128,256]{2,1,0:T(8,128)(2,1)} %sum_chips.1), calls=%async_computation.5 | async-start | bytes 1048576 | tf_op jit(solution)/shard_map/all_to_all | solution.py:523
  204.9 1.3 collective-permute-start.7
Sparse Core Ops, SparseCore 0:
  40.2 54.0 all-gather.1

commit v7 on v6

--- a/solution.py
+++ b/solution.py
@@ -135,38 +135,51 @@
     )(quarter, ids, weights, hidden, upstream, gain)
 
 
-def pack_kernel(count, q_ref, *refs):
-    for n in range(count):
-        g_ref, u_ref, d_ref = refs[3 * n : 3 * n + 3]
-        out_ref = refs[3 * count + n]
-        unit = g_ref.shape[2]
-        out_ref[0] = g_ref[0]
-        out_ref[1] = u_ref[0]
-        for k in range(d_ref.shape[2] // unit):
-            out_ref[2, k * unit : (k + 1) * unit] = d_ref[0, :, k * unit : (k + 1) * unit]
+def pack_kernel(count, q_ref, g_ref, u_ref, d_ref, *refs):
+    out_refs = refs[:count]
+    tall_ref, down_ref, in_sems, out_sems = refs[count:]
+    unit = g_ref.shape[2]
+    blocks = d_ref.shape[2] // unit
+    loads, stores = [], []
+    for n, out in enumerate(out_refs):
+        which = q_ref[n]
+        pairs = [(g_ref.at[which], tall_ref.at[n, 0]), (u_ref.at[which], tall_ref.at[n, 1]), (d_ref.at[which], down_ref.at[n])]
+        loads += [pltpu.make_async_copy(src, dst, in_sems.at[3 * n + k]) for k, (src, dst) in enumerate(pairs)]
+        pairs = [[(tall_ref.at[n, k], out.at[k])] for k in range(2)]
+        at = [pl.ds(k * unit, unit) for k in range(blocks)]
+        pairs.append([(down_ref.at[n, :, span], out.at[2, span]) for span in at])
+        for group in pairs:
+            first = sum([len(g) for g in stores])
+            stores.append([pltpu.make_async_copy(src, dst, out_sems.at[first + k]) for k, (src, dst) in enumerate(group)])
+    for load in loads:
+        load.start()
+    for load, group in zip(loads, stores):
+        load.wait()
+        for store in group:
+            store.start()
+    for group in stores:
+        for store in group:
+            store.wait()
 
 
 def pack(which, w_gate, w_up, w_down):
     width, unit = w_gate.shape[1:]
     count = which.shape[0]
-    rows = PACK_ROWS
-
-    def at(n):
-        tall = pl.BlockSpec((1, rows, unit), lambda i, q: (q[n], i, 0))
-        return [tall, tall, pl.BlockSpec((1, unit, rows), lambda i, q: (q[n], 0, i))]
-
+    hbm = pl.BlockSpec(memory_space=pltpu.HBM)
     return pl.pallas_call(
         lambda *refs: pack_kernel(count, *refs),
-        grid_spec=pltpu.PrefetchScalarGridSpec(
-            num_scalar_prefetch=1,
-            grid=(width // rows,),
-            in_specs=sum([at(n) for n in range(count)], []),
-            out_specs=[pl.BlockSpec((3, rows, unit), lambda i, q: (0, i, 0))] * count,
-        ),
+        in_specs=[pl.BlockSpec(memory_space=pltpu.SMEM), hbm, hbm, hbm],
+        out_specs=[hbm] * count,
         out_shape=[jax.ShapeDtypeStruct((3, width, unit), BF)] * count,
+        scratch_shapes=[
+            pltpu.VMEM((count, 2, width, unit), BF),
+            pltpu.VMEM((count, unit, width), BF),
+            pltpu.SemaphoreType.DMA((3 * count,)),
+            pltpu.SemaphoreType.DMA((count * (2 + width // unit),)),
+        ],
         compiler_params=params(),
         name="pack",
-    )(which, *[w_gate, w_up, w_down] * count)
+    )(which, w_gate, w_up, w_down)
 
 
 def pick_kernel(q_ref, w_ref, out_ref):

time: 229 us -> 229 us (level)
  no operation moved by 1% of the time
where the time goes in v7:
time: 229 us; the launch traced here: 228 us
  blocking collectives  71.5 us (31%)
  waiting for transfers between devices  61.3 us (27%)
  Pallas kernels  40.6 us (18%)
  starting transfers between devices  29.8 us (13%)
  between operations  14.2 us (6%)
  local copies, waits for them, and re-layouts  7.68 us (3%)
  other arithmetic  3.03 us (1%)
    all_to_all x1, blocking collectives, body(): lax.all_to_all(rows.reshape(ctx_count, PAIR, narrow), 'context', 0, 0, ti...  29.7 us
    all_to_all x1, blocking collectives, body(): lax.all_to_all(done, 'expert', 0, 0, tiled=True).reshape(tokens, wide)  21.2 us
    all_to_all x1, blocking collectives, body(): lax.all_to_all(part.reshape(chips, tokens, 2 * HEAD_DIM), 'context', 0, 0...  20.7 us
    ppermute x4, waiting for transfers between devices, trade(): return lax.ppermute(w, ('expert', 'context'), moves(step))  15.1 us
    all_to_all x1, waiting for transfers between devices, body(): lax.all_to_all(send.reshape(ctx_count, PAIR, width), 'context', 0, 0, til...  14.9 us
    all_to_all x1, waiting for transfers between devices, body(): part = lax.all_to_all(part, 'expert', 0, 0, tiled=True)  13.7 us
    pallas_call x5, Pallas kernels, on_chip(): pl.pallas_call(kernel, in_specs=[pl.BlockSpec(memory_space=pltpu.SMEM)] *...  12 us
    pallas_call x1, Pallas kernels, expert_near(): pl.pallas_call(lambda *refs: near_kernel(rows, *refs), grid_spec=pltpu.Pr...  11.7 us
  transfers between devices with their start and end apart: 12, of which 10 were waited for; matrix products, arithmetic and copies ran while one was open for 3% of the time, Pallas kernels for 13%

profile of v7, /device:TPU:2, one launch (start us, length us, event | category | flops | bytes accessed | tf_op | source)
XLA Modules:
  0.0 228.2 jit_solution(17565219579680669729)
XLA Ops:
  7.2 0.6 pad_add_fusion.refs_0_
  7.8 3.9 %pack.1 = (bf16[3,2048,128]{2,1,0:T(8,128)(2,1)}, bf16[3,2048,128]{2,1,0:T(8,128)(2,1)}) custom-call(s32[2]{0:T(128)} %pad_add_fusion.refs_0_, bf16[4,2048,128]{2,1,0:T(8,128)(2,1)} %refs_2_.4, bf16[4,2048,128]{2,1,0:T(8,128)(2,1)} %refs_3_.5, bf16[4,128,2048]{2,1,0:T(8,128)(2,1)} %w_ref.1), custom_call_target="tpu_custom_call" | custom-call | tf_op jit(solution)/shard_map/pack/pallas_call | solution.py:169
  11.6 2.0 collective-permute-start.2
  13.6 4.0 %collective-permute-start.3 = (bf16[3,2048,128]{2,1,0:T(8,128)(2,1)}, bf16[3,2048,128]{2,1,0:T(8,128)(2,1)}, u32[]{:S(2)}, u32[]{:S(2)}) collective-permute-start(bf16[3,2048,128]{2,1,0:T(8,128)(2,1)} %get-tuple-element.26), channel_id=1, source_target_pairs={{0,224},{32,0},{64,32},{96,64},{128,96},{160,128},{192,160},{224,1... | collective-permute-start | bytes 4718600 | tf_op jit(solution)/shard_map/ppermute | solution.py:478
  17.7 4.7 %route.1 = (bf16[768,2048]{1,0:T(8,128)(2,1)}, bf16[768,384]{1,0:T(8,128)(2,1)}) custom-call(s32[1]{0:T(128)} %bitcast.1.refs_0_.q_ref, s32[8,128]{1,0:T(8,128)} %bitcast.22, bf16[8,128]{1,0:T(8,128)(2,1)} %bitcast.28, bf16[128,2048]{1,0:T(8,128)(2,1)} %refs_4_.3, bf16[128,2048]{1,0:T(8,128)(2,1)} %up_ref.1, f32[1,2048]{1,0:T(1,128)} %bitcast.20), custom_call_target="tpu_custom_call" | custom-call | tf_op jit(solution)/shard_map/route/pallas_call | solution.py:109
  22.3 7.6 %all-to-all-start = ((bf16[32,24,2048]{2,1,0:T(8,128)(2,1)}), bf16[32,24,2048]{2,1,0:T(8,128)(2,1)S(1)}, u32[]{:S(2)}, u32[]{:S(2)}) async-start(bf16[32,24,2048]{2,1,0:T(8,128)(2,1)} %bitcast.27), calls=%async_computation | async-start | bytes 6291456 | tf_op jit(solution)/shard_map/all_to_all | solution.py:496
  30.0 0.0 all-gather.2.cloned.1.call-start
  30.0 1.3 constant_dynamic-slice_fusion.3
  31.3 0.0 copy-start.14
  31.3 1.1 pad_maximum_fusion
  32.5 2.4 %collective-permute-start = (bf16[2,2048,128]{2,1,0:T(8,128)(2,1)}, bf16[2,2048,128]{2,1,0:T(8,128)(2,1)}, u32[]{:S(2)}, u32[]{:S(2)}) collective-permute-start(bf16[2,2048,128]{2,1,0:T(8,128)(2,1)} %pad_maximum_fusion), channel_id=1, source_target_pairs={{0,192},{32,224},{64,0},{96,32},{128,64},{160,96},{192,128},{224,1... | collective-permute-start | bytes 3145736 | tf_op jit(solution)/shard_map/ppermute | solution.py:478
  34.9 1.9 constant_dynamic-slice_fusion.2
  36.7 2.6 %collective-permute-start.1 = (bf16[1,128,2048]{2,1,0:T(8,128)(2,1)}, bf16[1,128,2048]{2,1,0:T(8,128)(2,1)}, u32[]{:S(2)}, u32[]{:S(2)}) collective-permute-start(bf16[1,128,2048]{2,1,0:T(8,128)(2,1)} %constant_dynamic-slice_fusion.2), channel_id=1, source_target_pairs={{0,192},{32,224},{64,0},{96,32},{128,64},{160,96},{192,128},{224,1... | collective-permute-start | bytes 1572872 | tf_op jit(solution)/shard_map/ppermute | solution.py:478
  39.4 0.6 pad_maximum_fusion.1
  40.0 0.0 all-gather.2.cloned.1.call-update
  40.0 13.5 %collective-permute-done.2.refs_5_ = bf16[3,2048,128]{2,1,0:T(8,128)(2,1)} collective-permute-done((bf16[3,2048,128]{2,1,0:T(8,128)(2,1)}, bf16[3,2048,128]{2,1,0:T(8,128)(2,1)}, u32[]{:S(2)}, u32[]{:S(2)}) %collective-permute-start.2) | collective-permute-done | bytes 1572896 | tf_op jit(solution)/shard_map/ppermute | solution.py:478
  53.6 1.9 pick.1.refs_4_
  55.5 14.9 %all-to-all-done = bf16[32,24,2048]{2,1,0:T(8,128)(2,1)S(1)} async-done(((bf16[32,24,2048]{2,1,0:T(8,128)(2,1)}), bf16[32,24,2048]{2,1,0:T(8,128)(2,1)S(1)}, u32[]{:S(2)}, u32[]{:S(2)}) %all-to-all-start) | async-done | bytes 3145760 | tf_op jit(solution)/shard_map/all_to_all | solution.py:496
  70.4 1.6 copy-done.13
  72.0 11.7 %expert_near.1.near_ref = bf16[768,1152]{1,0:T(8,128)(2,1)} custom-call(s32[1]{0:T(128)} %bitcast.1.refs_0_.q_ref, bf16[768,2048]{1,0:T(8,128)(2,1)} %bitcast.24, bf16[4,2048,128]{2,1,0:T(8,128)(2,1)} %refs_2_.4, bf16[4,2048,128]{2,1,0:T(8,128)(2,1)} %refs_3_.5, bf16[1,128,2048]{2,1,0:T(8,128)(2,1)} %pick.1.refs_4_, ...), custom_call_target="tpu_custom_call" | custom-call | tf_op jit(solution)/shard_map/expert_near/pallas_call | solution.py:246
  83.8 1.6 collective-permute-done.1.down_ref
  85.3 6.3 %expert_far.1 = bf16[768,1152]{1,0:T(8,128)(2,1)} custom-call(bf16[768,2048]{1,0:T(8,128)(2,1)} %bitcast.25, bf16[2,2048,128]{2,1,0:T(8,128)(2,1)} %collective-permute-done.in_ref, bf16[1,128,2048]{2,1,0:T(8,128)(2,1)} %collective-permute-done.1.down_ref, bf16[768,1152]{1,0:T(8,128)(2,1)} %expert_near.1.near_ref), custom_call_target="tpu_custom_call" | custom-call | tf_op jit(solution)/shard_map/expert_far/pallas_call | solution.py:279
  91.7 2.6 %all-gather.2.cloned.1.call-done.refs_2_.refs_8_ = bf16[2048,256]{1,0:T(8,128)(2,1)} async-done(((bf16[128,256]{1,0:T(8,128)(2,1)}), bf16[2048,256]{1,0:T(8,128)(2,1)}) %all-gather.2.cloned.1.call-update) | async-done | bytes 1048592 | tf_op jit(solution)/shard_map/all_gather | solution.py:493
  94.3 29.7 %all_to_all.30 = bf16[32,24,1152]{2,1,0:T(8,128)(2,1)S(1)} all-to-all(bf16[32,24,1152]{2,1,0:T(8,128)(2,1)} %bitcast.26), channel_id=1, replica_groups=mesh['expert'=8,'context'=32] {'context'}, dimensions={0} | all-to-all | bytes 3538944 | tf_op jit(solution)/shard_map/all_to_all | solution.py:502
  124.0 0.0 copy-start.2
  124.0 1.7 gather_rows.1
  125.7 7.2 %all-to-all-start.2 = ((bf16[8,16,2176]{2,1,0:T(8,128)(2,1)}), bf16[8,16,2176]{2,1,0:T(8,128)(2,1)S(1)}, u32[]{:S(2)}, u32[]{:S(2)}) async-start(bf16[8,16,2176]{2,1,0:T(8,128)(2,1)} %bitcast.11), calls=%async_computation.2 | async-start | bytes 1114112 | tf_op jit(solution)/shard_map/all_to_all | solution.py:511
  132.9 0.3 collective-permute-start.4
  133.2 1.4 collective-permute-done.4.refs_1_.refs_4_
  134.6 0.6 copy-done.9
  135.2 4.6 %attention_probs.1 = (bf16[2048,512]{1,0:T(8,128)(2,1)}, f32[136,512]{1,0:T(8,128)}) custom-call(bf16[128,256]{1,0:T(8,128)(2,1)} %refs_3_.6, bf16[128,256]{1,0:T(8,128)(2,1)} %copy-done.9, bf16[2048,256]{1,0:T(8,128)(2,1)} %all-gather.2.cloned.1.call-done.refs_2_.refs_8_), custom_call_target="tpu_custom_call" | custom-call | tf_op jit(solution)/shard_map/attention_probs/pallas_call | solution.py:319
  139.8 0.2 collective-permute-start.5
  140.0 1.6 collective-permute-done.5.refs_7_
  141.6 0.7 copy-done.7
  142.3 9.3 %all-to-all-done.2.in_ref = bf16[8,16,2176]{2,1,0:T(8,128)(2,1)S(1)} async-done(((bf16[8,16,2176]{2,1,0:T(8,128)(2,1)}), bf16[8,16,2176]{2,1,0:T(8,128)(2,1)S(1)}, u32[]{:S(2)}, u32[]{:S(2)}) %all-to-all-start.2) | async-done | bytes 557088 | tf_op jit(solution)/shard_map/all_to_all | solution.py:511
  151.6 0.1 finish_hidden.1
  151.7 21.2 %all_to_all.31 = bf16[8,16,2176]{2,1,0:T(8,128)(2,1)S(1)} all-to-all(bf16[8,16,2176]{2,1,0:T(8,128)(2,1)S(1)} %finish_hidden.1), channel_id=1, replica_groups=mesh['expert'=8,'context'=32] {'expert'}, dimensions={0} | all-to-all | bytes 1114112 | tf_op jit(solution)/shard_map/all_to_all | solution.py:518
  172.8 2.0 collective-permute-done.6.refs_1_
  174.8 4.0 %attention_grads.1 = (f32[128,256]{1,0:T(8,128)S(1)}, f32[128,256]{1,0:T(8,128)S(1)}, bf16[2048,256]{1,0:T(8,128)(2,1)S(1)}) custom-call(bf16[128,2176]{1,0:T(8,128)(2,1)S(1)} %bitcast.16, bf16[128,2176]{1,0:T(8,128)(2,1)S(1)} %collective-permute-done.6.refs_1_, bf16[256,2048]{1,0:T(8,128)(2,1)S(1)} %copy-done.4, bf16[128,256]{1,0:T(8,128)(2,1)} %refs_3_.6, ...), custom_call_target="tpu_custom_call" | custom-call | tf_op jit(solution)/shard_map/attention_grads/pallas_call | solution.py:319
  178.9 20.7 %all_to_all.32.in_ref = bf16[16,128,256]{2,1,0:T(8,128)(2,1)S(1)} all-to-all(bf16[16,128,256]{2,1,0:T(8,128)(2,1)S(1)} %bitcast.19), channel_id=1, replica_groups={{0,2,4,6,8,10,12,14,16,18,20,22,24,26,28,30},{1,3,5,7,9,11,13,15,17,19,..., dimensions={0} | all-to-all | bytes 2097152 | tf_op jit(solution)/shard_map/all_to_all | solution.py:532
  199.6 0.9 sum_chips.1
  200.5 3.5 %all-to-all-start.5 = ((bf16[8,128,256]{2,1,0:T(8,128)(2,1)}), bf16[8,128,256]{2,1,0:T(8,128)(2,1)S(1)}, u32[]{:S(2)}, u32[]{:S(2)}) async-start(bf16[8,128,256]{2,1,0:T(8,128)(2,1)} %sum_chips.1), calls=%async_computation.5 | async-start | bytes 1048576 | tf_op jit(solution)/shard_map/all_to_all | solution.py:536
  204.0 0.8 slice.8
  204.9 0.7 copy.17
  205.5 0.7 collective-permute-done.7
  206.2 0.7 add.48
  206.9 13.7 %all-to-all-done.5.in_ref = bf16[8,128,256]{2,1,0:T(8,128)(2,1)S(1)} async-done(((bf16[8,128,256]{2,1,0:T(8,128)(2,1)}), bf16[8,128,256]{2,1,0:T(8,128)(2,1)S(1)}, u32[]{:S(2)}, u32[]{:S(2)}) %all-to-all-start.5) | async-done | bytes 524320 | tf_op jit(solution)/shard_map/all_to_all | solution.py:536
  220.6 0.7 sum_heads.1
  (33 shorter events, 0.1 us)
Async XLA Ops:
  11.6 41.9 %collective-permute-start.2 = (bf16[3,2048,128]{2,1,0:T(8,128)(2,1)}, bf16[3,2048,128]{2,1,0:T(8,128)(2,1)}, u32[]{:S(2)}, u32[]{:S(2)}) collective-permute-start(bf16[3,2048,128]{2,1,0:T(8,128)(2,1)} %get-tuple-element.25), channel_id=1, source_target_pairs={{0,32},{32,64},{64,96},{96,128},{128,160},{160,192},{192,224},{224... | collective-permute-start | bytes 4718600 | tf_op jit(solution)/shard_map/ppermute | solution.py:478
  13.6 40.0 %collective-permute-start.3 = (bf16[3,2048,128]{2,1,0:T(8,128)(2,1)}, bf16[3,2048,128]{2,1,0:T(8,128)(2,1)}, u32[]{:S(2)}, u32[]{:S(2)}) collective-permute-start(bf16[3,2048,128]{2,1,0:T(8,128)(2,1)} %get-tuple-element.26), channel_id=1, source_target_pairs={{0,224},{32,0},{64,32},{96,64},{128,96},{160,128},{192,160},{224,1... | collective-permute-start | bytes 4718600 | tf_op jit(solution)/shard_map/ppermute | solution.py:478
  22.3 48.1 %all-to-all-start = ((bf16[32,24,2048]{2,1,0:T(8,128)(2,1)}), bf16[32,24,2048]{2,1,0:T(8,128)(2,1)S(1)}, u32[]{:S(2)}, u32[]{:S(2)}) async-start(bf16[32,24,2048]{2,1,0:T(8,128)(2,1)} %bitcast.27), calls=%async_computation | async-start | bytes 6291456 | tf_op jit(solution)/shard_map/all_to_all | solution.py:496
  30.0 64.3 %all-gather.2.cloned.1.call-start = ((), (), s32[]{:S(2)}) async-start(), calls=%async_computation.6 | async-start | bytes 1114112 | tf_op jit(solution)/shard_map/all_gather | solution.py:493
  31.3 8.1 %copy-start.14 = (bf16[128,256]{1,0:T(8,128)(2,1)S(1)}, bf16[128,256]{1,0:T(8,128)(2,1)}, u32[]{:S(2)}) copy-start(bf16[128,256]{1,0:T(8,128)(2,1)} %param.23) | copy-start | bytes 196612
  31.3 8.0 %copy-start.15 = (bf16[128,256]{1,0:T(8,128)(2,1)S(1)}, bf16[128,256]{1,0:T(8,128)(2,1)}, u32[]{:S(2)}) copy-start(bf16[128,256]{1,0:T(8,128)(2,1)} %param.22) | copy-start | bytes 196612
  32.5 52.9 %collective-permute-start = (bf16[2,2048,128]{2,1,0:T(8,128)(2,1)}, bf16[2,2048,128]{2,1,0:T(8,128)(2,1)}, u32[]{:S(2)}, u32[]{:S(2)}) collective-permute-start(bf16[2,2048,128]{2,1,0:T(8,128)(2,1)} %pad_maximum_fusion), channel_id=1, source_target_pairs={{0,192},{32,224},{64,0},{96,32},{128,64},{160,96},{192,128},{224,1... | collective-permute-start | bytes 3145736 | tf_op jit(solution)/shard_map/ppermute | solution.py:478
  36.7 48.6 %collective-permute-start.1 = (bf16[1,128,2048]{2,1,0:T(8,128)(2,1)}, bf16[1,128,2048]{2,1,0:T(8,128)(2,1)}, u32[]{:S(2)}, u32[]{:S(2)}) collective-permute-start(bf16[1,128,2048]{2,1,0:T(8,128)(2,1)} %constant_dynamic-slice_fusion.2), channel_id=1, source_target_pairs={{0,192},{32,224},{64,0},{96,32},{128,64},{160,96},{192,128},{224,1... | collective-permute-start | bytes 1572872 | tf_op jit(solution)/shard_map/ppermute | solution.py:478
  70.4 1.6 copy-start.13
  91.7 32.3 %copy-start.3 = (bf16[128,2048]{1,0:T(8,128)(2,1)S(1)}, bf16[128,2048]{1,0:T(8,128)(2,1)}, u32[]{:S(2)}) copy-start(bf16[128,2048]{1,0:T(8,128)(2,1)} %refs_4_.3) | copy-start | bytes 1572868
  91.7 32.3 %copy-start.5 = (bf16[768,384]{1,0:T(8,128)(2,1)S(1)}, bf16[768,384]{1,0:T(8,128)(2,1)}, u32[]{:S(2)}) copy-start(bf16[768,384]{1,0:T(8,128)(2,1)} %get-tuple-element.31.refs_2_) | copy-start | bytes 1769476
  91.7 32.3 %copy-start.11 = (f32[2048]{0:T(1024)S(1)}, f32[2048]{0:T(1024)}, u32[]{:S(2)}) copy-start(f32[2048]{0:T(1024)} %param.14) | copy-start | bytes 24580
  91.7 32.3 %copy-start.12 = (s32[128,8]{0,1:T(8,128)S(1)}, s32[128,8]{0,1:T(8,128)}, u32[]{:S(2)}) copy-start(s32[128,8]{0,1:T(8,128)} %param.15) | copy-start | bytes 12292
  124.0 27.6 %copy-start.2 = (bf16[128,2048]{1,0:T(8,128)(2,1)S(1)}, bf16[128,2048]{1,0:T(8,128)(2,1)}, u32[]{:S(2)}) copy-start(bf16[128,2048]{1,0:T(8,128)(2,1)} %up_ref.1) | copy-start | bytes 1572868
  125.7 49.1 %copy-start.4 = (bf16[256,2048]{1,0:T(8,128)(2,1)S(1)}, bf16[256,2048]{1,0:T(8,128)(2,1)}, u32[]{:S(2)}) copy-start(bf16[256,2048]{1,0:T(8,128)(2,1)} %refs_2_.5) | copy-start | bytes 3145732
  125.7 25.9 %all-to-all-start.2 = ((bf16[8,16,2176]{2,1,0:T(8,128)(2,1)}), bf16[8,16,2176]{2,1,0:T(8,128)(2,1)S(1)}, u32[]{:S(2)}, u32[]{:S(2)}) async-start(bf16[8,16,2176]{2,1,0:T(8,128)(2,1)} %bitcast.11), calls=%async_computation.2 | async-start | bytes 1114112 | tf_op jit(solution)/shard_map/all_to_all | solution.py:511
  132.9 41.9 %copy-start = (bf16[2048,256]{1,0:T(8,128)(2,1)S(1)}, bf16[2048,256]{1,0:T(8,128)(2,1)}, u32[]{:S(2)}) copy-start(bf16[2048,256]{1,0:T(8,128)(2,1)} %all-gather.2.cloned.1.call-done.refs_2_.refs_8_) | copy-start | bytes 3145732
  132.9 1.7 collective-permute-start.4
  134.6 0.6 copy-start.9
  139.8 35.0 %copy-start.6 = (f32[136,512]{1,0:T(8,128)S(1)}, f32[136,512]{1,0:T(8,128)}, u32[]{:S(2)}) copy-start(f32[136,512]{1,0:T(8,128)} %get-tuple-element.34.refs_6_) | copy-start | bytes 835588
  139.8 35.0 %copy-start.10 = (bf16[128,256]{1,0:T(8,128)(2,1)S(1)}, bf16[128,256]{1,0:T(8,128)(2,1)}, u32[]{:S(2)}) copy-start(bf16[128,256]{1,0:T(8,128)(2,1)} %copy-done.9) | copy-start | bytes 196612
  139.8 1.8 collective-permute-start.5
  141.6 0.7 copy-start.7
  151.6 23.2 %copy-start.1 = (bf16[2048,512]{1,0:T(8,128)(2,1)S(1)}, bf16[2048,512]{1,0:T(8,128)(2,1)}, u32[]{:S(2)}) copy-start(bf16[2048,512]{1,0:T(8,128)(2,1)} %get-tuple-element.36.refs_5_) | copy-start | bytes 6291460
  151.6 23.3 %copy-start.8 = (f32[136,512]{1,0:T(8,128)S(1)}, f32[136,512]{1,0:T(8,128)}, u32[]{:S(2)}) copy-start(f32[136,512]{1,0:T(8,128)} %copy-done.7) | copy-start | bytes 835588
  172.8 2.0 collective-permute-start.6
  200.5 20.1 %all-to-all-start.5 = ((bf16[8,128,256]{2,1,0:T(8,128)(2,1)}), bf16[8,128,256]{2,1,0:T(8,128)(2,1)S(1)}, u32[]{:S(2)}, u32[]{:S(2)}) async-start(bf16[8,128,256]{2,1,0:T(8,128)(2,1)} %sum_chips.1), calls=%async_computation.5 | async-start | bytes 1048576 | tf_op jit(solution)/shard_map/all_to_all | solution.py:536
  204.8 1.3 collective-permute-start.7
Sparse Core Ops, SparseCore 0:
  40.2 54.0 all-gather.1
